TPU v7x, 256 devices: a whole 4x4x8 slice. The times are simulated.
256 devices in a mesh: ctx: 64 (over z, x, core), tp: 4 (over y).
Axes of the slice: x: 4, y: 4, z: 8, core: 2. Of those that a mesh axis runs over, the one named last changes fastest.
Arguments:
- query_one: bfloat16 [12288, 4096], P('ctx', 'tp'), may hold values from -64 to 64
- key_one: bfloat16 [12288, 1024], P('ctx', 'tp'), may hold values from -6 to 6
- value_one: bfloat16 [12288, 1024], P('ctx', 'tp'), may hold values from -6 to 6
- segments: int32 [12288], P('ctx'), may hold values from 0 to 3, never falling along the last dimension, each value on 1 to 6144 neighbouring positions
- query_base: bfloat16 [12288, 4096], P('ctx', 'tp'), may hold values from -20 to 20
- key_two: bfloat16 [12288, 1024], P('ctx', 'tp'), may hold values from -3 to 3
- value_two: bfloat16 [12288, 1024], P('ctx', 'tp'), may hold values from -64 to 64
Outputs:
- attended: bfloat16 [12288, 4096], P('ctx', 'tp')
Inputs may be any that keep to these rules, and one draw needn't show every extreme that they name: `segments`: document numbers never fall along the sequence; each of the 4 documents has 1 to 6144 tokens, one exactly that many.
All inputs are finite; a program needn't handle non-finite values.
Results may differ from a plain program's by a relative error of at most 0.0075.
Values may be sent and summed in bfloat16 or wider, within the bound.
No kernel may reach another device: no remote copies, remote signals or barrier semaphores. Data moves between devices by JAX's collectives and lax.ppermute only.
A program may use at most 192 MiB of HBM per device.

v0:
```python
import jax
import jax.numpy as jnp
from jax import lax
from jax.experimental import pallas as pl
from jax.experimental.pallas import tpu as pltpu
from jax.sharding import Mesh, PartitionSpec as P

HEAD_DIM = 128
WIDTH = 4096
EPSILON = 1e-05
NEGATIVE = -1e30

TOK = 192
PAIR = 384
REPEAT = 4
COLS = REPEAT * HEAD_DIM
Z, X, CORES, TP = 8, 4, 2, 4
CHUNK = 2
SCALE = HEAD_DIM ** (-0.5) * 1.4426950408889634

F32 = jnp.float32
BF16 = jnp.bfloat16
VMEM = pl.BlockSpec(memory_space=pltpu.VMEM)
SMEM = pl.BlockSpec(memory_space=pltpu.SMEM)
HBM = pl.BlockSpec(memory_space=pltpu.HBM)


def place():
    return lax.axis_index("z"), lax.axis_index("x"), lax.axis_index("core")


def call(kernel, outs, specs_in, specs_out, scratch=(), aliases=None, limit=16, name=None):
    return pl.pallas_call(
        kernel,
        out_shape=outs,
        in_specs=specs_in,
        out_specs=specs_out,
        scratch_shapes=list(scratch),
        input_output_aliases=aliases or {},
        compiler_params=pltpu.CompilerParams(vmem_limit_bytes=limit * 2**20),
        name=name,
    )


def count_below(ref, doc):
    found = jnp.int32(0)
    for step in (128, 64, 32, 16, 8, 4, 2, 1):
        tried = found + step
        last = ref[jnp.minimum(tried, TOK) - 1]
        found = jnp.where((tried <= TOK) & (last < doc), tried, found)
    return found


def half(core):
    return pl.ds(pl.multiple_of(core * HEAD_DIM, HEAD_DIM), HEAD_DIM)


def rows_of(core):
    return pl.ds(pl.multiple_of(core * TOK, 64), TOK)


def prep_kernel(seg, seg_r, own, other, own0_ref, first_ref, state_ref, info_ref):
    core = place()[2]
    for side, ref in ((core, own), (1 - core, other)):
        first_ref[rows_of(side), :HEAD_DIM] = ref[0]
        first_ref[rows_of(side), HEAD_DIM:] = ref[1]
        own0_ref[rows_of(side), :HEAD_DIM] = ref[2]
        own0_ref[rows_of(side), HEAD_DIM:] = ref[3]
    below = [count_below(seg, d) for d in (1, 2, 3)]
    below_r = [count_below(seg_r, d) for d in (1, 2, 3)]
    bounds = [a + b for a, b in zip(below, below_r)]
    first = jnp.where(core == 0, seg[0], seg_r[0])
    last = jnp.where(core == 0, seg_r[TOK - 1], seg[TOK - 1])

    def pick(values, doc):
        out = jnp.int32(0)
        for d in (1, 2, 3):
            out = jnp.where(doc == d, values[d - 1], out)
        return out

    count = PAIR - pick(bounds, last)
    first_end = jnp.where(first == 3, PAIR, pick(bounds, first + 1))
    for place_in, value in enumerate((*bounds, first, last, count, first_end, 0)):
        info_ref[place_in] = jnp.int32(value)
    rows = lax.broadcasted_iota(jnp.int32, (PAIR, HEAD_DIM), 0)
    masked = jnp.where(rows >= PAIR - count, first_ref[:, :HEAD_DIM].astype(F32), 0.0)
    state = lax.dot_general(
        masked.astype(BF16),
        first_ref[:, HEAD_DIM:],
        (((0,), (0,)), ((), ())),
        preferred_element_type=F32,
    )
    state_ref[:HEAD_DIM] = state.astype(BF16)
    state_ref[HEAD_DIM:] = notes(last.astype(F32), count.astype(F32)).astype(BF16)


def notes(last, count):
    row = lax.broadcasted_iota(jnp.int32, (16, HEAD_DIM), 0)
    high = jnp.floor(count * (1.0 / 64.0))
    return jnp.where(
        row == 0, last, jnp.where(row == 1, high, jnp.where(row == 2, count - 64.0 * high, 0.0))
    )


def read_state(ref):
    tail = ref[HEAD_DIM:].astype(F32)
    return ref[:HEAD_DIM].astype(F32), tail[0:1], tail[1:2] * 64.0 + tail[2:3]


def plane_kernel(
    info, own, from1, from2, from3, queries_r, prefix_ref, plane_ref
):
    x = place()[1]
    first = info[3].astype(F32)
    items = [read_state(ref) for ref in (own, from1, from2, from3)]
    prefix = jnp.zeros((HEAD_DIM, HEAD_DIM), F32)
    prefix_count = jnp.zeros((1, HEAD_DIM), F32)
    for shift in (1, 2, 3):
        state, doc, count = items[shift]
        chosen = jnp.where((doc == first) & (x >= shift), 1.0, 0.0)
        prefix += state * chosen
        prefix_count += count * chosen
    prefix_ref[:HEAD_DIM] = prefix
    prefix_ref[HEAD_DIM:] = jnp.broadcast_to(prefix_count, (8, HEAD_DIM))
    last = items[0][1]
    for item in items[1:]:
        last = jnp.maximum(last, item[1])
    total = jnp.zeros((HEAD_DIM, HEAD_DIM), F32)
    total_count = jnp.zeros((1, HEAD_DIM), F32)
    for state, doc, count in items:
        chosen = jnp.where(doc == last, 1.0, 0.0)
        total += state * chosen
        total_count += count * chosen
    plane_ref[:HEAD_DIM] = total.astype(BF16)
    plane_ref[HEAD_DIM:] = notes(last, total_count).astype(BF16)


def document_start(info, rows):
    start = jnp.zeros_like(rows)
    for d in range(3):
        start = jnp.where(rows >= info[d], jnp.maximum(start, info[d]), start)
    return start


def split_dot(wide, narrow):
    high = wide.astype(BF16)
    low = (wide - high.astype(F32)).astype(BF16)
    return jnp.dot(high, narrow, preferred_element_type=F32) + jnp.dot(
        low, narrow, preferred_element_type=F32
    )


def inside_kernel(info, keep, queries_r, packed, inside_ref, query_ref):
    core = place()[2]
    query_ref[rows_of(core), :] = keep[0]
    query_ref[rows_of(1 - core), :] = queries_r[0]
    row = lax.broadcasted_iota(jnp.int32, (PAIR, PAIR), 0)
    column = lax.broadcasted_iota(jnp.int32, (PAIR, PAIR), 1)
    visible = (column <= row) & (column >= document_start(info, row))
    for head in range(REPEAT):
        cols = slice(head * HEAD_DIM, (head + 1) * HEAD_DIM)
        scores = lax.dot_general(
            query_ref[:, cols],
            packed[:, :HEAD_DIM],
            (((1,), (1,)), ((), ())),
            preferred_element_type=F32,
        )
        scores = jnp.where(visible, scores, 0.0)
        inside_ref[:, cols] = split_dot(scores, packed[:, HEAD_DIM:])


def row_sums(squares):
    high = squares.astype(BF16)
    low = (squares - high.astype(F32)).astype(BF16)
    ones = jnp.ones((8, squares.shape[1]), BF16)
    dims = (((1,), (1,)), ((), ()))
    return lax.dot_general(ones, high, dims, preferred_element_type=F32) + lax.dot_general(
        ones, low, dims, preferred_element_type=F32
    )


def first_kernel(
    info, prefix, from1, from2, from3, from4, inside, query, first_ref, sums_ref, count_ref
):
    z = place()[0]
    first = info[3].astype(F32)
    state = prefix[:HEAD_DIM]
    count = prefix[HEAD_DIM : HEAD_DIM + 1]
    for back, ref in enumerate((from1, from2, from3, from4), 1):
        one_state, doc, one_count = read_state(ref)
        chosen = jnp.where((doc == first) & (z >= back), 1.0, 0.0)
        state += one_state * chosen
        count += one_count * chosen
    count_ref[0] = jnp.max(count).astype(jnp.int32)
    high = state.astype(BF16)
    low = (state - high.astype(F32)).astype(BF16)
    in_first = lax.broadcasted_iota(jnp.int32, (PAIR, HEAD_DIM), 0) < info[6]
    squares = jnp.zeros((PAIR, HEAD_DIM), F32)
    for head in range(REPEAT):
        cols = slice(head * HEAD_DIM, (head + 1) * HEAD_DIM)
        queries = query[:, cols]
        earlier = jnp.dot(queries, high, preferred_element_type=F32) + jnp.dot(
            queries, low, preferred_element_type=F32
        )
        out = inside[:, cols] + jnp.where(in_first, earlier, 0.0)
        first_ref[:, cols] = out
        squares += out * out
    sums = row_sums(squares)
    for to in range(CORES * TP):
        sums_ref[to] = sums


def row_scale(sums):
    total = sums[0]
    for device in range(1, CORES * TP):
        total = total + sums[device]
    return lax.transpose(lax.rsqrt(total * (1.0 / WIDTH) + EPSILON), (1, 0))[:, :1]


TILE = 128
TILES = [(head, slice(at, at + TILE)) for head in range(REPEAT) for at in range(0, PAIR, TILE)]


def scores_of(queries, keys, head, part, rows):
    return lax.dot_general(
        queries[head, part],
        keys[rows, :HEAD_DIM],
        (((1,), (1,)), ((), ())),
        preferred_element_type=F32,
    )


def sweep(queries, kv, tops, acc, rows, visible=None, begin=False):
    ahead = scores_of(queries, kv, *TILES[0], rows)
    for at, (head, part) in enumerate(TILES):
        scores = ahead
        if at + 1 < len(TILES):
            ahead = scores_of(queries, kv, *TILES[at + 1], rows)
        if visible is not None:
            scores = jnp.where(visible(part), scores, NEGATIVE)
        top = jnp.max(scores, axis=1, keepdims=True)
        if begin:
            top = jnp.broadcast_to(top, (TILE, HEAD_DIM))
        else:
            old_top = tops[head, part]
            top = jnp.maximum(old_top, top)
        wide_top = jnp.concatenate([top] * (scores.shape[1] // HEAD_DIM), axis=1)
        weights = jnp.exp2((scores - wide_top) * SCALE)
        summed = jnp.dot(weights.astype(BF16), kv[rows, HEAD_DIM:], preferred_element_type=F32)
        tops[head, part] = top
        if begin:
            acc[head, part] = summed
        else:
            shrink = jnp.exp2((old_top - top) * SCALE)
            acc[head, part] = acc[head, part] * jnp.concatenate([shrink, shrink], axis=1) + summed


class Window:
    def __init__(self, info, prior, blocks, kv, bounds, sems):
        self.info, self.kv, self.bounds = info, kv, bounds
        used = jnp.int32(0)
        self.copies = []
        for at, (ref, distance) in enumerate(blocks):
            distance = jnp.int32(distance)
            needed = (distance >= 1) & (distance <= 16) & (prior > (distance - 1) * PAIR)
            slot = jnp.minimum(used, bounds.shape[0] - 1)
            rows = pl.ds(pl.multiple_of(slot * PAIR, PAIR), PAIR)
            copy = pltpu.make_async_copy(ref, kv.at[rows, pl.ds(0, 2 * HEAD_DIM)], sems.at[at])
            self.copies.append((needed, copy))

            @pl.when(needed)
            def _():
                copy.start()
                bounds[slot] = jnp.maximum(distance * PAIR - prior, 0)

            used = used + needed.astype(jnp.int32)
        self.steps = (used + CHUNK - 1) // CHUNK
        kv[:, 2 * HEAD_DIM :] = jnp.ones((kv.shape[0], HEAD_DIM), BF16)

        @pl.when(used % CHUNK != 0)
        def _():
            rows = pl.ds(pl.multiple_of(used * PAIR, PAIR), PAIR)
            kv[rows, : 2 * HEAD_DIM] = jnp.zeros((PAIR, 2 * HEAD_DIM), BF16)
            bounds[used] = jnp.int32(PAIR)

    def absorb(self, queries, tops, acc):
        for needed, copy in self.copies:
            pl.when(needed)(copy.wait)

        @pl.loop(0, self.steps)
        def _(step):
            rows = pl.ds(pl.multiple_of(step * CHUNK * PAIR, CHUNK * PAIR), CHUNK * PAIR)
            low0, low1 = self.bounds[step * CHUNK], self.bounds[step * CHUNK + 1]
            first_end = self.info[6]
            whole = (low0 == 0) & (low1 == 0) & (first_end == PAIR)

            @pl.when(whole)
            def _():
                sweep(queries, self.kv, tops, acc, rows)

            @pl.when(jnp.logical_not(whole))
            def _():
                def visible(part):
                    row = lax.broadcasted_iota(jnp.int32, (TILE, CHUNK * PAIR), 0) + part.start
                    column = lax.broadcasted_iota(jnp.int32, (TILE, CHUNK * PAIR), 1)
                    low = jnp.where(column < PAIR, low0, PAIR + low1)
                    return (column >= low) & (row < first_end)

                sweep(queries, self.kv, tops, acc, rows, visible)


SLOTS = 10


def near_kernel(
    info, reach, sums, first, keep, queries_r, own0, own1, own2, own3, own4, *refs
):
    others1, others2 = refs[:3], refs[3:6]
    queries, tops, acc, kv, own, scales, bounds, sems = refs[6:]
    _, x, core = place()
    blocks = [(own1, 4), (own2, 8), (own3, 12), (own4, 16)]
    for shift, other1, other2 in zip((1, 2, 3), others1, others2):
        wrapped = jnp.where(x < shift, 4, 0)
        blocks.append((other1, 4 + shift - wrapped))
        blocks.append((other2, 8 + shift - wrapped))
    window = Window(info, reach[0], blocks, kv, bounds, sems)
    own[:, : 2 * HEAD_DIM] = own0[...]
    own[:, 2 * HEAD_DIM :] = jnp.ones((PAIR, HEAD_DIM), BF16)
    scales[...] = jnp.broadcast_to(row_scale(sums), (PAIR, HEAD_DIM))
    for part, where in ((keep.at[1], rows_of(core)), (queries_r.at[1], rows_of(1 - core))):
        for head in range(REPEAT):
            cols = slice(head * HEAD_DIM, (head + 1) * HEAD_DIM)
            value = part[:, cols].astype(F32) + first[where, cols] * scales[where, :]
            queries[head, where, :] = value.astype(BF16)

    def own_visible(part):
        row = lax.broadcasted_iota(jnp.int32, (TILE, PAIR), 0) + part.start
        column = lax.broadcasted_iota(jnp.int32, (TILE, PAIR), 1)
        return (column <= row) & (column >= document_start(info, row))

    sweep(queries, own, tops, acc, slice(0, PAIR), own_visible, begin=True)
    window.absorb(queries, tops, acc)


def far_kernel(info, reach, queries, old_tops, old_acc, *refs):
    others3, others04 = refs[:3], refs[3:6]
    mine_ref, send_ref, sums_ref, tops, acc, kv, bounds, sems = refs[6:]
    _, x, core = place()
    blocks = []
    for shift, other3, other04 in zip((1, 2, 3), others3, others04):
        blocks.append((other3, 12 + shift - jnp.where(x < shift, 4, 0)))
        blocks.append((other04, jnp.where(x < shift, 12 + shift, shift)))
    window = Window(info, reach[0], blocks, kv, bounds, sems)
    window.absorb(queries, tops, acc)
    for side in range(CORES):
        where = slice(side * TOK, (side + 1) * TOK)
        squares = jnp.zeros((TOK, HEAD_DIM), F32)
        outs = []
        for head in range(REPEAT):
            summed = acc[head, where, :]
            out = (summed[:, :HEAD_DIM] / summed[:, HEAD_DIM:]).astype(BF16)
            outs.append(out)
            widened = out.astype(F32)
            squares += widened * widened
        whole = jnp.concatenate(outs, axis=1)

        @pl.when(core == side)
        def _():
            mine_ref[...] = whole

        @pl.when(core != side)
        def _():
            send_ref[...] = whole

        sums = row_sums(squares)
        for to in range(TP):
            sums_ref[side * TP + to] = sums


def last_kernel(sums, mine, theirs, out_ref):
    core = place()[2]
    scale = row_scale(sums)
    for ref, side in ((mine, core), (theirs, 1 - core)):
        cols = pl.ds(pl.multiple_of(side * COLS, COLS), COLS)
        out_ref[:, cols] = (ref[...].astype(F32) * scale).astype(BF16)


CTX = ("z", "x", "core")


def move(value, z_shift=0, x_shift=0, core_shift=0, keep=lambda x: True):
    pairs = []
    for z in range(Z):
        for x in range(X):
            for core in range(CORES):
                to = ((z + z_shift) % Z * X + (x + x_shift) % X) * CORES
                if keep(x):
                    pairs.append(((z * X + x) * CORES + core, to + (core + core_shift) % CORES))
    return lax.ppermute(value, CTX, pairs)


def swap(value):
    return move(value, core_shift=1)


def exchange(sums):
    return lax.all_to_all(sums, ("core", "tp"), 0, 0, tiled=True)


def shape(dims, kind):
    return jax.ShapeDtypeStruct(dims, kind)


def shards(query_one, key_one, value_one, segments, query_base, key_two, value_two):
    core = lax.axis_index("core")

    def halves(arrays):
        low = jnp.stack([array[:, : array.shape[1] // 2] for array in arrays])
        high = jnp.stack([array[:, array.shape[1] // 2 :] for array in arrays])
        return jnp.where(core == 0, low, high), jnp.where(core == 0, high, low)

    segments_r = swap(segments)
    own_keep, own_send = halves((key_one, value_one, key_two, value_two))
    own0, packed, state, info = call(
        prep_kernel,
        (
            shape((PAIR, 2 * HEAD_DIM), BF16),
            shape((PAIR, 2 * HEAD_DIM), BF16),
            shape((144, HEAD_DIM), BF16),
            shape((8,), jnp.int32),
        ),
        [SMEM, SMEM, VMEM, VMEM],
        (VMEM,) * 3 + (SMEM,),
        name="prep",
    )(segments, segments_r, own_keep, swap(own_send))
    keep, query_send = halves((query_one, query_base))
    queries_r = swap(query_send)

    own1 = move(own0, z_shift=1)
    near = [move(state, x_shift=shift) for shift in (1, 2, 3)]
    prefix, plane = call(
        plane_kernel,
        (shape((HEAD_DIM + 8, HEAD_DIM), F32), shape((144, HEAD_DIM), BF16)),
        [SMEM] + [VMEM] * 5,
        (VMEM,) * 2,
        name="plane",
    )(info, state, *near, queries_r)
    far = [move(plane, z_shift=back) for back in (1, 2, 3, 4)]

    def after(known, value):
        return jnp.where(known >= 0, value, jnp.zeros_like(value))

    own2 = move(own1, z_shift=1)
    own3 = move(own2, z_shift=1)
    own4 = move(own3, z_shift=1)

    inside, query = call(
        inside_kernel,
        (shape((PAIR, COLS), F32), shape((PAIR, COLS), BF16)),
        [SMEM] + [VMEM] * 3,
        (VMEM,) * 2,
        name="inside",
    )(info, keep, queries_r, packed)
    first, sums, reach = call(
        first_kernel,
        (
            shape((PAIR, COLS), F32),
            shape((CORES * TP, 8, PAIR), F32),
            shape((1,), jnp.int32),
        ),
        [SMEM] + [VMEM] * 7,
        (VMEM, VMEM, SMEM),
        name="first",
    )(info, prefix, *far, inside, query)


    all_sums = exchange(sums)
    x = lax.axis_index("x")
    x_shifts = (1, 2, 3)
    others = [move(after(reach[0], own1), x_shift=shift) for shift in x_shifts]
    others += [move(own2, x_shift=shift) for shift in x_shifts]
    others += [move(own3, x_shift=shift) for shift in x_shifts]
    late4 = after(all_sums[0, 0, 0], own4)
    others += [move(jnp.where(x + shift < X, own0, late4), x_shift=shift) for shift in x_shifts]
    queries, tops, acc = call(
        near_kernel,
        (
            shape((REPEAT, PAIR, HEAD_DIM), BF16),
            shape((REPEAT, PAIR, HEAD_DIM), F32),
            shape((REPEAT, PAIR, 2 * HEAD_DIM), F32),
        ),
        [SMEM, SMEM] + [VMEM] * 15,
        (VMEM,) * 3,
        scratch=(
            pltpu.VMEM((SLOTS * PAIR, 3 * HEAD_DIM), BF16),
            pltpu.VMEM((PAIR, 3 * HEAD_DIM), BF16),
            pltpu.VMEM((PAIR, HEAD_DIM), F32),
            pltpu.SMEM((SLOTS,), jnp.int32),
            pltpu.SemaphoreType.DMA((10,)),
        ),
        name="near",
    )(
        info, reach, all_sums, first, keep, queries_r, own0, own1, own2, own3, own4, *others[:6]
    )
    mine, send, out_sums, _, _ = call(
        far_kernel,
        (
            shape((TOK, COLS), BF16),
            shape((TOK, COLS), BF16),
            shape((CORES * TP, 8, TOK), F32),
            shape((REPEAT, PAIR, HEAD_DIM), F32),
            shape((REPEAT, PAIR, 2 * HEAD_DIM), F32),
        ),
        [SMEM, SMEM] + [VMEM] * 9,
        (VMEM,) * 5,
        scratch=(
            pltpu.VMEM((SLOTS * PAIR, 3 * HEAD_DIM), BF16),
            pltpu.SMEM((SLOTS,), jnp.int32),
            pltpu.SemaphoreType.DMA((10,)),
        ),
        aliases={3: 3, 4: 4},
        name="far",
    )(info, reach, queries, tops, acc, *others[6:])
    theirs = swap(send)
    return call(
        last_kernel, shape((TOK, 2 * COLS), BF16), [VMEM] * 3, VMEM, name="last"
    )(exchange(out_sums), mine, theirs)


def solution(mesh):
    grid = Mesh(mesh.devices.reshape(Z, X, CORES, TP), ("z", "x", "core", "tp"))
    tokens, both = P(CTX), P(CTX, "tp")
    return jax.shard_map(
        shards,
        mesh=grid,
        in_specs=(both,) * 3 + (tokens,) + (both,) * 3,
        out_specs=both,
        check_vma=False,
    )
```

profile of v0, /device:TPU:103, one launch (start us, length us, event | category | flops | bytes accessed | tf_op | source)
XLA Modules:
  0.0 110.0 jit_solution(14858466226332037854)
XLA Ops:
  3.5 1.2 %collective-permute-done.seg_r = s32[192]{0:T(256)S(1)} collective-permute-done((s32[192]{0:T(256)S(1)}, s32[192]{0:T(256)S(1)}, u32[]{:S(2)}, u32[]{:S(2)}) %collective-permute-start) | collective-permute-done | bytes 800 | tf_op jit(solution)/shard_map/ppermute | solution.py:399
  4.7 1.4 %prep.1 = (bf16[384,256]{1,0:T(8,128)(2,1)S(1)}, bf16[384,256]{1,0:T(8,128)(2,1)S(1)}, bf16[144,128]{1,0:T(8,128)(2,1)S(1)}, s32[8]{0:T(128)S(1)}) custom-call(s32[192]{0:T(256)S(1)} %copy-done, s32[192]{0:T(256)S(1)} %collective-permute-done.seg_r, bf16[4,192,128]{2,1,0:T(8,128)(2,1)S(1)} %get-tuple-element.49.own, ...), custom_call_target="tpu_custom_call" | custom-call | tf_op jit(solution)/shard_map/prep/pallas_call | solution.py:424
  6.0 2.9 %collective-permute-start.10 = (bf16[384,256]{1,0:T(8,128)(2,1)S(1)}, bf16[384,256]{1,0:T(8,128)(2,1)S(1)}, u32[]{:S(2)}, u32[]{:S(2)}) collective-permute-start(bf16[384,256]{1,0:T(8,128)(2,1)S(1)} %get-tuple-element.32.own0), channel_id=1, source_target_pairs={{0,32},{4,36},{8,40},{12,44},{16,48},{20,52},{24,56},{28,60},{32,6... | collective-permute-start | bytes 589832 | tf_op jit(solution)/shard_map/ppermute | solution.py:399
  9.0 4.2 %collective-permute-done.10.own1 = bf16[384,256]{1,0:T(8,128)(2,1)S(1)} collective-permute-done((bf16[384,256]{1,0:T(8,128)(2,1)S(1)}, bf16[384,256]{1,0:T(8,128)(2,1)S(1)}, u32[]{:S(2)}, u32[]{:S(2)}) %collective-permute-start.10) | collective-permute-done | bytes 196640 | tf_op jit(solution)/shard_map/ppermute | solution.py:399
  13.1 3.4 %collective-permute-start.11 = (bf16[384,256]{1,0:T(8,128)(2,1)S(1)}, bf16[384,256]{1,0:T(8,128)(2,1)S(1)}, u32[]{:S(2)}, u32[]{:S(2)}) collective-permute-start(bf16[384,256]{1,0:T(8,128)(2,1)S(1)} %collective-permute-done.10.own1), channel_id=1, source_target_pairs={{0,32},{4,36},{8,40},{12,44},{16,48},{20,52},{24,56},{28,60},{32,6... | collective-permute-start | bytes 589832 | tf_op jit(solution)/shard_map/ppermute | solution.py:399
  16.7 2.1 %collective-permute-start.3 = (bf16[144,128]{1,0:T(8,128)(2,1)S(1)}, bf16[144,128]{1,0:T(8,128)(2,1)S(1)}, u32[]{:S(2)}, u32[]{:S(2)}) collective-permute-start(bf16[144,128]{1,0:T(8,128)(2,1)S(1)} %get-tuple-element.23.own), channel_id=1, source_target_pairs={{0,16},{4,20},{8,24},{12,28},{16,0},{20,4},{24,8},{28,12},{32,48},... | collective-permute-start | bytes 110600 | tf_op jit(solution)/shard_map/ppermute | solution.py:399
  19.7 1.4 %collective-permute-done.3.from2 = bf16[144,128]{1,0:T(8,128)(2,1)S(1)} collective-permute-done((bf16[144,128]{1,0:T(8,128)(2,1)S(1)}, bf16[144,128]{1,0:T(8,128)(2,1)S(1)}, u32[]{:S(2)}, u32[]{:S(2)}) %collective-permute-start.3) | collective-permute-done | bytes 36896 | tf_op jit(solution)/shard_map/ppermute | solution.py:399
  21.1 2.4 %collective-permute-done.4.from3 = bf16[144,128]{1,0:T(8,128)(2,1)S(1)} collective-permute-done((bf16[144,128]{1,0:T(8,128)(2,1)S(1)}, bf16[144,128]{1,0:T(8,128)(2,1)S(1)}, u32[]{:S(2)}, u32[]{:S(2)}) %collective-permute-start.4) | collective-permute-done | bytes 36896 | tf_op jit(solution)/shard_map/ppermute | solution.py:399
  25.9 3.9 %collective-permute-start.9 = (bf16[144,128]{1,0:T(8,128)(2,1)S(1)}, bf16[144,128]{1,0:T(8,128)(2,1)S(1)}, u32[]{:S(2)}, u32[]{:S(2)}) collective-permute-start(bf16[144,128]{1,0:T(8,128)(2,1)S(1)} %get-tuple-element.25), channel_id=1, source_target_pairs={{0,128},{4,132},{8,136},{12,140},{16,144},{20,148},{24,152},{28,15... | collective-permute-start | bytes 110600 | tf_op jit(solution)/shard_map/ppermute | solution.py:399
  29.8 1.9 %inside.1 = (f32[384,512]{1,0:T(8,128)S(1)}, bf16[384,512]{1,0:T(8,128)(2,1)S(1)}) custom-call(s32[8]{0:T(128)S(1)} %get-tuple-element.22.info, bf16[2,192,512]{2,1,0:T(8,128)(2,1)S(1)} %get-tuple-element.39.keep, bf16[2,192,512]{2,1,0:T(8,128)(2,1)S(1)} %collective-permute-done.5.queries_r, bf16[384,256]{1,0:T(8,128)(2,1)S(1)} %get-tuple-element.26.packed), custom_call_target="tpu_custom_call" | custom-call | tf_op jit(solution)/shard_map/inside/pallas_call | solution.py:457
  32.7 1.8 %first.1 = (f32[384,512]{1,0:T(8,128)S(1)}, f32[8,8,384]{2,1,0:T(8,128)}, s32[1]{0:T(128)}) custom-call(s32[8]{0:T(128)S(1)} %get-tuple-element.22.info, f32[136,128]{1,0:T(8,128)S(1)} %get-tuple-element.24.prefix, bf16[144,128]{1,0:T(8,128)(2,1)S(1)} %collective-permute-done.6.from1, bf16[144,128]{1,0:T(8,128)(2,1)S(1)} %collective-permute-done.7.from2, ...), custom_call_target="tpu_custom_call" | custom-call | tf_op jit(solution)/shard_map/first/pallas_call | solution.py:464
  35.1 2.3 %collective-permute-start.12 = (bf16[384,256]{1,0:T(8,128)(2,1)S(1)}, bf16[384,256]{1,0:T(8,128)(2,1)S(1)}, u32[]{:S(2)}, u32[]{:S(2)}) collective-permute-start(bf16[384,256]{1,0:T(8,128)(2,1)S(1)} %collective-permute-done.11.own2), channel_id=1, source_target_pairs={{0,32},{4,36},{8,40},{12,44},{16,48},{20,52},{24,56},{28,60},{32,6... | collective-permute-start | bytes 589832 | tf_op jit(solution)/shard_map/ppermute | solution.py:399
  37.8 2.2 %collective-permute-done.12.own3 = bf16[384,256]{1,0:T(8,128)(2,1)S(1)} collective-permute-done((bf16[384,256]{1,0:T(8,128)(2,1)S(1)}, bf16[384,256]{1,0:T(8,128)(2,1)S(1)}, u32[]{:S(2)}, u32[]{:S(2)}) %collective-permute-start.12) | collective-permute-done | bytes 196640 | tf_op jit(solution)/shard_map/ppermute | solution.py:399
  40.0 3.1 %collective-permute-start.13 = (bf16[384,256]{1,0:T(8,128)(2,1)S(1)}, bf16[384,256]{1,0:T(8,128)(2,1)S(1)}, u32[]{:S(2)}, u32[]{:S(2)}) collective-permute-start(bf16[384,256]{1,0:T(8,128)(2,1)S(1)} %collective-permute-done.12.own3), channel_id=1, source_target_pairs={{0,32},{4,36},{8,40},{12,44},{16,48},{20,52},{24,56},{28,60},{32,6... | collective-permute-start | bytes 589832 | tf_op jit(solution)/shard_map/ppermute | solution.py:399
  43.1 11.0 %all-to-all-start = ((f32[8,8,384]{2,1,0:T(8,128)}), f32[8,8,384]{2,1,0:T(8,128)S(1)}, u32[]{:S(2)}, u32[]{:S(2)}) async-start(f32[8,8,384]{2,1,0:T(8,128)} %get-tuple-element.30), calls=%async_computation | async-start | bytes 196608 | tf_op jit(solution)/shard_map/all_to_all | solution.py:407
  54.1 5.0 %all-to-all-done.sums = f32[8,8,384]{2,1,0:T(8,128)S(1)} async-done(((f32[8,8,384]{2,1,0:T(8,128)}), f32[8,8,384]{2,1,0:T(8,128)S(1)}, u32[]{:S(2)}, u32[]{:S(2)}) %all-to-all-start) | async-done | bytes 98336 | tf_op jit(solution)/shard_map/all_to_all | solution.py:407
  61.9 2.4 %collective-permute-start.20 = (bf16[384,256]{1,0:T(8,128)(2,1)S(1)}, bf16[384,256]{1,0:T(8,128)(2,1)S(1)}, u32[]{:S(2)}, u32[]{:S(2)}) collective-permute-start(bf16[384,256]{1,0:T(8,128)(2,1)S(1)} %collective-permute-done.12.own3), channel_id=1, source_target_pairs={{0,8},{4,12},{8,16},{12,20},{16,24},{20,28},{24,0},{28,4},{32,40},... | collective-permute-start | bytes 589832 | tf_op jit(solution)/shard_map/ppermute | solution.py:399
  64.4 1.2 %collective-permute-start.21 = (bf16[384,256]{1,0:T(8,128)(2,1)S(1)}, bf16[384,256]{1,0:T(8,128)(2,1)S(1)}, u32[]{:S(2)}, u32[]{:S(2)}) collective-permute-start(bf16[384,256]{1,0:T(8,128)(2,1)S(1)} %collective-permute-done.12.own3), channel_id=1, source_target_pairs={{0,16},{4,20},{8,24},{12,28},{16,0},{20,4},{24,8},{28,12},{32,48},... | collective-permute-start | bytes 589832 | tf_op jit(solution)/shard_map/ppermute | solution.py:399
  66.4 1.6 %collective-permute-done.18.refs_4_ = bf16[384,256]{1,0:T(8,128)(2,1)S(1)} collective-permute-done((bf16[384,256]{1,0:T(8,128)(2,1)S(1)}, bf16[384,256]{1,0:T(8,128)(2,1)S(1)}, u32[]{:S(2)}, u32[]{:S(2)}) %collective-permute-start.18) | collective-permute-done | bytes 196640 | tf_op jit(solution)/shard_map/ppermute | solution.py:399
  68.0 5.1 %collective-permute-start.23 = (bf16[384,256]{1,0:T(8,128)(2,1)S(1)}, bf16[384,256]{1,0:T(8,128)(2,1)S(1)}, u32[]{:S(2)}, u32[]{:S(2)}) collective-permute-start(bf16[384,256]{1,0:T(8,128)(2,1)S(1)} %get-tuple-element.43), channel_id=1, source_target_pairs={{0,8},{4,12},{8,16},{12,20},{16,24},{20,28},{24,0},{28,4},{32,40},... | collective-permute-start | bytes 589832 | tf_op jit(solution)/shard_map/ppermute | solution.py:399
  74.9 15.1 %near.1 = (bf16[4,384,128]{2,1,0:T(8,128)(2,1)S(1)}, f32[4,384,128]{2,1,0:T(8,128)S(1)}, f32[4,384,256]{2,1,0:T(8,128)S(1)}) custom-call(s32[8]{0:T(128)S(1)} %get-tuple-element.22.info, s32[1]{0:T(128)} %get-tuple-element.29.reach, f32[8,8,384]{2,1,0:T(8,128)S(1)} %all-to-all-done.sums, f32[384,512]{1,0:T(8,128)S(1)} %get-tuple-element.31.first, ...), custom_call_target="tpu_custom_call" | custom-call | tf_op jit(solution)/shard_map/near/pallas_call | solution.py:485
  90.1 6.7 %far.1 = (bf16[192,512]{1,0:T(8,128)(2,1)S(1)}, bf16[192,512]{1,0:T(8,128)(2,1)S(1)}, f32[8,8,192]{2,1,0:T(8,128)S(1)}, f32[4,384,128]{2,1,0:T(8,128)S(1)}, f32[4,384,256]{2,1,0:T(8,128)S(1)}) custom-call(s32[8]{0:T(128)S(1)} %get-tuple-element.22.info, s32[1]{0:T(128)} %get-tuple-element.29.reach, ...), custom_call_target="tpu_custom_call", output_to_operand_aliasing={{3}: (3, {}), {4}: (4, {})} | custom-call | tf_op jit(solution)/shard_map/far/pallas_call | solution.py:505
  96.8 4.9 %collective-permute-start.26 = (bf16[192,512]{1,0:T(8,128)(2,1)S(1)}, bf16[192,512]{1,0:T(8,128)(2,1)S(1)}, u32[]{:S(2)}, u32[]{:S(2)}) collective-permute-start(bf16[192,512]{1,0:T(8,128)(2,1)S(1)} %get-tuple-element.38), channel_id=1, source_target_pairs={{0,4},{4,0},{8,12},{12,8},{16,20},{20,16},{24,28},{28,24},{32,36},... | collective-permute-start | bytes 589832 | tf_op jit(solution)/shard_map/ppermute | solution.py:399
  101.7 7.3 %all_to_all.10.sums = f32[8,8,192]{2,1,0:T(8,128)S(1)} all-to-all(f32[8,8,192]{2,1,0:T(8,128)S(1)} %get-tuple-element.36), channel_id=1, replica_groups=mesh['z'=8,'x'=4,'core'=2,'tp'=4] {'core','tp'}, dimensions={0} | all-to-all | bytes 98304 | tf_op jit(solution)/shard_map/all_to_all | solution.py:407
  (54 shorter events, 14.1 us)
Async XLA Ops:
  2.9 20.6 %collective-permute-start.5 = (bf16[2,192,512]{2,1,0:T(8,128)(2,1)S(1)}, bf16[2,192,512]{2,1,0:T(8,128)(2,1)S(1)}, u32[]{:S(2)}, u32[]{:S(2)}) collective-permute-start(bf16[2,192,512]{2,1,0:T(8,128)(2,1)S(1)} %get-tuple-element.40), channel_id=1, source_target_pairs={{0,4},{4,0},{8,12},{12,8},{16,20},{20,16},{24,28},{28,24},{32,36},... | collective-permute-start | bytes 1179656 | tf_op jit(solution)/shard_map/ppermute | solution.py:399
  6.0 7.1 %collective-permute-start.10 = (bf16[384,256]{1,0:T(8,128)(2,1)S(1)}, bf16[384,256]{1,0:T(8,128)(2,1)S(1)}, u32[]{:S(2)}, u32[]{:S(2)}) collective-permute-start(bf16[384,256]{1,0:T(8,128)(2,1)S(1)} %get-tuple-element.32.own0), channel_id=1, source_target_pairs={{0,32},{4,36},{8,40},{12,44},{16,48},{20,52},{24,56},{28,60},{32,6... | collective-permute-start | bytes 589832 | tf_op jit(solution)/shard_map/ppermute | solution.py:399
  13.1 21.9 %collective-permute-start.11 = (bf16[384,256]{1,0:T(8,128)(2,1)S(1)}, bf16[384,256]{1,0:T(8,128)(2,1)S(1)}, u32[]{:S(2)}, u32[]{:S(2)}) collective-permute-start(bf16[384,256]{1,0:T(8,128)(2,1)S(1)} %collective-permute-done.10.own1), channel_id=1, source_target_pairs={{0,32},{4,36},{8,40},{12,44},{16,48},{20,52},{24,56},{28,60},{32,6... | collective-permute-start | bytes 589832 | tf_op jit(solution)/shard_map/ppermute | solution.py:399
  18.9 4.6 %collective-permute-start.4 = (bf16[144,128]{1,0:T(8,128)(2,1)S(1)}, bf16[144,128]{1,0:T(8,128)(2,1)S(1)}, u32[]{:S(2)}, u32[]{:S(2)}) collective-permute-start(bf16[144,128]{1,0:T(8,128)(2,1)S(1)} %get-tuple-element.23.own), channel_id=1, source_target_pairs={{0,24},{4,28},{8,0},{12,4},{16,8},{20,12},{24,16},{28,20},{32,56},... | collective-permute-start | bytes 110600 | tf_op jit(solution)/shard_map/ppermute | solution.py:399
  24.1 7.7 %collective-permute-start.6 = (bf16[144,128]{1,0:T(8,128)(2,1)S(1)}, bf16[144,128]{1,0:T(8,128)(2,1)S(1)}, u32[]{:S(2)}, u32[]{:S(2)}) collective-permute-start(bf16[144,128]{1,0:T(8,128)(2,1)S(1)} %get-tuple-element.25), channel_id=1, source_target_pairs={{0,32},{4,36},{8,40},{12,44},{16,48},{20,52},{24,56},{28,60},{32,6... | collective-permute-start | bytes 110600 | tf_op jit(solution)/shard_map/ppermute | solution.py:399
  24.2 7.6 %collective-permute-start.7 = (bf16[144,128]{1,0:T(8,128)(2,1)S(1)}, bf16[144,128]{1,0:T(8,128)(2,1)S(1)}, u32[]{:S(2)}, u32[]{:S(2)}) collective-permute-start(bf16[144,128]{1,0:T(8,128)(2,1)S(1)} %get-tuple-element.25), channel_id=1, source_target_pairs={{0,64},{4,68},{8,72},{12,76},{16,80},{20,84},{24,88},{28,92},{32,9... | collective-permute-start | bytes 110600 | tf_op jit(solution)/shard_map/ppermute | solution.py:399
  24.9 6.9 %collective-permute-start.8 = (bf16[144,128]{1,0:T(8,128)(2,1)S(1)}, bf16[144,128]{1,0:T(8,128)(2,1)S(1)}, u32[]{:S(2)}, u32[]{:S(2)}) collective-permute-start(bf16[144,128]{1,0:T(8,128)(2,1)S(1)} %get-tuple-element.25), channel_id=1, source_target_pairs={{0,96},{4,100},{8,104},{12,108},{16,112},{20,116},{24,120},{28,124... | collective-permute-start | bytes 110600 | tf_op jit(solution)/shard_map/ppermute | solution.py:399
  25.9 6.7 %collective-permute-start.9 = (bf16[144,128]{1,0:T(8,128)(2,1)S(1)}, bf16[144,128]{1,0:T(8,128)(2,1)S(1)}, u32[]{:S(2)}, u32[]{:S(2)}) collective-permute-start(bf16[144,128]{1,0:T(8,128)(2,1)S(1)} %get-tuple-element.25), channel_id=1, source_target_pairs={{0,128},{4,132},{8,136},{12,140},{16,144},{20,148},{24,152},{28,15... | collective-permute-start | bytes 110600 | tf_op jit(solution)/shard_map/ppermute | solution.py:399
  35.1 4.9 %collective-permute-start.12 = (bf16[384,256]{1,0:T(8,128)(2,1)S(1)}, bf16[384,256]{1,0:T(8,128)(2,1)S(1)}, u32[]{:S(2)}, u32[]{:S(2)}) collective-permute-start(bf16[384,256]{1,0:T(8,128)(2,1)S(1)} %collective-permute-done.11.own2), channel_id=1, source_target_pairs={{0,32},{4,36},{8,40},{12,44},{16,48},{20,52},{24,56},{28,60},{32,6... | collective-permute-start | bytes 589832 | tf_op jit(solution)/shard_map/ppermute | solution.py:399
  37.4 23.3 %collective-permute-start.14 = (bf16[384,256]{1,0:T(8,128)(2,1)S(1)}, bf16[384,256]{1,0:T(8,128)(2,1)S(1)}, u32[]{:S(2)}, u32[]{:S(2)}) collective-permute-start(bf16[384,256]{1,0:T(8,128)(2,1)S(1)} %broadcast_select_fusion.6), channel_id=1, source_target_pairs={{0,8},{4,12},{8,16},{12,20},{16,24},{20,28},{24,0},{28,4},{32,40},... | collective-permute-start | bytes 589832 | tf_op jit(solution)/shard_map/ppermute | solution.py:399
  37.8 23.3 %collective-permute-start.15 = (bf16[384,256]{1,0:T(8,128)(2,1)S(1)}, bf16[384,256]{1,0:T(8,128)(2,1)S(1)}, u32[]{:S(2)}, u32[]{:S(2)}) collective-permute-start(bf16[384,256]{1,0:T(8,128)(2,1)S(1)} %broadcast_select_fusion.6), channel_id=1, source_target_pairs={{0,16},{4,20},{8,24},{12,28},{16,0},{20,4},{24,8},{28,12},{32,48},... | collective-permute-start | bytes 589832 | tf_op jit(solution)/shard_map/ppermute | solution.py:399
  40.0 21.9 %collective-permute-start.13 = (bf16[384,256]{1,0:T(8,128)(2,1)S(1)}, bf16[384,256]{1,0:T(8,128)(2,1)S(1)}, u32[]{:S(2)}, u32[]{:S(2)}) collective-permute-start(bf16[384,256]{1,0:T(8,128)(2,1)S(1)} %collective-permute-done.12.own3), channel_id=1, source_target_pairs={{0,32},{4,36},{8,40},{12,44},{16,48},{20,52},{24,56},{28,60},{32,6... | collective-permute-start | bytes 589832 | tf_op jit(solution)/shard_map/ppermute | solution.py:399
  43.1 16.0 %all-to-all-start = ((f32[8,8,384]{2,1,0:T(8,128)}), f32[8,8,384]{2,1,0:T(8,128)S(1)}, u32[]{:S(2)}, u32[]{:S(2)}) async-start(f32[8,8,384]{2,1,0:T(8,128)} %get-tuple-element.30), calls=%async_computation | async-start | bytes 196608 | tf_op jit(solution)/shard_map/all_to_all | solution.py:407
  54.1 10.3 %collective-permute-start.16 = (bf16[384,256]{1,0:T(8,128)(2,1)S(1)}, bf16[384,256]{1,0:T(8,128)(2,1)S(1)}, u32[]{:S(2)}, u32[]{:S(2)}) collective-permute-start(bf16[384,256]{1,0:T(8,128)(2,1)S(1)} %broadcast_select_fusion.6), channel_id=1, source_target_pairs={{0,24},{4,28},{8,0},{12,4},{16,8},{20,12},{24,16},{28,20},{32,56},... | collective-permute-start | bytes 589832 | tf_op jit(solution)/shard_map/ppermute | solution.py:399
  60.3 6.2 %collective-permute-start.17 = (bf16[384,256]{1,0:T(8,128)(2,1)S(1)}, bf16[384,256]{1,0:T(8,128)(2,1)S(1)}, u32[]{:S(2)}, u32[]{:S(2)}) collective-permute-start(bf16[384,256]{1,0:T(8,128)(2,1)S(1)} %collective-permute-done.11.own2), channel_id=1, source_target_pairs={{0,8},{4,12},{8,16},{12,20},{16,24},{20,28},{24,0},{28,4},{32,40},... | collective-permute-start | bytes 589832 | tf_op jit(solution)/shard_map/ppermute | solution.py:399
  60.7 7.3 %collective-permute-start.18 = (bf16[384,256]{1,0:T(8,128)(2,1)S(1)}, bf16[384,256]{1,0:T(8,128)(2,1)S(1)}, u32[]{:S(2)}, u32[]{:S(2)}) collective-permute-start(bf16[384,256]{1,0:T(8,128)(2,1)S(1)} %collective-permute-done.11.own2), channel_id=1, source_target_pairs={{0,16},{4,20},{8,24},{12,28},{16,0},{20,4},{24,8},{28,12},{32,48},... | collective-permute-start | bytes 589832 | tf_op jit(solution)/shard_map/ppermute | solution.py:399
  61.1 13.1 %collective-permute-start.19 = (bf16[384,256]{1,0:T(8,128)(2,1)S(1)}, bf16[384,256]{1,0:T(8,128)(2,1)S(1)}, u32[]{:S(2)}, u32[]{:S(2)}) collective-permute-start(bf16[384,256]{1,0:T(8,128)(2,1)S(1)} %collective-permute-done.11.own2), channel_id=1, source_target_pairs={{0,24},{4,28},{8,0},{12,4},{16,8},{20,12},{24,16},{28,20},{32,56},... | collective-permute-start | bytes 589832 | tf_op jit(solution)/shard_map/ppermute | solution.py:399
  61.9 13.0 %collective-permute-start.20 = (bf16[384,256]{1,0:T(8,128)(2,1)S(1)}, bf16[384,256]{1,0:T(8,128)(2,1)S(1)}, u32[]{:S(2)}, u32[]{:S(2)}) collective-permute-start(bf16[384,256]{1,0:T(8,128)(2,1)S(1)} %collective-permute-done.12.own3), channel_id=1, source_target_pairs={{0,8},{4,12},{8,16},{12,20},{16,24},{20,28},{24,0},{28,4},{32,40},... | collective-permute-start | bytes 589832 | tf_op jit(solution)/shard_map/ppermute | solution.py:399
  64.4 25.7 %collective-permute-start.21 = (bf16[384,256]{1,0:T(8,128)(2,1)S(1)}, bf16[384,256]{1,0:T(8,128)(2,1)S(1)}, u32[]{:S(2)}, u32[]{:S(2)}) collective-permute-start(bf16[384,256]{1,0:T(8,128)(2,1)S(1)} %collective-permute-done.12.own3), channel_id=1, source_target_pairs={{0,16},{4,20},{8,24},{12,28},{16,0},{20,4},{24,8},{28,12},{32,48},... | collective-permute-start | bytes 589832 | tf_op jit(solution)/shard_map/ppermute | solution.py:399
  66.4 23.6 %collective-permute-start.22 = (bf16[384,256]{1,0:T(8,128)(2,1)S(1)}, bf16[384,256]{1,0:T(8,128)(2,1)S(1)}, u32[]{:S(2)}, u32[]{:S(2)}) collective-permute-start(bf16[384,256]{1,0:T(8,128)(2,1)S(1)} %collective-permute-done.12.own3), channel_id=1, source_target_pairs={{0,24},{4,28},{8,0},{12,4},{16,8},{20,12},{24,16},{28,20},{32,56},... | collective-permute-start | bytes 589832 | tf_op jit(solution)/shard_map/ppermute | solution.py:399
  68.0 22.1 %collective-permute-start.23 = (bf16[384,256]{1,0:T(8,128)(2,1)S(1)}, bf16[384,256]{1,0:T(8,128)(2,1)S(1)}, u32[]{:S(2)}, u32[]{:S(2)}) collective-permute-start(bf16[384,256]{1,0:T(8,128)(2,1)S(1)} %get-tuple-element.43), channel_id=1, source_target_pairs={{0,8},{4,12},{8,16},{12,20},{16,24},{20,28},{24,0},{28,4},{32,40},... | collective-permute-start | bytes 589832 | tf_op jit(solution)/shard_map/ppermute | solution.py:399
  74.2 15.8 %collective-permute-start.24 = (bf16[384,256]{1,0:T(8,128)(2,1)S(1)}, bf16[384,256]{1,0:T(8,128)(2,1)S(1)}, u32[]{:S(2)}, u32[]{:S(2)}) collective-permute-start(bf16[384,256]{1,0:T(8,128)(2,1)S(1)} %get-tuple-element.42), channel_id=1, source_target_pairs={{0,16},{4,20},{8,24},{12,28},{16,0},{20,4},{24,8},{28,12},{32,48},... | collective-permute-start | bytes 589832 | tf_op jit(solution)/shard_map/ppermute | solution.py:399
  74.9 15.2 %collective-permute-start.25 = (bf16[384,256]{1,0:T(8,128)(2,1)S(1)}, bf16[384,256]{1,0:T(8,128)(2,1)S(1)}, u32[]{:S(2)}, u32[]{:S(2)}) collective-permute-start(bf16[384,256]{1,0:T(8,128)(2,1)S(1)} %get-tuple-element.41), channel_id=1, source_target_pairs={{0,24},{4,28},{8,0},{12,4},{16,8},{20,12},{24,16},{28,20},{32,56},... | collective-permute-start | bytes 589832 | tf_op jit(solution)/shard_map/ppermute | solution.py:399
  96.8 12.2 %collective-permute-start.26 = (bf16[192,512]{1,0:T(8,128)(2,1)S(1)}, bf16[192,512]{1,0:T(8,128)(2,1)S(1)}, u32[]{:S(2)}, u32[]{:S(2)}) collective-permute-start(bf16[192,512]{1,0:T(8,128)(2,1)S(1)} %get-tuple-element.38), channel_id=1, source_target_pairs={{0,4},{4,0},{8,12},{12,8},{16,20},{20,16},{24,28},{28,24},{32,36},... | collective-permute-start | bytes 589832 | tf_op jit(solution)/shard_map/ppermute | solution.py:399
  (7 other events, 18.3 us)
where the time goes:
time: 111 us; the launch traced here: 110 us
  starting transfers between devices  48.1 us (43%)
  Pallas kernels  28.5 us (26%)
  waiting for transfers between devices  21.9 us (20%)
  blocking collectives  7.35 us (7%)
  local copies, waits for them, and re-layouts  2.44 us (2%)
  between operations  1.49 us (1%)
    ppermute x27, starting transfers between devices, move(): return lax.ppermute(value, CTX, pairs)  37.2 us
    ppermute x27, waiting for transfers between devices, move(): return lax.ppermute(value, CTX, pairs)  16.9 us
    pallas_call x1, Pallas kernels, shards(): call(near_kernel, (shape((REPEAT, PAIR, HEAD_DIM), BF16), shape((REPEAT,...  15.1 us
    all_to_all x1, starting transfers between devices, exchange(): return lax.all_to_all(sums, ('core', 'tp'), 0, 0, tiled=True)  11 us
    all_to_all x1, blocking collectives, exchange(): return lax.all_to_all(sums, ('core', 'tp'), 0, 0, tiled=True)  7.35 us
    pallas_call x1, Pallas kernels, shards(): call(far_kernel, (shape((TOK, COLS), BF16), shape((TOK, COLS), BF16), sha...  6.68 us
    all_to_all x1, waiting for transfers between devices, exchange(): return lax.all_to_all(sums, ('core', 'tp'), 0, 0, tiled=True)  5.01 us
  transfers between devices with their start and end apart: 28, of which 12 were waited for; matrix products, arithmetic and copies ran while one was open for 1% of the time, Pallas kernels for 19%

commit v1 on v0

--- a/solution.py
+++ b/solution.py
@@ -108,9 +108,10 @@
 
 
 def plane_kernel(
-    info, own, from1, from2, from3, queries_r, prefix_ref, plane_ref
+    info, own, from1, from2, from3, own1, queries_r, prefix_ref, plane_ref, later1_ref
 ):
     x = place()[1]
+    later1_ref[...] = own1[...]
     first = info[3].astype(F32)
     items = [read_state(ref) for ref in (own, from1, from2, from3)]
     prefix = jnp.zeros((HEAD_DIM, HEAD_DIM), F32)
@@ -230,7 +231,7 @@
     )
 
 
-def sweep(queries, kv, tops, acc, rows, visible=None, begin=False):
+def sweep(queries, kv, tops, acc, rows, visible=None):
     ahead = scores_of(queries, kv, *TILES[0], rows)
     for at, (head, part) in enumerate(TILES):
         scores = ahead
@@ -239,25 +240,19 @@
         if visible is not None:
             scores = jnp.where(visible(part), scores, NEGATIVE)
         top = jnp.max(scores, axis=1, keepdims=True)
-        if begin:
-            top = jnp.broadcast_to(top, (TILE, HEAD_DIM))
-        else:
-            old_top = tops[head, part]
-            top = jnp.maximum(old_top, top)
+        old_top = tops[head, part]
+        top = jnp.maximum(old_top, top)
         wide_top = jnp.concatenate([top] * (scores.shape[1] // HEAD_DIM), axis=1)
         weights = jnp.exp2((scores - wide_top) * SCALE)
         summed = jnp.dot(weights.astype(BF16), kv[rows, HEAD_DIM:], preferred_element_type=F32)
         tops[head, part] = top
-        if begin:
-            acc[head, part] = summed
-        else:
-            shrink = jnp.exp2((old_top - top) * SCALE)
-            acc[head, part] = acc[head, part] * jnp.concatenate([shrink, shrink], axis=1) + summed
+        shrink = jnp.exp2((old_top - top) * SCALE)
+        acc[head, part] = acc[head, part] * jnp.concatenate([shrink, shrink], axis=1) + summed
 
 
 class Window:
-    def __init__(self, info, prior, blocks, kv, bounds, sems):
-        self.info, self.kv, self.bounds = info, kv, bounds
+    def __init__(self, prior, blocks, kv, bounds, sems):
+        self.kv, self.bounds = kv, bounds
         used = jnp.int32(0)
         self.copies = []
         for at, (ref, distance) in enumerate(blocks):
@@ -291,8 +286,7 @@
         def _(step):
             rows = pl.ds(pl.multiple_of(step * CHUNK * PAIR, CHUNK * PAIR), CHUNK * PAIR)
             low0, low1 = self.bounds[step * CHUNK], self.bounds[step * CHUNK + 1]
-            first_end = self.info[6]
-            whole = (low0 == 0) & (low1 == 0) & (first_end == PAIR)
+            whole = (low0 == 0) & (low1 == 0)
 
             @pl.when(whole)
             def _():
@@ -300,58 +294,63 @@
 
             @pl.when(jnp.logical_not(whole))
             def _():
-                def visible(part):
-                    row = lax.broadcasted_iota(jnp.int32, (TILE, CHUNK * PAIR), 0) + part.start
-                    column = lax.broadcasted_iota(jnp.int32, (TILE, CHUNK * PAIR), 1)
-                    low = jnp.where(column < PAIR, low0, PAIR + low1)
-                    return (column >= low) & (row < first_end)
-
-                sweep(queries, self.kv, tops, acc, rows, visible)
+                column = lax.broadcasted_iota(jnp.int32, (1, CHUNK * PAIR), 1)
+                seen = column >= jnp.where(column < PAIR, low0, PAIR + low1)
+                sweep(queries, self.kv, tops, acc, rows, lambda part: seen)
 
 
 SLOTS = 10
 
 
 def near_kernel(
-    info, reach, sums, first, keep, queries_r, own0, own1, own2, own3, own4, *refs
+    reach, sums, first, keep, queries_r, own1, own2, own3, own4, *refs
 ):
     others1, others2 = refs[:3], refs[3:6]
-    queries, tops, acc, kv, own, scales, bounds, sems = refs[6:]
+    queries, tops, acc, kv, scales, bounds, sems = refs[6:]
     _, x, core = place()
     blocks = [(own1, 4), (own2, 8), (own3, 12), (own4, 16)]
     for shift, other1, other2 in zip((1, 2, 3), others1, others2):
         wrapped = jnp.where(x < shift, 4, 0)
         blocks.append((other1, 4 + shift - wrapped))
         blocks.append((other2, 8 + shift - wrapped))
-    window = Window(info, reach[0], blocks, kv, bounds, sems)
-    own[:, : 2 * HEAD_DIM] = own0[...]
-    own[:, 2 * HEAD_DIM :] = jnp.ones((PAIR, HEAD_DIM), BF16)
+    window = Window(reach[0], blocks, kv, bounds, sems)
+    tops[...] = jnp.full(tops.shape, NEGATIVE, F32)
+    acc[...] = jnp.zeros(acc.shape, F32)
     scales[...] = jnp.broadcast_to(row_scale(sums), (PAIR, HEAD_DIM))
     for part, where in ((keep.at[1], rows_of(core)), (queries_r.at[1], rows_of(1 - core))):
         for head in range(REPEAT):
             cols = slice(head * HEAD_DIM, (head + 1) * HEAD_DIM)
             value = part[:, cols].astype(F32) + first[where, cols] * scales[where, :]
             queries[head, where, :] = value.astype(BF16)
-
-    def own_visible(part):
-        row = lax.broadcasted_iota(jnp.int32, (TILE, PAIR), 0) + part.start
-        column = lax.broadcasted_iota(jnp.int32, (TILE, PAIR), 1)
-        return (column <= row) & (column >= document_start(info, row))
-
-    sweep(queries, own, tops, acc, slice(0, PAIR), own_visible, begin=True)
     window.absorb(queries, tops, acc)
 
 
-def far_kernel(info, reach, queries, old_tops, old_acc, *refs):
+def far_kernel(info, reach, queries, old_tops, old_acc, own0, *refs):
     others3, others04 = refs[:3], refs[3:6]
-    mine_ref, send_ref, sums_ref, tops, acc, kv, bounds, sems = refs[6:]
+    mine_ref, send_ref, sums_ref, tops, acc, kv, own, bounds, sems = refs[6:]
     _, x, core = place()
     blocks = []
     for shift, other3, other04 in zip((1, 2, 3), others3, others04):
         blocks.append((other3, 12 + shift - jnp.where(x < shift, 4, 0)))
         blocks.append((other04, jnp.where(x < shift, 12 + shift, shift)))
-    window = Window(info, reach[0], blocks, kv, bounds, sems)
+    window = Window(reach[0], blocks, kv, bounds, sems)
+    own[:, : 2 * HEAD_DIM] = own0[...]
+    own[:, 2 * HEAD_DIM :] = jnp.ones((PAIR, HEAD_DIM), BF16)
     window.absorb(queries, tops, acc)
+
+    @pl.when(info[6] < PAIR)
+    def _():
+        in_first = lax.broadcasted_iota(jnp.int32, (PAIR, HEAD_DIM), 0) < info[6]
+        for head in range(REPEAT):
+            tops[head] = jnp.where(in_first, tops[head], NEGATIVE)
+            acc[head] = jnp.where(jnp.concatenate([in_first, in_first], axis=1), acc[head], 0.0)
+
+    def own_visible(part):
+        row = lax.broadcasted_iota(jnp.int32, (TILE, PAIR), 0) + part.start
+        column = lax.broadcasted_iota(jnp.int32, (TILE, PAIR), 1)
+        return (column <= row) & (column >= document_start(info, row))
+
+    sweep(queries, own, tops, acc, slice(0, PAIR), own_visible)
     for side in range(CORES):
         where = slice(side * TOK, (side + 1) * TOK)
         squares = jnp.zeros((TOK, HEAD_DIM), F32)
@@ -438,19 +437,23 @@
 
     own1 = move(own0, z_shift=1)
     near = [move(state, x_shift=shift) for shift in (1, 2, 3)]
-    prefix, plane = call(
+    prefix, plane, later1 = call(
         plane_kernel,
-        (shape((HEAD_DIM + 8, HEAD_DIM), F32), shape((144, HEAD_DIM), BF16)),
-        [SMEM] + [VMEM] * 5,
-        (VMEM,) * 2,
+        (
+            shape((HEAD_DIM + 8, HEAD_DIM), F32),
+            shape((144, HEAD_DIM), BF16),
+            shape((PAIR, 2 * HEAD_DIM), BF16),
+        ),
+        [SMEM] + [VMEM] * 6,
+        (VMEM,) * 3,
         name="plane",
-    )(info, state, *near, queries_r)
+    )(info, state, *near, own1, queries_r)
     far = [move(plane, z_shift=back) for back in (1, 2, 3, 4)]
 
     def after(known, value):
         return jnp.where(known >= 0, value, jnp.zeros_like(value))
 
-    own2 = move(own1, z_shift=1)
+    own2 = move(later1, z_shift=1)
     own3 = move(own2, z_shift=1)
     own4 = move(own3, z_shift=1)
 
@@ -489,18 +492,17 @@
             shape((REPEAT, PAIR, HEAD_DIM), F32),
             shape((REPEAT, PAIR, 2 * HEAD_DIM), F32),
         ),
-        [SMEM, SMEM] + [VMEM] * 15,
+        [SMEM] + [VMEM] * 14,
         (VMEM,) * 3,
         scratch=(
             pltpu.VMEM((SLOTS * PAIR, 3 * HEAD_DIM), BF16),
-            pltpu.VMEM((PAIR, 3 * HEAD_DIM), BF16),
             pltpu.VMEM((PAIR, HEAD_DIM), F32),
             pltpu.SMEM((SLOTS,), jnp.int32),
             pltpu.SemaphoreType.DMA((10,)),
         ),
         name="near",
     )(
-        info, reach, all_sums, first, keep, queries_r, own0, own1, own2, own3, own4, *others[:6]
+        reach, all_sums, first, keep, queries_r, own1, own2, own3, own4, *others[:6]
     )
     mine, send, out_sums, _, _ = call(
         far_kernel,
@@ -511,16 +513,17 @@
             shape((REPEAT, PAIR, HEAD_DIM), F32),
             shape((REPEAT, PAIR, 2 * HEAD_DIM), F32),
         ),
-        [SMEM, SMEM] + [VMEM] * 9,
+        [SMEM, SMEM] + [VMEM] * 10,
         (VMEM,) * 5,
         scratch=(
             pltpu.VMEM((SLOTS * PAIR, 3 * HEAD_DIM), BF16),
+            pltpu.VMEM((PAIR, 3 * HEAD_DIM), BF16),
             pltpu.SMEM((SLOTS,), jnp.int32),
             pltpu.SemaphoreType.DMA((10,)),
         ),
         aliases={3: 3, 4: 4},
         name="far",
-    )(info, reach, queries, tops, acc, *others[6:])
+    )(info, reach, queries, tops, acc, own0, *others[6:])
     theirs = swap(send)
     return call(
         last_kernel, shape((TOK, 2 * COLS), BF16), [VMEM] * 3, VMEM, name="last"

time: 111 us -> 106 us (0.955)
  waiting for transfers between devices: 21.9 us -> 17.3 us
    ppermute x27, waiting for transfers between devices: 16.9 us -> 12.3 us  [move(): return lax.ppermute(value, CTX, pairs)]
    pallas_call x1, Pallas kernels: 6.68 us -> 9.82 us  [shards(): call(far_kernel, (shape((TOK, COLS), BF16), shape((TOK, COLS), BF16), sha...]
    pallas_call x1, Pallas kernels: 15.1 us -> 12.3 us  [shards(): call(near_kernel, (shape((REPEAT, PAIR, HEAD_DIM), BF16), shape((REPEAT,...]
  transfers between devices with their start and end apart: 28 -> 28, of which waited for: 12 -> 11; matrix products, arithmetic and copies ran while one was open for 1% -> 1% of each run, Pallas kernels for 19% -> 16%
where the time goes in v1:
time: 106 us
  starting transfers between devices  48.5 us (46%)
  Pallas kernels  28.8 us (27%)
  waiting for transfers between devices  17.3 us (16%)
  blocking collectives  7.35 us (7%)
  local copies, waits for them, and re-layouts  2.42 us (2%)
  between operations  1.47 us (1%)
    ppermute x27, starting transfers between devices, move(): return lax.ppermute(value, CTX, pairs)  36.5 us
    pallas_call x1, Pallas kernels, shards(): call(near_kernel, (shape((REPEAT, PAIR, HEAD_DIM), BF16), shape((REPEAT,...  12.3 us
    ppermute x27, waiting for transfers between devices, move(): return lax.ppermute(value, CTX, pairs)  12.3 us
    all_to_all x1, starting transfers between devices, exchange(): return lax.all_to_all(sums, ('core', 'tp'), 0, 0, tiled=True)  12 us
    pallas_call x1, Pallas kernels, shards(): call(far_kernel, (shape((TOK, COLS), BF16), shape((TOK, COLS), BF16), sha...  9.82 us
    all_to_all x1, blocking collectives, exchange(): return lax.all_to_all(sums, ('core', 'tp'), 0, 0, tiled=True)  7.35 us
    all_to_all x1, waiting for transfers between devices, exchange(): return lax.all_to_all(sums, ('core', 'tp'), 0, 0, tiled=True)  5.01 us
  transfers between devices with their start and end apart: 28, of which 11 were waited for; matrix products, arithmetic and copies ran while one was open for 1% of the time, Pallas kernels for 16%

profile of v1, /device:TPU:103, one launch (start us, length us, event | category | flops | bytes accessed | tf_op | source)
XLA Modules:
  0.0 106.0 jit_solution(3217417572735631107)
XLA Ops:
  3.4 1.2 %collective-permute-done.seg_r = s32[192]{0:T(256)S(1)} collective-permute-done((s32[192]{0:T(256)S(1)}, s32[192]{0:T(256)S(1)}, u32[]{:S(2)}, u32[]{:S(2)}) %collective-permute-start) | collective-permute-done | bytes 800 | tf_op jit(solution)/shard_map/ppermute | solution.py:398
  4.7 1.4 %prep.1 = (bf16[384,256]{1,0:T(8,128)(2,1)S(1)}, bf16[384,256]{1,0:T(8,128)(2,1)S(1)}, bf16[144,128]{1,0:T(8,128)(2,1)S(1)}, s32[8]{0:T(128)S(1)}) custom-call(s32[192]{0:T(256)S(1)} %copy-done, s32[192]{0:T(256)S(1)} %collective-permute-done.seg_r, bf16[4,192,128]{2,1,0:T(8,128)(2,1)S(1)} %get-tuple-element.51.own, ...), custom_call_target="tpu_custom_call" | custom-call | tf_op jit(solution)/shard_map/prep/pallas_call | solution.py:423
  6.0 2.9 %collective-permute-start.5 = (bf16[384,256]{1,0:T(8,128)(2,1)S(1)}, bf16[384,256]{1,0:T(8,128)(2,1)S(1)}, u32[]{:S(2)}, u32[]{:S(2)}) collective-permute-start(bf16[384,256]{1,0:T(8,128)(2,1)S(1)} %get-tuple-element.25.own0), channel_id=1, source_target_pairs={{0,32},{4,36},{8,40},{12,44},{16,48},{20,52},{24,56},{28,60},{32,6... | collective-permute-start | bytes 589832 | tf_op jit(solution)/shard_map/ppermute | solution.py:398
  9.2 2.1 %collective-permute-start.3 = (bf16[144,128]{1,0:T(8,128)(2,1)S(1)}, bf16[144,128]{1,0:T(8,128)(2,1)S(1)}, u32[]{:S(2)}, u32[]{:S(2)}) collective-permute-start(bf16[144,128]{1,0:T(8,128)(2,1)S(1)} %get-tuple-element.24.own), channel_id=1, source_target_pairs={{0,16},{4,20},{8,24},{12,28},{16,0},{20,4},{24,8},{28,12},{32,48},... | collective-permute-start | bytes 110600 | tf_op jit(solution)/shard_map/ppermute | solution.py:398
  12.1 1.4 %collective-permute-done.3.from2 = bf16[144,128]{1,0:T(8,128)(2,1)S(1)} collective-permute-done((bf16[144,128]{1,0:T(8,128)(2,1)S(1)}, bf16[144,128]{1,0:T(8,128)(2,1)S(1)}, u32[]{:S(2)}, u32[]{:S(2)}) %collective-permute-start.3) | collective-permute-done | bytes 36896 | tf_op jit(solution)/shard_map/ppermute | solution.py:398
  13.5 1.8 %collective-permute-done.4.from3 = bf16[144,128]{1,0:T(8,128)(2,1)S(1)} collective-permute-done((bf16[144,128]{1,0:T(8,128)(2,1)S(1)}, bf16[144,128]{1,0:T(8,128)(2,1)S(1)}, u32[]{:S(2)}, u32[]{:S(2)}) %collective-permute-start.4) | collective-permute-done | bytes 36896 | tf_op jit(solution)/shard_map/ppermute | solution.py:398
  15.9 1.3 %collective-permute-start.11 = (bf16[384,256]{1,0:T(8,128)(2,1)S(1)}, bf16[384,256]{1,0:T(8,128)(2,1)S(1)}, u32[]{:S(2)}, u32[]{:S(2)}) collective-permute-start(bf16[384,256]{1,0:T(8,128)(2,1)S(1)} %get-tuple-element.34), channel_id=1, source_target_pairs={{0,32},{4,36},{8,40},{12,44},{16,48},{20,52},{24,56},{28,60},{32,6... | collective-permute-start | bytes 589832 | tf_op jit(solution)/shard_map/ppermute | solution.py:398
  18.0 1.4 %collective-permute-start.9 = (bf16[144,128]{1,0:T(8,128)(2,1)S(1)}, bf16[144,128]{1,0:T(8,128)(2,1)S(1)}, u32[]{:S(2)}, u32[]{:S(2)}) collective-permute-start(bf16[144,128]{1,0:T(8,128)(2,1)S(1)} %get-tuple-element.27), channel_id=1, source_target_pairs={{0,96},{4,100},{8,104},{12,108},{16,112},{20,116},{24,120},{28,124... | collective-permute-start | bytes 110600 | tf_op jit(solution)/shard_map/ppermute | solution.py:398
  19.4 4.2 %collective-permute-start.10 = (bf16[144,128]{1,0:T(8,128)(2,1)S(1)}, bf16[144,128]{1,0:T(8,128)(2,1)S(1)}, u32[]{:S(2)}, u32[]{:S(2)}) collective-permute-start(bf16[144,128]{1,0:T(8,128)(2,1)S(1)} %get-tuple-element.27), channel_id=1, source_target_pairs={{0,128},{4,132},{8,136},{12,140},{16,144},{20,148},{24,152},{28,15... | collective-permute-start | bytes 110600 | tf_op jit(solution)/shard_map/ppermute | solution.py:398
  23.6 1.9 %inside.1 = (f32[384,512]{1,0:T(8,128)S(1)}, bf16[384,512]{1,0:T(8,128)(2,1)S(1)}) custom-call(s32[8]{0:T(128)S(1)} %get-tuple-element.23.info, bf16[2,192,512]{2,1,0:T(8,128)(2,1)S(1)} %get-tuple-element.41.keep, bf16[2,192,512]{2,1,0:T(8,128)(2,1)S(1)} %collective-permute-done.6.queries_r, bf16[384,256]{1,0:T(8,128)(2,1)S(1)} %get-tuple-element.28.packed), custom_call_target="tpu_custom_call" | custom-call | tf_op jit(solution)/shard_map/inside/pallas_call | solution.py:460
  26.2 1.8 %first.1 = (f32[384,512]{1,0:T(8,128)S(1)}, f32[8,8,384]{2,1,0:T(8,128)}, s32[1]{0:T(128)}) custom-call(s32[8]{0:T(128)S(1)} %get-tuple-element.23.info, f32[136,128]{1,0:T(8,128)S(1)} %get-tuple-element.26.prefix, bf16[144,128]{1,0:T(8,128)(2,1)S(1)} %collective-permute-done.7.from1, bf16[144,128]{1,0:T(8,128)(2,1)S(1)} %collective-permute-done.8.from2, ...), custom_call_target="tpu_custom_call" | custom-call | tf_op jit(solution)/shard_map/first/pallas_call | solution.py:467
  28.6 2.9 %collective-permute-start.12 = (bf16[384,256]{1,0:T(8,128)(2,1)S(1)}, bf16[384,256]{1,0:T(8,128)(2,1)S(1)}, u32[]{:S(2)}, u32[]{:S(2)}) collective-permute-start(bf16[384,256]{1,0:T(8,128)(2,1)S(1)} %collective-permute-done.11.own2), channel_id=1, source_target_pairs={{0,32},{4,36},{8,40},{12,44},{16,48},{20,52},{24,56},{28,60},{32,6... | collective-permute-start | bytes 589832 | tf_op jit(solution)/shard_map/ppermute | solution.py:398
  34.1 3.1 %collective-permute-start.13 = (bf16[384,256]{1,0:T(8,128)(2,1)S(1)}, bf16[384,256]{1,0:T(8,128)(2,1)S(1)}, u32[]{:S(2)}, u32[]{:S(2)}) collective-permute-start(bf16[384,256]{1,0:T(8,128)(2,1)S(1)} %collective-permute-done.12.own3), channel_id=1, source_target_pairs={{0,32},{4,36},{8,40},{12,44},{16,48},{20,52},{24,56},{28,60},{32,6... | collective-permute-start | bytes 589832 | tf_op jit(solution)/shard_map/ppermute | solution.py:398
  37.2 12.0 %all-to-all-start = ((f32[8,8,384]{2,1,0:T(8,128)}), f32[8,8,384]{2,1,0:T(8,128)S(1)}, u32[]{:S(2)}, u32[]{:S(2)}) async-start(f32[8,8,384]{2,1,0:T(8,128)} %get-tuple-element.32), calls=%async_computation | async-start | bytes 196608 | tf_op jit(solution)/shard_map/all_to_all | solution.py:406
  49.2 5.0 %all-to-all-done.sums = f32[8,8,384]{2,1,0:T(8,128)S(1)} async-done(((f32[8,8,384]{2,1,0:T(8,128)}), f32[8,8,384]{2,1,0:T(8,128)S(1)}, u32[]{:S(2)}, u32[]{:S(2)}) %all-to-all-start) | async-done | bytes 98336 | tf_op jit(solution)/shard_map/all_to_all | solution.py:406
  55.8 1.2 %collective-permute-start.18 = (bf16[384,256]{1,0:T(8,128)(2,1)S(1)}, bf16[384,256]{1,0:T(8,128)(2,1)S(1)}, u32[]{:S(2)}, u32[]{:S(2)}) collective-permute-start(bf16[384,256]{1,0:T(8,128)(2,1)S(1)} %collective-permute-done.11.own2), channel_id=1, source_target_pairs={{0,16},{4,20},{8,24},{12,28},{16,0},{20,4},{24,8},{28,12},{32,48},... | collective-permute-start | bytes 589832 | tf_op jit(solution)/shard_map/ppermute | solution.py:398
  57.0 2.6 %collective-permute-start.20 = (bf16[384,256]{1,0:T(8,128)(2,1)S(1)}, bf16[384,256]{1,0:T(8,128)(2,1)S(1)}, u32[]{:S(2)}, u32[]{:S(2)}) collective-permute-start(bf16[384,256]{1,0:T(8,128)(2,1)S(1)} %collective-permute-done.12.own3), channel_id=1, source_target_pairs={{0,8},{4,12},{8,16},{12,20},{16,24},{20,28},{24,0},{28,4},{32,40},... | collective-permute-start | bytes 589832 | tf_op jit(solution)/shard_map/ppermute | solution.py:398
  61.6 1.5 %collective-permute-done.18.refs_4_ = bf16[384,256]{1,0:T(8,128)(2,1)S(1)} collective-permute-done((bf16[384,256]{1,0:T(8,128)(2,1)S(1)}, bf16[384,256]{1,0:T(8,128)(2,1)S(1)}, u32[]{:S(2)}, u32[]{:S(2)}) %collective-permute-start.18) | collective-permute-done | bytes 196640 | tf_op jit(solution)/shard_map/ppermute | solution.py:398
  63.1 5.1 %collective-permute-start.23 = (bf16[384,256]{1,0:T(8,128)(2,1)S(1)}, bf16[384,256]{1,0:T(8,128)(2,1)S(1)}, u32[]{:S(2)}, u32[]{:S(2)}) collective-permute-start(bf16[384,256]{1,0:T(8,128)(2,1)S(1)} %get-tuple-element.45), channel_id=1, source_target_pairs={{0,8},{4,12},{8,16},{12,20},{16,24},{20,28},{24,0},{28,4},{32,40},... | collective-permute-start | bytes 589832 | tf_op jit(solution)/shard_map/ppermute | solution.py:398
  70.5 12.3 %near.1 = (bf16[4,384,128]{2,1,0:T(8,128)(2,1)S(1)}, f32[4,384,128]{2,1,0:T(8,128)S(1)}, f32[4,384,256]{2,1,0:T(8,128)S(1)}) custom-call(s32[1]{0:T(128)} %get-tuple-element.31.reach, f32[8,8,384]{2,1,0:T(8,128)S(1)} %all-to-all-done.sums, f32[384,512]{1,0:T(8,128)S(1)} %get-tuple-element.33.first, bf16[2,192,512]{2,1,0:T(8,128)(2,1)S(1)} %get-tuple-element.41.keep, ...), custom_call_target="tpu_custom_call" | custom-call | tf_op jit(solution)/shard_map/near/pallas_call | solution.py:488
  82.9 2.3 %collective-permute-done.25.refs_5_ = bf16[384,256]{1,0:T(8,128)(2,1)S(1)} collective-permute-done((bf16[384,256]{1,0:T(8,128)(2,1)S(1)}, bf16[384,256]{1,0:T(8,128)(2,1)S(1)}, u32[]{:S(2)}, u32[]{:S(2)}) %collective-permute-start.25) | collective-permute-done | bytes 196640 | tf_op jit(solution)/shard_map/ppermute | solution.py:398
  85.2 9.8 %far.1 = (bf16[192,512]{1,0:T(8,128)(2,1)S(1)}, bf16[192,512]{1,0:T(8,128)(2,1)S(1)}, f32[8,8,192]{2,1,0:T(8,128)S(1)}, f32[4,384,128]{2,1,0:T(8,128)S(1)}, f32[4,384,256]{2,1,0:T(8,128)S(1)}) custom-call(s32[8]{0:T(128)S(1)} %get-tuple-element.23.info, s32[1]{0:T(128)} %get-tuple-element.31.reach, ...), custom_call_target="tpu_custom_call", output_to_operand_aliasing={{3}: (3, {}), {4}: (4, {})} | custom-call | tf_op jit(solution)/shard_map/far/pallas_call | solution.py:507
  95.0 2.6 %collective-permute-start.26 = (bf16[192,512]{1,0:T(8,128)(2,1)S(1)}, bf16[192,512]{1,0:T(8,128)(2,1)S(1)}, u32[]{:S(2)}, u32[]{:S(2)}) collective-permute-start(bf16[192,512]{1,0:T(8,128)(2,1)S(1)} %get-tuple-element.40), channel_id=1, source_target_pairs={{0,4},{4,0},{8,12},{12,8},{16,20},{20,16},{24,28},{28,24},{32,36},... | collective-permute-start | bytes 589832 | tf_op jit(solution)/shard_map/ppermute | solution.py:398
  97.6 7.3 %all_to_all.10.sums = f32[8,8,192]{2,1,0:T(8,128)S(1)} all-to-all(f32[8,8,192]{2,1,0:T(8,128)S(1)} %get-tuple-element.38), channel_id=1, replica_groups=mesh['z'=8,'x'=4,'core'=2,'tp'=4] {'core','tp'}, dimensions={0} | all-to-all | bytes 98304 | tf_op jit(solution)/shard_map/all_to_all | solution.py:406
  (54 shorter events, 15.2 us)
Async XLA Ops:
  2.8 12.5 %collective-permute-start.6 = (bf16[2,192,512]{2,1,0:T(8,128)(2,1)S(1)}, bf16[2,192,512]{2,1,0:T(8,128)(2,1)S(1)}, u32[]{:S(2)}, u32[]{:S(2)}) collective-permute-start(bf16[2,192,512]{2,1,0:T(8,128)(2,1)S(1)} %get-tuple-element.42), channel_id=1, source_target_pairs={{0,4},{4,0},{8,12},{12,8},{16,20},{20,16},{24,28},{28,24},{32,36},... | collective-permute-start | bytes 1179656 | tf_op jit(solution)/shard_map/ppermute | solution.py:398
  6.0 9.3 %collective-permute-start.5 = (bf16[384,256]{1,0:T(8,128)(2,1)S(1)}, bf16[384,256]{1,0:T(8,128)(2,1)S(1)}, u32[]{:S(2)}, u32[]{:S(2)}) collective-permute-start(bf16[384,256]{1,0:T(8,128)(2,1)S(1)} %get-tuple-element.25.own0), channel_id=1, source_target_pairs={{0,32},{4,36},{8,40},{12,44},{16,48},{20,52},{24,56},{28,60},{32,6... | collective-permute-start | bytes 589832 | tf_op jit(solution)/shard_map/ppermute | solution.py:398
  9.2 4.3 %collective-permute-start.3 = (bf16[144,128]{1,0:T(8,128)(2,1)S(1)}, bf16[144,128]{1,0:T(8,128)(2,1)S(1)}, u32[]{:S(2)}, u32[]{:S(2)}) collective-permute-start(bf16[144,128]{1,0:T(8,128)(2,1)S(1)} %get-tuple-element.24.own), channel_id=1, source_target_pairs={{0,16},{4,20},{8,24},{12,28},{16,0},{20,4},{24,8},{28,12},{32,48},... | collective-permute-start | bytes 110600 | tf_op jit(solution)/shard_map/ppermute | solution.py:398
  15.9 12.6 %collective-permute-start.11 = (bf16[384,256]{1,0:T(8,128)(2,1)S(1)}, bf16[384,256]{1,0:T(8,128)(2,1)S(1)}, u32[]{:S(2)}, u32[]{:S(2)}) collective-permute-start(bf16[384,256]{1,0:T(8,128)(2,1)S(1)} %get-tuple-element.34), channel_id=1, source_target_pairs={{0,32},{4,36},{8,40},{12,44},{16,48},{20,52},{24,56},{28,60},{32,6... | collective-permute-start | bytes 589832 | tf_op jit(solution)/shard_map/ppermute | solution.py:398
  17.2 8.3 %collective-permute-start.7 = (bf16[144,128]{1,0:T(8,128)(2,1)S(1)}, bf16[144,128]{1,0:T(8,128)(2,1)S(1)}, u32[]{:S(2)}, u32[]{:S(2)}) collective-permute-start(bf16[144,128]{1,0:T(8,128)(2,1)S(1)} %get-tuple-element.27), channel_id=1, source_target_pairs={{0,32},{4,36},{8,40},{12,44},{16,48},{20,52},{24,56},{28,60},{32,6... | collective-permute-start | bytes 110600 | tf_op jit(solution)/shard_map/ppermute | solution.py:398
  17.5 8.1 %collective-permute-start.8 = (bf16[144,128]{1,0:T(8,128)(2,1)S(1)}, bf16[144,128]{1,0:T(8,128)(2,1)S(1)}, u32[]{:S(2)}, u32[]{:S(2)}) collective-permute-start(bf16[144,128]{1,0:T(8,128)(2,1)S(1)} %get-tuple-element.27), channel_id=1, source_target_pairs={{0,64},{4,68},{8,72},{12,76},{16,80},{20,84},{24,88},{28,92},{32,9... | collective-permute-start | bytes 110600 | tf_op jit(solution)/shard_map/ppermute | solution.py:398
  18.0 7.5 %collective-permute-start.9 = (bf16[144,128]{1,0:T(8,128)(2,1)S(1)}, bf16[144,128]{1,0:T(8,128)(2,1)S(1)}, u32[]{:S(2)}, u32[]{:S(2)}) collective-permute-start(bf16[144,128]{1,0:T(8,128)(2,1)S(1)} %get-tuple-element.27), channel_id=1, source_target_pairs={{0,96},{4,100},{8,104},{12,108},{16,112},{20,116},{24,120},{28,124... | collective-permute-start | bytes 110600 | tf_op jit(solution)/shard_map/ppermute | solution.py:398
  19.4 6.8 %collective-permute-start.10 = (bf16[144,128]{1,0:T(8,128)(2,1)S(1)}, bf16[144,128]{1,0:T(8,128)(2,1)S(1)}, u32[]{:S(2)}, u32[]{:S(2)}) collective-permute-start(bf16[144,128]{1,0:T(8,128)(2,1)S(1)} %get-tuple-element.27), channel_id=1, source_target_pairs={{0,128},{4,132},{8,136},{12,140},{16,144},{20,148},{24,152},{28,15... | collective-permute-start | bytes 110600 | tf_op jit(solution)/shard_map/ppermute | solution.py:398
  28.6 5.5 %collective-permute-start.12 = (bf16[384,256]{1,0:T(8,128)(2,1)S(1)}, bf16[384,256]{1,0:T(8,128)(2,1)S(1)}, u32[]{:S(2)}, u32[]{:S(2)}) collective-permute-start(bf16[384,256]{1,0:T(8,128)(2,1)S(1)} %collective-permute-done.11.own2), channel_id=1, source_target_pairs={{0,32},{4,36},{8,40},{12,44},{16,48},{20,52},{24,56},{28,60},{32,6... | collective-permute-start | bytes 589832 | tf_op jit(solution)/shard_map/ppermute | solution.py:398
  31.5 24.3 %collective-permute-start.14 = (bf16[384,256]{1,0:T(8,128)(2,1)S(1)}, bf16[384,256]{1,0:T(8,128)(2,1)S(1)}, u32[]{:S(2)}, u32[]{:S(2)}) collective-permute-start(bf16[384,256]{1,0:T(8,128)(2,1)S(1)} %broadcast_select_fusion.6), channel_id=1, source_target_pairs={{0,8},{4,12},{8,16},{12,20},{16,24},{20,28},{24,0},{28,4},{32,40},... | collective-permute-start | bytes 589832 | tf_op jit(solution)/shard_map/ppermute | solution.py:398
  32.3 24.6 %collective-permute-start.15 = (bf16[384,256]{1,0:T(8,128)(2,1)S(1)}, bf16[384,256]{1,0:T(8,128)(2,1)S(1)}, u32[]{:S(2)}, u32[]{:S(2)}) collective-permute-start(bf16[384,256]{1,0:T(8,128)(2,1)S(1)} %broadcast_select_fusion.6), channel_id=1, source_target_pairs={{0,16},{4,20},{8,24},{12,28},{16,0},{20,4},{24,8},{28,12},{32,48},... | collective-permute-start | bytes 589832 | tf_op jit(solution)/shard_map/ppermute | solution.py:398
  34.1 22.9 %collective-permute-start.13 = (bf16[384,256]{1,0:T(8,128)(2,1)S(1)}, bf16[384,256]{1,0:T(8,128)(2,1)S(1)}, u32[]{:S(2)}, u32[]{:S(2)}) collective-permute-start(bf16[384,256]{1,0:T(8,128)(2,1)S(1)} %collective-permute-done.12.own3), channel_id=1, source_target_pairs={{0,32},{4,36},{8,40},{12,44},{16,48},{20,52},{24,56},{28,60},{32,6... | collective-permute-start | bytes 589832 | tf_op jit(solution)/shard_map/ppermute | solution.py:398
  37.2 17.0 %all-to-all-start = ((f32[8,8,384]{2,1,0:T(8,128)}), f32[8,8,384]{2,1,0:T(8,128)S(1)}, u32[]{:S(2)}, u32[]{:S(2)}) async-start(f32[8,8,384]{2,1,0:T(8,128)} %get-tuple-element.32), calls=%async_computation | async-start | bytes 196608 | tf_op jit(solution)/shard_map/all_to_all | solution.py:406
  49.2 10.5 %collective-permute-start.16 = (bf16[384,256]{1,0:T(8,128)(2,1)S(1)}, bf16[384,256]{1,0:T(8,128)(2,1)S(1)}, u32[]{:S(2)}, u32[]{:S(2)}) collective-permute-start(bf16[384,256]{1,0:T(8,128)(2,1)S(1)} %broadcast_select_fusion.6), channel_id=1, source_target_pairs={{0,24},{4,28},{8,0},{12,4},{16,8},{20,12},{24,16},{28,20},{32,56},... | collective-permute-start | bytes 589832 | tf_op jit(solution)/shard_map/ppermute | solution.py:398
  55.4 6.2 %collective-permute-start.17 = (bf16[384,256]{1,0:T(8,128)(2,1)S(1)}, bf16[384,256]{1,0:T(8,128)(2,1)S(1)}, u32[]{:S(2)}, u32[]{:S(2)}) collective-permute-start(bf16[384,256]{1,0:T(8,128)(2,1)S(1)} %collective-permute-done.11.own2), channel_id=1, source_target_pairs={{0,8},{4,12},{8,16},{12,20},{16,24},{20,28},{24,0},{28,4},{32,40},... | collective-permute-start | bytes 589832 | tf_op jit(solution)/shard_map/ppermute | solution.py:398
  55.8 7.3 %collective-permute-start.18 = (bf16[384,256]{1,0:T(8,128)(2,1)S(1)}, bf16[384,256]{1,0:T(8,128)(2,1)S(1)}, u32[]{:S(2)}, u32[]{:S(2)}) collective-permute-start(bf16[384,256]{1,0:T(8,128)(2,1)S(1)} %collective-permute-done.11.own2), channel_id=1, source_target_pairs={{0,16},{4,20},{8,24},{12,28},{16,0},{20,4},{24,8},{28,12},{32,48},... | collective-permute-start | bytes 589832 | tf_op jit(solution)/shard_map/ppermute | solution.py:398
  57.0 12.3 %collective-permute-start.19 = (bf16[384,256]{1,0:T(8,128)(2,1)S(1)}, bf16[384,256]{1,0:T(8,128)(2,1)S(1)}, u32[]{:S(2)}, u32[]{:S(2)}) collective-permute-start(bf16[384,256]{1,0:T(8,128)(2,1)S(1)} %collective-permute-done.11.own2), channel_id=1, source_target_pairs={{0,24},{4,28},{8,0},{12,4},{16,8},{20,12},{24,16},{28,20},{32,56},... | collective-permute-start | bytes 589832 | tf_op jit(solution)/shard_map/ppermute | solution.py:398
  57.0 13.5 %collective-permute-start.20 = (bf16[384,256]{1,0:T(8,128)(2,1)S(1)}, bf16[384,256]{1,0:T(8,128)(2,1)S(1)}, u32[]{:S(2)}, u32[]{:S(2)}) collective-permute-start(bf16[384,256]{1,0:T(8,128)(2,1)S(1)} %collective-permute-done.12.own3), channel_id=1, source_target_pairs={{0,8},{4,12},{8,16},{12,20},{16,24},{20,28},{24,0},{28,4},{32,40},... | collective-permute-start | bytes 589832 | tf_op jit(solution)/shard_map/ppermute | solution.py:398
  59.7 23.1 %collective-permute-start.21 = (bf16[384,256]{1,0:T(8,128)(2,1)S(1)}, bf16[384,256]{1,0:T(8,128)(2,1)S(1)}, u32[]{:S(2)}, u32[]{:S(2)}) collective-permute-start(bf16[384,256]{1,0:T(8,128)(2,1)S(1)} %collective-permute-done.12.own3), channel_id=1, source_target_pairs={{0,16},{4,20},{8,24},{12,28},{16,0},{20,4},{24,8},{28,12},{32,48},... | collective-permute-start | bytes 589832 | tf_op jit(solution)/shard_map/ppermute | solution.py:398
  61.6 21.3 %collective-permute-start.22 = (bf16[384,256]{1,0:T(8,128)(2,1)S(1)}, bf16[384,256]{1,0:T(8,128)(2,1)S(1)}, u32[]{:S(2)}, u32[]{:S(2)}) collective-permute-start(bf16[384,256]{1,0:T(8,128)(2,1)S(1)} %collective-permute-done.12.own3), channel_id=1, source_target_pairs={{0,24},{4,28},{8,0},{12,4},{16,8},{20,12},{24,16},{28,20},{32,56},... | collective-permute-start | bytes 589832 | tf_op jit(solution)/shard_map/ppermute | solution.py:398
  63.1 19.8 %collective-permute-start.23 = (bf16[384,256]{1,0:T(8,128)(2,1)S(1)}, bf16[384,256]{1,0:T(8,128)(2,1)S(1)}, u32[]{:S(2)}, u32[]{:S(2)}) collective-permute-start(bf16[384,256]{1,0:T(8,128)(2,1)S(1)} %get-tuple-element.45), channel_id=1, source_target_pairs={{0,8},{4,12},{8,16},{12,20},{16,24},{20,28},{24,0},{28,4},{32,40},... | collective-permute-start | bytes 589832 | tf_op jit(solution)/shard_map/ppermute | solution.py:398
  69.3 13.5 %collective-permute-start.24 = (bf16[384,256]{1,0:T(8,128)(2,1)S(1)}, bf16[384,256]{1,0:T(8,128)(2,1)S(1)}, u32[]{:S(2)}, u32[]{:S(2)}) collective-permute-start(bf16[384,256]{1,0:T(8,128)(2,1)S(1)} %get-tuple-element.44), channel_id=1, source_target_pairs={{0,16},{4,20},{8,24},{12,28},{16,0},{20,4},{24,8},{28,12},{32,48},... | collective-permute-start | bytes 589832 | tf_op jit(solution)/shard_map/ppermute | solution.py:398
  70.5 14.6 %collective-permute-start.25 = (bf16[384,256]{1,0:T(8,128)(2,1)S(1)}, bf16[384,256]{1,0:T(8,128)(2,1)S(1)}, u32[]{:S(2)}, u32[]{:S(2)}) collective-permute-start(bf16[384,256]{1,0:T(8,128)(2,1)S(1)} %get-tuple-element.43), channel_id=1, source_target_pairs={{0,24},{4,28},{8,0},{12,4},{16,8},{20,12},{24,16},{28,20},{32,56},... | collective-permute-start | bytes 589832 | tf_op jit(solution)/shard_map/ppermute | solution.py:398
  95.0 10.0 %collective-permute-start.26 = (bf16[192,512]{1,0:T(8,128)(2,1)S(1)}, bf16[192,512]{1,0:T(8,128)(2,1)S(1)}, u32[]{:S(2)}, u32[]{:S(2)}) collective-permute-start(bf16[192,512]{1,0:T(8,128)(2,1)S(1)} %get-tuple-element.40), channel_id=1, source_target_pairs={{0,4},{4,0},{8,12},{12,8},{16,20},{20,16},{24,28},{28,24},{32,36},... | collective-permute-start | bytes 589832 | tf_op jit(solution)/shard_map/ppermute | solution.py:398
  (7 other events, 18.0 us)

commit v2 on v1

--- a/solution.py
+++ b/solution.py
@@ -181,8 +181,12 @@
 
 
 def first_kernel(
-    info, prefix, from1, from2, from3, from4, inside, query, first_ref, sums_ref, count_ref
+    info, prefix, from1, from2, from3, from4, inside, query, own1, own2,
+    first_ref, sums_ref, count_ref, pair12_ref, later2_ref
 ):
+    pair12_ref[:PAIR] = own1[...]
+    pair12_ref[PAIR:] = own2[...]
+    later2_ref[...] = own2[...]
     z = place()[0]
     first = info[3].astype(F32)
     state = prefix[:HEAD_DIM]
@@ -218,6 +222,20 @@
     return lax.transpose(lax.rsqrt(total * (1.0 / WIDTH) + EPSILON), (1, 0))[:, :1]
 
 
+def payload_kernel(own0, own3, own4, *refs):
+    x = place()[1]
+    for shift, payload in enumerate(refs[4:], 1):
+        payload[:PAIR] = own3[...]
+
+        @pl.when(x + shift < X)
+        def _():
+            payload[PAIR:] = own0[...]
+
+        @pl.when(x + shift >= X)
+        def _():
+            payload[PAIR:] = own4[...]
+
+
 TILE = 128
 TILES = [(head, slice(at, at + TILE)) for head in range(REPEAT) for at in range(0, PAIR, TILE)]
 
@@ -305,14 +323,14 @@
 def near_kernel(
     reach, sums, first, keep, queries_r, own1, own2, own3, own4, *refs
 ):
-    others1, others2 = refs[:3], refs[3:6]
-    queries, tops, acc, kv, scales, bounds, sems = refs[6:]
+    others = refs[:3]
+    queries, tops, acc, kv, scales, bounds, sems = refs[3:]
     _, x, core = place()
     blocks = [(own1, 4), (own2, 8), (own3, 12), (own4, 16)]
-    for shift, other1, other2 in zip((1, 2, 3), others1, others2):
+    for shift, other in enumerate(others, 1):
         wrapped = jnp.where(x < shift, 4, 0)
-        blocks.append((other1, 4 + shift - wrapped))
-        blocks.append((other2, 8 + shift - wrapped))
+        blocks.append((other.at[pl.ds(0, PAIR)], 4 + shift - wrapped))
+        blocks.append((other.at[pl.ds(PAIR, PAIR)], 8 + shift - wrapped))
     window = Window(reach[0], blocks, kv, bounds, sems)
     tops[...] = jnp.full(tops.shape, NEGATIVE, F32)
     acc[...] = jnp.zeros(acc.shape, F32)
@@ -326,13 +344,14 @@
 
 
 def far_kernel(info, reach, queries, old_tops, old_acc, own0, *refs):
-    others3, others04 = refs[:3], refs[3:6]
-    mine_ref, send_ref, sums_ref, tops, acc, kv, own, bounds, sems = refs[6:]
+    others = refs[:3]
+    mine_ref, send_ref, sums_ref, tops, acc, kv, own, bounds, sems = refs[3:]
     _, x, core = place()
     blocks = []
-    for shift, other3, other04 in zip((1, 2, 3), others3, others04):
-        blocks.append((other3, 12 + shift - jnp.where(x < shift, 4, 0)))
-        blocks.append((other04, jnp.where(x < shift, 12 + shift, shift)))
+    for shift, other in enumerate(others, 1):
+        wrapped = x < shift
+        blocks.append((other.at[pl.ds(0, PAIR)], 12 + shift - jnp.where(wrapped, 4, 0)))
+        blocks.append((other.at[pl.ds(PAIR, PAIR)], shift + jnp.where(wrapped, 12, 0)))
     window = Window(reach[0], blocks, kv, bounds, sems)
     own[:, : 2 * HEAD_DIM] = own0[...]
     own[:, 2 * HEAD_DIM :] = jnp.ones((PAIR, HEAD_DIM), BF16)
@@ -450,12 +469,7 @@
     )(info, state, *near, own1, queries_r)
     far = [move(plane, z_shift=back) for back in (1, 2, 3, 4)]
 
-    def after(known, value):
-        return jnp.where(known >= 0, value, jnp.zeros_like(value))
-
     own2 = move(later1, z_shift=1)
-    own3 = move(own2, z_shift=1)
-    own4 = move(own3, z_shift=1)
 
     inside, query = call(
         inside_kernel,
@@ -464,27 +478,34 @@
         (VMEM,) * 2,
         name="inside",
     )(info, keep, queries_r, packed)
-    first, sums, reach = call(
+    first, sums, reach, pair12, later2 = call(
         first_kernel,
         (
             shape((PAIR, COLS), F32),
             shape((CORES * TP, 8, PAIR), F32),
             shape((1,), jnp.int32),
-        ),
-        [SMEM] + [VMEM] * 7,
-        (VMEM, VMEM, SMEM),
+            shape((2 * PAIR, 2 * HEAD_DIM), BF16),
+            shape((PAIR, 2 * HEAD_DIM), BF16),
+        ),
+        [SMEM] + [VMEM] * 9,
+        (VMEM, VMEM, SMEM, VMEM, VMEM),
         name="first",
-    )(info, prefix, *far, inside, query)
+    )(info, prefix, *far, inside, query, own1, own2)
+    own3 = move(later2, z_shift=1)
+    own4 = move(own3, z_shift=1)
 
 
     all_sums = exchange(sums)
-    x = lax.axis_index("x")
     x_shifts = (1, 2, 3)
-    others = [move(after(reach[0], own1), x_shift=shift) for shift in x_shifts]
-    others += [move(own2, x_shift=shift) for shift in x_shifts]
-    others += [move(own3, x_shift=shift) for shift in x_shifts]
-    late4 = after(all_sums[0, 0, 0], own4)
-    others += [move(jnp.where(x + shift < X, own0, late4), x_shift=shift) for shift in x_shifts]
+    others12 = [move(pair12, x_shift=shift) for shift in x_shifts]
+    payloads34 = call(
+        payload_kernel,
+        (shape((2 * PAIR, 2 * HEAD_DIM), BF16),) * 3,
+        [VMEM] * 7,
+        (VMEM,) * 3,
+        name="payload",
+    )(own0, own3, own4, *others12, all_sums)
+    others34 = [move(value, x_shift=shift) for shift, value in zip(x_shifts, payloads34)]
     queries, tops, acc = call(
         near_kernel,
         (
@@ -492,7 +513,7 @@
             shape((REPEAT, PAIR, HEAD_DIM), F32),
             shape((REPEAT, PAIR, 2 * HEAD_DIM), F32),
         ),
-        [SMEM] + [VMEM] * 14,
+        [SMEM] + [VMEM] * 11,
         (VMEM,) * 3,
         scratch=(
             pltpu.VMEM((SLOTS * PAIR, 3 * HEAD_DIM), BF16),
@@ -502,7 +523,7 @@
         ),
         name="near",
     )(
-        reach, all_sums, first, keep, queries_r, own1, own2, own3, own4, *others[:6]
+        reach, all_sums, first, keep, queries_r, own1, own2, own3, own4, *others12
     )
     mine, send, out_sums, _, _ = call(
         far_kernel,
@@ -513,7 +534,7 @@
             shape((REPEAT, PAIR, HEAD_DIM), F32),
             shape((REPEAT, PAIR, 2 * HEAD_DIM), F32),
         ),
-        [SMEM, SMEM] + [VMEM] * 10,
+        [SMEM, SMEM] + [VMEM] * 7,
         (VMEM,) * 5,
         scratch=(
             pltpu.VMEM((SLOTS * PAIR, 3 * HEAD_DIM), BF16),
@@ -523,7 +544,7 @@
         ),
         aliases={3: 3, 4: 4},
         name="far",
-    )(info, reach, queries, tops, acc, own0, *others[6:])
+    )(info, reach, queries, tops, acc, own0, *others34)
     theirs = swap(send)
     return call(
         last_kernel, shape((TOK, 2 * COLS), BF16), [VMEM] * 3, VMEM, name="last"

time: 106 us -> 96.8 us (0.913); the launches traced: 106 us -> 95 us
  starting transfers between devices: 48.5 us -> 29.5 us
  blocking collectives: 7.35 us -> 22.4 us
  Pallas kernels: 28.8 us -> 18.2 us
  waiting for transfers between devices: 17.3 us -> 22.7 us
  between operations: 1.47 us -> 0.13 us
    all_to_all x1 -> x2, blocking collectives: 7.35 us -> 22.4 us  [exchange(): return lax.all_to_all(sums, ('core', 'tp'), 0, 0, tiled=True)]
    all_to_all x1 -> x0, starting transfers between devices: 12 us -> none  [exchange(): return lax.all_to_all(sums, ('core', 'tp'), 0, 0, tiled=True)]
    ppermute x27 -> x21, waiting for transfers between devices: 12.3 us -> 22.7 us  [move(): return lax.ppermute(value, CTX, pairs)]
    pallas_call x1, Pallas kernels: 12.3 us -> 3.59 us  [shards(): call(near_kernel, (shape((REPEAT, PAIR, HEAD_DIM), BF16), shape((REPEAT,...]
    ppermute x27 -> x21, starting transfers between devices: 36.5 us -> 29.5 us  [move(): return lax.ppermute(value, CTX, pairs)]
    all_to_all x1 -> x0, waiting for transfers between devices: 5.01 us -> none  [exchange(): return lax.all_to_all(sums, ('core', 'tp'), 0, 0, tiled=True)]
    pallas_call x1, Pallas kernels: 9.82 us -> 7.98 us  [shards(): call(far_kernel, (shape((TOK, COLS), BF16), shape((TOK, COLS), BF16), sha...]
  transfers between devices with their start and end apart: 28 -> 21, of which waited for: 11 -> 9; matrix products, arithmetic and copies ran while one was open for 1% -> 0% of each run, Pallas kernels for 16% -> 7%
where the time goes in v2:
time: 96.8 us; the launch traced here: 95 us
  starting transfers between devices  29.5 us (30%)
  waiting for transfers between devices  22.7 us (23%)
  blocking collectives  22.4 us (23%)
  Pallas kernels  18.2 us (19%)
  local copies, waits for them, and re-layouts  1.92 us (2%)
    ppermute x21, starting transfers between devices, move(): return lax.ppermute(value, CTX, pairs)  29.5 us
    ppermute x21, waiting for transfers between devices, move(): return lax.ppermute(value, CTX, pairs)  22.7 us
    all_to_all x2, blocking collectives, exchange(): return lax.all_to_all(sums, ('core', 'tp'), 0, 0, tiled=True)  22.4 us
    pallas_call x1, Pallas kernels, shards(): call(far_kernel, (shape((TOK, COLS), BF16), shape((TOK, COLS), BF16), sha...  7.98 us
    pallas_call x1, Pallas kernels, shards(): call(near_kernel, (shape((REPEAT, PAIR, HEAD_DIM), BF16), shape((REPEAT,...  3.59 us
  transfers between devices with their start and end apart: 21, of which 9 were waited for; matrix products, arithmetic and copies ran while one was open for 0% of the time, Pallas kernels for 7%

profile of v2, /device:TPU:103, one launch (start us, length us, event | category | flops | bytes accessed | tf_op | source)
XLA Modules:
  0.0 95.0 jit_solution(13337290776219960770)
XLA Ops:
  3.5 1.2 %collective-permute-done.seg_r = s32[192]{0:T(256)S(1)} collective-permute-done((s32[192]{0:T(256)S(1)}, s32[192]{0:T(256)S(1)}, u32[]{:S(2)}, u32[]{:S(2)}) %collective-permute-start) | collective-permute-done | bytes 800 | tf_op jit(solution)/shard_map/ppermute | solution.py:417
  4.7 1.4 %prep.1 = (bf16[384,256]{1,0:T(8,128)(2,1)S(1)}, bf16[384,256]{1,0:T(8,128)(2,1)S(1)}, bf16[144,128]{1,0:T(8,128)(2,1)S(1)}, s32[8]{0:T(128)S(1)}) custom-call(s32[192]{0:T(256)S(1)} %copy-done, s32[192]{0:T(256)S(1)} %collective-permute-done.seg_r, bf16[4,192,128]{2,1,0:T(8,128)(2,1)S(1)} %get-tuple-element.58.own, ...), custom_call_target="tpu_custom_call" | custom-call | tf_op jit(solution)/shard_map/prep/pallas_call | solution.py:442
  6.0 2.9 %collective-permute-start.5 = (bf16[384,256]{1,0:T(8,128)(2,1)S(1)}, bf16[384,256]{1,0:T(8,128)(2,1)S(1)}, u32[]{:S(2)}, u32[]{:S(2)}) collective-permute-start(bf16[384,256]{1,0:T(8,128)(2,1)S(1)} %get-tuple-element.30.own0), channel_id=1, source_target_pairs={{0,32},{4,36},{8,40},{12,44},{16,48},{20,52},{24,56},{28,60},{32,6... | collective-permute-start | bytes 589832 | tf_op jit(solution)/shard_map/ppermute | solution.py:417
  10.4 1.8 %collective-permute-start.2 = (bf16[144,128]{1,0:T(8,128)(2,1)S(1)}, bf16[144,128]{1,0:T(8,128)(2,1)S(1)}, u32[]{:S(2)}, u32[]{:S(2)}) collective-permute-start(bf16[144,128]{1,0:T(8,128)(2,1)S(1)} %get-tuple-element.29.own), channel_id=1, source_target_pairs={{0,8},{4,12},{8,16},{12,20},{16,24},{20,28},{24,0},{28,4},{32,40},... | collective-permute-start | bytes 110600 | tf_op jit(solution)/shard_map/ppermute | solution.py:417
  14.9 2.4 %collective-permute-start.11 = (bf16[384,256]{1,0:T(8,128)(2,1)S(1)}, bf16[384,256]{1,0:T(8,128)(2,1)S(1)}, u32[]{:S(2)}, u32[]{:S(2)}) collective-permute-start(bf16[384,256]{1,0:T(8,128)(2,1)S(1)} %get-tuple-element.36), channel_id=1, source_target_pairs={{0,32},{4,36},{8,40},{12,44},{16,48},{20,52},{24,56},{28,60},{32,6... | collective-permute-start | bytes 589832 | tf_op jit(solution)/shard_map/ppermute | solution.py:417
  17.2 1.6 %collective-permute-start.10 = (bf16[144,128]{1,0:T(8,128)(2,1)S(1)}, bf16[144,128]{1,0:T(8,128)(2,1)S(1)}, u32[]{:S(2)}, u32[]{:S(2)}) collective-permute-start(bf16[144,128]{1,0:T(8,128)(2,1)S(1)} %get-tuple-element.32), channel_id=1, source_target_pairs={{0,128},{4,132},{8,136},{12,140},{16,144},{20,148},{24,152},{28,15... | collective-permute-start | bytes 110600 | tf_op jit(solution)/shard_map/ppermute | solution.py:417
  18.9 1.8 %collective-permute-start.9 = (bf16[144,128]{1,0:T(8,128)(2,1)S(1)}, bf16[144,128]{1,0:T(8,128)(2,1)S(1)}, u32[]{:S(2)}, u32[]{:S(2)}) collective-permute-start(bf16[144,128]{1,0:T(8,128)(2,1)S(1)} %get-tuple-element.32), channel_id=1, source_target_pairs={{0,96},{4,100},{8,104},{12,108},{16,112},{20,116},{24,120},{28,124... | collective-permute-start | bytes 110600 | tf_op jit(solution)/shard_map/ppermute | solution.py:417
  20.6 2.1 %collective-permute-start.8 = (bf16[144,128]{1,0:T(8,128)(2,1)S(1)}, bf16[144,128]{1,0:T(8,128)(2,1)S(1)}, u32[]{:S(2)}, u32[]{:S(2)}) collective-permute-start(bf16[144,128]{1,0:T(8,128)(2,1)S(1)} %get-tuple-element.32), channel_id=1, source_target_pairs={{0,64},{4,68},{8,72},{12,76},{16,80},{20,84},{24,88},{28,92},{32,9... | collective-permute-start | bytes 110600 | tf_op jit(solution)/shard_map/ppermute | solution.py:417
  22.9 1.9 %inside.1 = (f32[384,512]{1,0:T(8,128)S(1)}, bf16[384,512]{1,0:T(8,128)(2,1)S(1)}) custom-call(s32[8]{0:T(128)S(1)} %get-tuple-element.28.info, bf16[2,192,512]{2,1,0:T(8,128)(2,1)S(1)} %get-tuple-element.51.keep, bf16[2,192,512]{2,1,0:T(8,128)(2,1)S(1)} %collective-permute-done.6.queries_r, bf16[384,256]{1,0:T(8,128)(2,1)S(1)} %get-tuple-element.33.packed), custom_call_target="tpu_custom_call" | custom-call | tf_op jit(solution)/shard_map/inside/pallas_call | solution.py:474
  24.9 1.0 %collective-permute-done.8.from2 = bf16[144,128]{1,0:T(8,128)(2,1)S(1)} collective-permute-done((bf16[144,128]{1,0:T(8,128)(2,1)S(1)}, bf16[144,128]{1,0:T(8,128)(2,1)S(1)}, u32[]{:S(2)}, u32[]{:S(2)}) %collective-permute-start.8) | collective-permute-done | bytes 36896 | tf_op jit(solution)/shard_map/ppermute | solution.py:417
  26.8 1.6 %first.1 = (f32[384,512]{1,0:T(8,128)S(1)}, f32[8,8,384]{2,1,0:T(8,128)S(1)}, s32[1]{0:T(128)}, bf16[768,256]{1,0:T(8,128)(2,1)S(1)}, bf16[384,256]{1,0:T(8,128)(2,1)S(1)}) custom-call(s32[8]{0:T(128)S(1)} %get-tuple-element.28.info, f32[136,128]{1,0:T(8,128)S(1)} %get-tuple-element.31.prefix, bf16[144,128]{1,0:T(8,128)(2,1)S(1)} %collective-permute-done.7.from1, ...), custom_call_target="tpu_custom_call" | custom-call | tf_op jit(solution)/shard_map/first/pallas_call | solution.py:481
  28.4 3.2 %collective-permute-start.12 = (bf16[384,256]{1,0:T(8,128)(2,1)S(1)}, bf16[384,256]{1,0:T(8,128)(2,1)S(1)}, u32[]{:S(2)}, u32[]{:S(2)}) collective-permute-start(bf16[384,256]{1,0:T(8,128)(2,1)S(1)} %get-tuple-element.40), channel_id=1, source_target_pairs={{0,32},{4,36},{8,40},{12,44},{16,48},{20,52},{24,56},{28,60},{32,6... | collective-permute-start | bytes 589832 | tf_op jit(solution)/shard_map/ppermute | solution.py:417
  32.3 1.1 %collective-permute-start.15 = (bf16[768,256]{1,0:T(8,128)(2,1)S(1)}, bf16[768,256]{1,0:T(8,128)(2,1)S(1)}, u32[]{:S(2)}, u32[]{:S(2)}) collective-permute-start(bf16[768,256]{1,0:T(8,128)(2,1)S(1)} %get-tuple-element.41), channel_id=1, source_target_pairs={{0,16},{4,20},{8,24},{12,28},{16,0},{20,4},{24,8},{28,12},{32,48},... | collective-permute-start | bytes 1179656 | tf_op jit(solution)/shard_map/ppermute | solution.py:417
  33.3 1.5 %collective-permute-start.14 = (bf16[768,256]{1,0:T(8,128)(2,1)S(1)}, bf16[768,256]{1,0:T(8,128)(2,1)S(1)}, u32[]{:S(2)}, u32[]{:S(2)}) collective-permute-start(bf16[768,256]{1,0:T(8,128)(2,1)S(1)} %get-tuple-element.41), channel_id=1, source_target_pairs={{0,8},{4,12},{8,16},{12,20},{16,24},{20,28},{24,0},{28,4},{32,40},... | collective-permute-start | bytes 1179656 | tf_op jit(solution)/shard_map/ppermute | solution.py:417
  34.8 2.5 %collective-permute-start.13 = (bf16[384,256]{1,0:T(8,128)(2,1)S(1)}, bf16[384,256]{1,0:T(8,128)(2,1)S(1)}, u32[]{:S(2)}, u32[]{:S(2)}) collective-permute-start(bf16[384,256]{1,0:T(8,128)(2,1)S(1)} %collective-permute-done.12.own3), channel_id=1, source_target_pairs={{0,32},{4,36},{8,40},{12,44},{16,48},{20,52},{24,56},{28,60},{32,6... | collective-permute-start | bytes 589832 | tf_op jit(solution)/shard_map/ppermute | solution.py:417
  37.3 13.0 %all_to_all.10.sums.refs_3_ = f32[8,8,384]{2,1,0:T(8,128)S(1)} all-to-all(f32[8,8,384]{2,1,0:T(8,128)S(1)} %get-tuple-element.38), channel_id=1, replica_groups=mesh['z'=8,'x'=4,'core'=2,'tp'=4] {'core','tp'}, dimensions={0} | all-to-all | bytes 196608 | tf_op jit(solution)/shard_map/all_to_all | solution.py:425
  50.4 1.5 %collective-permute-done.14.refs_0_ = bf16[768,256]{1,0:T(8,128)(2,1)S(1)} collective-permute-done((bf16[768,256]{1,0:T(8,128)(2,1)S(1)}, bf16[768,256]{1,0:T(8,128)(2,1)S(1)}, u32[]{:S(2)}, u32[]{:S(2)}) %collective-permute-start.14) | collective-permute-done | bytes 393248 | tf_op jit(solution)/shard_map/ppermute | solution.py:417
  51.9 3.5 %collective-permute-start.17 = (bf16[768,256]{1,0:T(8,128)(2,1)S(1)}, bf16[768,256]{1,0:T(8,128)(2,1)S(1)}, u32[]{:S(2)}, u32[]{:S(2)}) collective-permute-start(bf16[768,256]{1,0:T(8,128)(2,1)S(1)} %get-tuple-element.45), channel_id=1, source_target_pairs={{0,8},{4,12},{8,16},{12,20},{16,24},{20,28},{24,0},{28,4},{32,40},... | collective-permute-start | bytes 1179656 | tf_op jit(solution)/shard_map/ppermute | solution.py:417
  56.1 3.6 %near.1 = (bf16[4,384,128]{2,1,0:T(8,128)(2,1)S(1)}, f32[4,384,128]{2,1,0:T(8,128)S(1)}, f32[4,384,256]{2,1,0:T(8,128)S(1)}) custom-call(s32[1]{0:T(128)} %get-tuple-element.37.reach, f32[8,8,384]{2,1,0:T(8,128)S(1)} %all_to_all.10.sums.refs_3_, f32[384,512]{1,0:T(8,128)S(1)} %get-tuple-element.39.first, bf16[2,192,512]{2,1,0:T(8,128)(2,1)S(1)} %get-tuple-element.51.keep, ...), custom_call_target="tpu_custom_call" | custom-call | tf_op jit(solution)/shard_map/near/pallas_call | solution.py:509
  59.7 12.0 %collective-permute-done.17.refs_0_ = bf16[768,256]{1,0:T(8,128)(2,1)S(1)} collective-permute-done((bf16[768,256]{1,0:T(8,128)(2,1)S(1)}, bf16[768,256]{1,0:T(8,128)(2,1)S(1)}, u32[]{:S(2)}, u32[]{:S(2)}) %collective-permute-start.17) | collective-permute-done | bytes 393248 | tf_op jit(solution)/shard_map/ppermute | solution.py:417
  71.7 4.0 %collective-permute-done.19.refs_2_ = bf16[768,256]{1,0:T(8,128)(2,1)S(1)} collective-permute-done((bf16[768,256]{1,0:T(8,128)(2,1)S(1)}, bf16[768,256]{1,0:T(8,128)(2,1)S(1)}, u32[]{:S(2)}, u32[]{:S(2)}) %collective-permute-start.19) | collective-permute-done | bytes 393248 | tf_op jit(solution)/shard_map/ppermute | solution.py:417
  75.7 8.0 %far.1 = (bf16[192,512]{1,0:T(8,128)(2,1)S(1)}, bf16[192,512]{1,0:T(8,128)(2,1)S(1)}, f32[8,8,192]{2,1,0:T(8,128)S(1)}, f32[4,384,128]{2,1,0:T(8,128)S(1)}, f32[4,384,256]{2,1,0:T(8,128)S(1)}) custom-call(s32[8]{0:T(128)S(1)} %get-tuple-element.28.info, s32[1]{0:T(128)} %get-tuple-element.37.reach, ...), custom_call_target="tpu_custom_call", output_to_operand_aliasing={{3}: (3, {}), {4}: (4, {})} | custom-call | tf_op jit(solution)/shard_map/far/pallas_call | solution.py:528
  84.6 9.3 %all_to_all.11.sums = f32[8,8,192]{2,1,0:T(8,128)S(1)} all-to-all(f32[8,8,192]{2,1,0:T(8,128)S(1)} %get-tuple-element.48), channel_id=1, replica_groups=mesh['z'=8,'x'=4,'core'=2,'tp'=4] {'core','tp'}, dimensions={0} | all-to-all | bytes 98304 | tf_op jit(solution)/shard_map/all_to_all | solution.py:425
  94.0 1.0 %last.1 = bf16[192,1024]{1,0:T(8,128)(2,1)} custom-call(f32[8,8,192]{2,1,0:T(8,128)S(1)} %all_to_all.11.sums, bf16[192,512]{1,0:T(8,128)(2,1)S(1)} %get-tuple-element.49.mine, bf16[192,512]{1,0:T(8,128)(2,1)S(1)} %collective-permute-done.20.theirs), custom_call_target="tpu_custom_call" | custom-call | tf_op jit(solution)/shard_map/last/pallas_call | solution.py:549
  (39 shorter events, 11.0 us)
Async XLA Ops:
  0.0 2.7 %copy-start.1 = (bf16[192,1024]{1,0:T(8,128)(2,1)S(1)}, bf16[192,1024]{1,0:T(8,128)(2,1)}, u32[]{:S(2)}) copy-start(bf16[192,1024]{1,0:T(8,128)(2,1)} %param.11) | copy-start | bytes 1179652
  0.0 2.7 %copy-start.2 = (bf16[192,1024]{1,0:T(8,128)(2,1)S(1)}, bf16[192,1024]{1,0:T(8,128)(2,1)}, u32[]{:S(2)}) copy-start(bf16[192,1024]{1,0:T(8,128)(2,1)} %param.7) | copy-start | bytes 1179652
  1.9 1.1 %copy-start = (s32[192]{0:T(256)S(1)}, s32[192]{0:T(256)}, u32[]{:S(2)}) copy-start(s32[192]{0:T(256)} %seg.1) | copy-start | bytes 2308
  1.9 2.7 %collective-permute-start.1 = (bf16[4,192,128]{2,1,0:T(8,128)(2,1)S(1)}, bf16[4,192,128]{2,1,0:T(8,128)(2,1)S(1)}, u32[]{:S(2)}, u32[]{:S(2)}) collective-permute-start(bf16[4,192,128]{2,1,0:T(8,128)(2,1)S(1)} %get-tuple-element.57), channel_id=1, source_target_pairs={{0,4},{4,0},{8,12},{12,8},{16,20},{20,16},{24,28},{28,24},{32,36},... | collective-permute-start | bytes 589832 | tf_op jit(solution)/shard_map/ppermute | solution.py:417
  2.9 11.4 %collective-permute-start.6 = (bf16[2,192,512]{2,1,0:T(8,128)(2,1)S(1)}, bf16[2,192,512]{2,1,0:T(8,128)(2,1)S(1)}, u32[]{:S(2)}, u32[]{:S(2)}) collective-permute-start(bf16[2,192,512]{2,1,0:T(8,128)(2,1)S(1)} %get-tuple-element.52), channel_id=1, source_target_pairs={{0,4},{4,0},{8,12},{12,8},{16,20},{20,16},{24,28},{28,24},{32,36},... | collective-permute-start | bytes 1179656 | tf_op jit(solution)/shard_map/ppermute | solution.py:417
  3.0 1.7 %collective-permute-start = (s32[192]{0:T(256)S(1)}, s32[192]{0:T(256)S(1)}, u32[]{:S(2)}, u32[]{:S(2)}) collective-permute-start(s32[192]{0:T(256)S(1)} %copy-done), channel_id=1, source_target_pairs={{0,4},{4,0},{8,12},{12,8},{16,20},{20,16},{24,28},{28,24},{32,36},... | collective-permute-start | bytes 2312 | tf_op jit(solution)/shard_map/ppermute | solution.py:417
  6.0 8.2 %collective-permute-start.5 = (bf16[384,256]{1,0:T(8,128)(2,1)S(1)}, bf16[384,256]{1,0:T(8,128)(2,1)S(1)}, u32[]{:S(2)}, u32[]{:S(2)}) collective-permute-start(bf16[384,256]{1,0:T(8,128)(2,1)S(1)} %get-tuple-element.30.own0), channel_id=1, source_target_pairs={{0,32},{4,36},{8,40},{12,44},{16,48},{20,52},{24,56},{28,60},{32,6... | collective-permute-start | bytes 589832 | tf_op jit(solution)/shard_map/ppermute | solution.py:417
  9.0 4.0 %collective-permute-start.4 = (bf16[144,128]{1,0:T(8,128)(2,1)S(1)}, bf16[144,128]{1,0:T(8,128)(2,1)S(1)}, u32[]{:S(2)}, u32[]{:S(2)}) collective-permute-start(bf16[144,128]{1,0:T(8,128)(2,1)S(1)} %get-tuple-element.29.own), channel_id=1, source_target_pairs={{0,24},{4,28},{8,0},{12,4},{16,8},{20,12},{24,16},{28,20},{32,56},... | collective-permute-start | bytes 110600 | tf_op jit(solution)/shard_map/ppermute | solution.py:417
  9.5 4.3 %collective-permute-start.3 = (bf16[144,128]{1,0:T(8,128)(2,1)S(1)}, bf16[144,128]{1,0:T(8,128)(2,1)S(1)}, u32[]{:S(2)}, u32[]{:S(2)}) collective-permute-start(bf16[144,128]{1,0:T(8,128)(2,1)S(1)} %get-tuple-element.29.own), channel_id=1, source_target_pairs={{0,16},{4,20},{8,24},{12,28},{16,0},{20,4},{24,8},{28,12},{32,48},... | collective-permute-start | bytes 110600 | tf_op jit(solution)/shard_map/ppermute | solution.py:417
  10.4 3.9 %collective-permute-start.2 = (bf16[144,128]{1,0:T(8,128)(2,1)S(1)}, bf16[144,128]{1,0:T(8,128)(2,1)S(1)}, u32[]{:S(2)}, u32[]{:S(2)}) collective-permute-start(bf16[144,128]{1,0:T(8,128)(2,1)S(1)} %get-tuple-element.29.own), channel_id=1, source_target_pairs={{0,8},{4,12},{8,16},{12,20},{16,24},{20,28},{24,0},{28,4},{32,40},... | collective-permute-start | bytes 110600 | tf_op jit(solution)/shard_map/ppermute | solution.py:417
  14.9 11.9 %collective-permute-start.11 = (bf16[384,256]{1,0:T(8,128)(2,1)S(1)}, bf16[384,256]{1,0:T(8,128)(2,1)S(1)}, u32[]{:S(2)}, u32[]{:S(2)}) collective-permute-start(bf16[384,256]{1,0:T(8,128)(2,1)S(1)} %get-tuple-element.36), channel_id=1, source_target_pairs={{0,32},{4,36},{8,40},{12,44},{16,48},{20,52},{24,56},{28,60},{32,6... | collective-permute-start | bytes 589832 | tf_op jit(solution)/shard_map/ppermute | solution.py:417
  17.2 7.6 %collective-permute-start.10 = (bf16[144,128]{1,0:T(8,128)(2,1)S(1)}, bf16[144,128]{1,0:T(8,128)(2,1)S(1)}, u32[]{:S(2)}, u32[]{:S(2)}) collective-permute-start(bf16[144,128]{1,0:T(8,128)(2,1)S(1)} %get-tuple-element.32), channel_id=1, source_target_pairs={{0,128},{4,132},{8,136},{12,140},{16,144},{20,148},{24,152},{28,15... | collective-permute-start | bytes 110600 | tf_op jit(solution)/shard_map/ppermute | solution.py:417
  18.9 6.0 %collective-permute-start.9 = (bf16[144,128]{1,0:T(8,128)(2,1)S(1)}, bf16[144,128]{1,0:T(8,128)(2,1)S(1)}, u32[]{:S(2)}, u32[]{:S(2)}) collective-permute-start(bf16[144,128]{1,0:T(8,128)(2,1)S(1)} %get-tuple-element.32), channel_id=1, source_target_pairs={{0,96},{4,100},{8,104},{12,108},{16,112},{20,116},{24,120},{28,124... | collective-permute-start | bytes 110600 | tf_op jit(solution)/shard_map/ppermute | solution.py:417
  20.6 5.3 %collective-permute-start.8 = (bf16[144,128]{1,0:T(8,128)(2,1)S(1)}, bf16[144,128]{1,0:T(8,128)(2,1)S(1)}, u32[]{:S(2)}, u32[]{:S(2)}) collective-permute-start(bf16[144,128]{1,0:T(8,128)(2,1)S(1)} %get-tuple-element.32), channel_id=1, source_target_pairs={{0,64},{4,68},{8,72},{12,76},{16,80},{20,84},{24,88},{28,92},{32,9... | collective-permute-start | bytes 110600 | tf_op jit(solution)/shard_map/ppermute | solution.py:417
  22.7 4.1 %collective-permute-start.7 = (bf16[144,128]{1,0:T(8,128)(2,1)S(1)}, bf16[144,128]{1,0:T(8,128)(2,1)S(1)}, u32[]{:S(2)}, u32[]{:S(2)}) collective-permute-start(bf16[144,128]{1,0:T(8,128)(2,1)S(1)} %get-tuple-element.32), channel_id=1, source_target_pairs={{0,32},{4,36},{8,40},{12,44},{16,48},{20,52},{24,56},{28,60},{32,6... | collective-permute-start | bytes 110600 | tf_op jit(solution)/shard_map/ppermute | solution.py:417
  28.4 6.4 %collective-permute-start.12 = (bf16[384,256]{1,0:T(8,128)(2,1)S(1)}, bf16[384,256]{1,0:T(8,128)(2,1)S(1)}, u32[]{:S(2)}, u32[]{:S(2)}) collective-permute-start(bf16[384,256]{1,0:T(8,128)(2,1)S(1)} %get-tuple-element.40), channel_id=1, source_target_pairs={{0,32},{4,36},{8,40},{12,44},{16,48},{20,52},{24,56},{28,60},{32,6... | collective-permute-start | bytes 589832 | tf_op jit(solution)/shard_map/ppermute | solution.py:417
  31.6 18.8 %collective-permute-start.16 = (bf16[768,256]{1,0:T(8,128)(2,1)S(1)}, bf16[768,256]{1,0:T(8,128)(2,1)S(1)}, u32[]{:S(2)}, u32[]{:S(2)}) collective-permute-start(bf16[768,256]{1,0:T(8,128)(2,1)S(1)} %get-tuple-element.41), channel_id=1, source_target_pairs={{0,24},{4,28},{8,0},{12,4},{16,8},{20,12},{24,16},{28,20},{32,56},... | collective-permute-start | bytes 1179656 | tf_op jit(solution)/shard_map/ppermute | solution.py:417
  32.3 18.1 %collective-permute-start.15 = (bf16[768,256]{1,0:T(8,128)(2,1)S(1)}, bf16[768,256]{1,0:T(8,128)(2,1)S(1)}, u32[]{:S(2)}, u32[]{:S(2)}) collective-permute-start(bf16[768,256]{1,0:T(8,128)(2,1)S(1)} %get-tuple-element.41), channel_id=1, source_target_pairs={{0,16},{4,20},{8,24},{12,28},{16,0},{20,4},{24,8},{28,12},{32,48},... | collective-permute-start | bytes 1179656 | tf_op jit(solution)/shard_map/ppermute | solution.py:417
  33.3 18.5 %collective-permute-start.14 = (bf16[768,256]{1,0:T(8,128)(2,1)S(1)}, bf16[768,256]{1,0:T(8,128)(2,1)S(1)}, u32[]{:S(2)}, u32[]{:S(2)}) collective-permute-start(bf16[768,256]{1,0:T(8,128)(2,1)S(1)} %get-tuple-element.41), channel_id=1, source_target_pairs={{0,8},{4,12},{8,16},{12,20},{16,24},{20,28},{24,0},{28,4},{32,40},... | collective-permute-start | bytes 1179656 | tf_op jit(solution)/shard_map/ppermute | solution.py:417
  34.8 15.5 %collective-permute-start.13 = (bf16[384,256]{1,0:T(8,128)(2,1)S(1)}, bf16[384,256]{1,0:T(8,128)(2,1)S(1)}, u32[]{:S(2)}, u32[]{:S(2)}) collective-permute-start(bf16[384,256]{1,0:T(8,128)(2,1)S(1)} %collective-permute-done.12.own3), channel_id=1, source_target_pairs={{0,32},{4,36},{8,40},{12,44},{16,48},{20,52},{24,56},{28,60},{32,6... | collective-permute-start | bytes 589832 | tf_op jit(solution)/shard_map/ppermute | solution.py:417
  51.9 19.8 %collective-permute-start.17 = (bf16[768,256]{1,0:T(8,128)(2,1)S(1)}, bf16[768,256]{1,0:T(8,128)(2,1)S(1)}, u32[]{:S(2)}, u32[]{:S(2)}) collective-permute-start(bf16[768,256]{1,0:T(8,128)(2,1)S(1)} %get-tuple-element.45), channel_id=1, source_target_pairs={{0,8},{4,12},{8,16},{12,20},{16,24},{20,28},{24,0},{28,4},{32,40},... | collective-permute-start | bytes 1179656 | tf_op jit(solution)/shard_map/ppermute | solution.py:417
  55.4 16.3 %collective-permute-start.18 = (bf16[768,256]{1,0:T(8,128)(2,1)S(1)}, bf16[768,256]{1,0:T(8,128)(2,1)S(1)}, u32[]{:S(2)}, u32[]{:S(2)}) collective-permute-start(bf16[768,256]{1,0:T(8,128)(2,1)S(1)} %get-tuple-element.46), channel_id=1, source_target_pairs={{0,16},{4,20},{8,24},{12,28},{16,0},{20,4},{24,8},{28,12},{32,48},... | collective-permute-start | bytes 1179656 | tf_op jit(solution)/shard_map/ppermute | solution.py:417
  55.4 20.3 %collective-permute-start.19 = (bf16[768,256]{1,0:T(8,128)(2,1)S(1)}, bf16[768,256]{1,0:T(8,128)(2,1)S(1)}, u32[]{:S(2)}, u32[]{:S(2)}) collective-permute-start(bf16[768,256]{1,0:T(8,128)(2,1)S(1)} %get-tuple-element.47), channel_id=1, source_target_pairs={{0,24},{4,28},{8,0},{12,4},{16,8},{20,12},{24,16},{28,20},{32,56},... | collective-permute-start | bytes 1179656 | tf_op jit(solution)/shard_map/ppermute | solution.py:417
  83.7 10.3 %collective-permute-start.20 = (bf16[192,512]{1,0:T(8,128)(2,1)S(1)}, bf16[192,512]{1,0:T(8,128)(2,1)S(1)}, u32[]{:S(2)}, u32[]{:S(2)}) collective-permute-start(bf16[192,512]{1,0:T(8,128)(2,1)S(1)} %get-tuple-element.50), channel_id=1, source_target_pairs={{0,4},{4,0},{8,12},{12,8},{16,20},{20,16},{24,28},{28,24},{32,36},... | collective-permute-start | bytes 589832 | tf_op jit(solution)/shard_map/ppermute | solution.py:417

commit v3 on v2

--- a/solution.py
+++ b/solution.py
@@ -222,9 +222,9 @@
     return lax.transpose(lax.rsqrt(total * (1.0 / WIDTH) + EPSILON), (1, 0))[:, :1]
 
 
-def payload_kernel(own0, own3, own4, *refs):
+def payload_kernel(own0, own3, own4, *payloads):
     x = place()[1]
-    for shift, payload in enumerate(refs[4:], 1):
+    for shift, payload in enumerate(payloads, 1):
         payload[:PAIR] = own3[...]
 
         @pl.when(x + shift < X)
@@ -501,10 +501,10 @@
     payloads34 = call(
         payload_kernel,
         (shape((2 * PAIR, 2 * HEAD_DIM), BF16),) * 3,
-        [VMEM] * 7,
+        [VMEM] * 3,
         (VMEM,) * 3,
         name="payload",
-    )(own0, own3, own4, *others12, all_sums)
+    )(own0, own3, own4)
     others34 = [move(value, x_shift=shift) for shift, value in zip(x_shifts, payloads34)]
     queries, tops, acc = call(
         near_kernel,

time: 96.8 us -> 99.4 us (1.027)
  the two profiles are of different devices: /device:TPU:103 before, /device:TPU:161 now
where the time goes in v3:
time: 99.4 us; the launch traced here: 98.1 us
  blocking collectives  33 us (33%)
  Pallas kernels  26.6 us (27%)
  starting transfers between devices  23.6 us (24%)
  waiting for transfers between devices  12.7 us (13%)
  local copies, waits for them, and re-layouts  1.92 us (2%)
    all_to_all x2, blocking collectives, exchange(): return lax.all_to_all(sums, ('core', 'tp'), 0, 0, tiled=True)  33 us
    ppermute x21, starting transfers between devices, move(): return lax.ppermute(value, CTX, pairs)  23.6 us
    ppermute x21, waiting for transfers between devices, move(): return lax.ppermute(value, CTX, pairs)  12.7 us
    pallas_call x1, Pallas kernels, shards(): call(near_kernel, (shape((REPEAT, PAIR, HEAD_DIM), BF16), shape((REPEAT,...  12 us
    pallas_call x1, Pallas kernels, shards(): call(far_kernel, (shape((TOK, COLS), BF16), shape((TOK, COLS), BF16), sha...  7.98 us
  transfers between devices with their start and end apart: 21, of which 7 were waited for; matrix products, arithmetic and copies ran while one was open for 0% of the time, Pallas kernels for 16%

profile of v3, /device:TPU:161, one launch (start us, length us, event | category | flops | bytes accessed | tf_op | source)
XLA Modules:
  0.0 98.1 jit_solution(17261160912987684305)
XLA Ops:
  0.0 1.0 slice_bitcast_fusion.10
  1.0 0.9 slice_bitcast_fusion.8
  3.5 1.2 %collective-permute-done.seg_r = s32[192]{0:T(256)S(1)} collective-permute-done((s32[192]{0:T(256)S(1)}, s32[192]{0:T(256)S(1)}, u32[]{:S(2)}, u32[]{:S(2)}) %collective-permute-start) | collective-permute-done | bytes 800 | tf_op jit(solution)/shard_map/ppermute | solution.py:417
  4.7 1.4 %prep.1 = (bf16[384,256]{1,0:T(8,128)(2,1)S(1)}, bf16[384,256]{1,0:T(8,128)(2,1)S(1)}, bf16[144,128]{1,0:T(8,128)(2,1)S(1)}, s32[8]{0:T(128)S(1)}) custom-call(s32[192]{0:T(256)S(1)} %copy-done, s32[192]{0:T(256)S(1)} %collective-permute-done.seg_r, bf16[4,192,128]{2,1,0:T(8,128)(2,1)S(1)} %get-tuple-element.58.own, ...), custom_call_target="tpu_custom_call" | custom-call | tf_op jit(solution)/shard_map/prep/pallas_call | solution.py:442
  6.0 0.8 collective-permute-start.5
  6.9 2.5 %collective-permute-start.4 = (bf16[144,128]{1,0:T(8,128)(2,1)S(1)}, bf16[144,128]{1,0:T(8,128)(2,1)S(1)}, u32[]{:S(2)}, u32[]{:S(2)}) collective-permute-start(bf16[144,128]{1,0:T(8,128)(2,1)S(1)} %get-tuple-element.29.own), channel_id=1, source_target_pairs={{0,24},{4,28},{8,0},{12,4},{16,8},{20,12},{24,16},{28,20},{32,56},... | collective-permute-start | bytes 110600 | tf_op jit(solution)/shard_map/ppermute | solution.py:417
  10.5 3.2 %collective-permute-done.3.from2 = bf16[144,128]{1,0:T(8,128)(2,1)S(1)} collective-permute-done((bf16[144,128]{1,0:T(8,128)(2,1)S(1)}, bf16[144,128]{1,0:T(8,128)(2,1)S(1)}, u32[]{:S(2)}, u32[]{:S(2)}) %collective-permute-start.3) | collective-permute-done | bytes 36896 | tf_op jit(solution)/shard_map/ppermute | solution.py:417
  14.7 0.8 collective-permute-start.11
  15.5 1.2 %collective-permute-start.10 = (bf16[144,128]{1,0:T(8,128)(2,1)S(1)}, bf16[144,128]{1,0:T(8,128)(2,1)S(1)}, u32[]{:S(2)}, u32[]{:S(2)}) collective-permute-start(bf16[144,128]{1,0:T(8,128)(2,1)S(1)} %get-tuple-element.32), channel_id=1, source_target_pairs={{0,128},{4,132},{8,136},{12,140},{16,144},{20,148},{24,152},{28,15... | collective-permute-start | bytes 110600 | tf_op jit(solution)/shard_map/ppermute | solution.py:417
  16.6 3.8 %collective-permute-start.9 = (bf16[144,128]{1,0:T(8,128)(2,1)S(1)}, bf16[144,128]{1,0:T(8,128)(2,1)S(1)}, u32[]{:S(2)}, u32[]{:S(2)}) collective-permute-start(bf16[144,128]{1,0:T(8,128)(2,1)S(1)} %get-tuple-element.32), channel_id=1, source_target_pairs={{0,96},{4,100},{8,104},{12,108},{16,112},{20,116},{24,120},{28,124... | collective-permute-start | bytes 110600 | tf_op jit(solution)/shard_map/ppermute | solution.py:417
  21.5 1.9 %inside.1 = (f32[384,512]{1,0:T(8,128)S(1)}, bf16[384,512]{1,0:T(8,128)(2,1)S(1)}) custom-call(s32[8]{0:T(128)S(1)} %get-tuple-element.28.info, bf16[2,192,512]{2,1,0:T(8,128)(2,1)S(1)} %get-tuple-element.51.keep, bf16[2,192,512]{2,1,0:T(8,128)(2,1)S(1)} %collective-permute-done.6.queries_r, bf16[384,256]{1,0:T(8,128)(2,1)S(1)} %get-tuple-element.33.packed), custom_call_target="tpu_custom_call" | custom-call | tf_op jit(solution)/shard_map/inside/pallas_call | solution.py:474
  24.1 2.0 %collective-permute-done.8.from2 = bf16[144,128]{1,0:T(8,128)(2,1)S(1)} collective-permute-done((bf16[144,128]{1,0:T(8,128)(2,1)S(1)}, bf16[144,128]{1,0:T(8,128)(2,1)S(1)}, u32[]{:S(2)}, u32[]{:S(2)}) %collective-permute-start.8) | collective-permute-done | bytes 36896 | tf_op jit(solution)/shard_map/ppermute | solution.py:417
  26.1 1.6 %first.1 = (f32[384,512]{1,0:T(8,128)S(1)}, f32[8,8,384]{2,1,0:T(8,128)S(1)}, s32[1]{0:T(128)}, bf16[768,256]{1,0:T(8,128)(2,1)S(1)}, bf16[384,256]{1,0:T(8,128)(2,1)S(1)}) custom-call(s32[8]{0:T(128)S(1)} %get-tuple-element.28.info, f32[136,128]{1,0:T(8,128)S(1)} %get-tuple-element.31.prefix, bf16[144,128]{1,0:T(8,128)(2,1)S(1)} %collective-permute-done.7.from1, ...), custom_call_target="tpu_custom_call" | custom-call | tf_op jit(solution)/shard_map/first/pallas_call | solution.py:481
  27.9 3.0 %collective-permute-start.16 = (bf16[768,256]{1,0:T(8,128)(2,1)S(1)}, bf16[768,256]{1,0:T(8,128)(2,1)S(1)}, u32[]{:S(2)}, u32[]{:S(2)}) collective-permute-start(bf16[768,256]{1,0:T(8,128)(2,1)S(1)} %get-tuple-element.41), channel_id=1, source_target_pairs={{0,24},{4,28},{8,0},{12,4},{16,8},{20,12},{24,16},{28,20},{32,56},... | collective-permute-start | bytes 1179656 | tf_op jit(solution)/shard_map/ppermute | solution.py:417
  30.8 2.0 %collective-permute-done.12.own3 = bf16[384,256]{1,0:T(8,128)(2,1)S(1)} collective-permute-done((bf16[384,256]{1,0:T(8,128)(2,1)S(1)}, bf16[384,256]{1,0:T(8,128)(2,1)S(1)}, u32[]{:S(2)}, u32[]{:S(2)}) %collective-permute-start.12) | collective-permute-done | bytes 196640 | tf_op jit(solution)/shard_map/ppermute | solution.py:417
  32.9 2.5 %collective-permute-start.15 = (bf16[768,256]{1,0:T(8,128)(2,1)S(1)}, bf16[768,256]{1,0:T(8,128)(2,1)S(1)}, u32[]{:S(2)}, u32[]{:S(2)}) collective-permute-start(bf16[768,256]{1,0:T(8,128)(2,1)S(1)} %get-tuple-element.41), channel_id=1, source_target_pairs={{0,16},{4,20},{8,24},{12,28},{16,0},{20,4},{24,8},{28,12},{32,48},... | collective-permute-start | bytes 1179656 | tf_op jit(solution)/shard_map/ppermute | solution.py:417
  35.9 3.1 %collective-permute-done.13.own4 = bf16[384,256]{1,0:T(8,128)(2,1)S(1)} collective-permute-done((bf16[384,256]{1,0:T(8,128)(2,1)S(1)}, bf16[384,256]{1,0:T(8,128)(2,1)S(1)}, u32[]{:S(2)}, u32[]{:S(2)}) %collective-permute-start.13) | collective-permute-done | bytes 196640 | tf_op jit(solution)/shard_map/ppermute | solution.py:417
  40.0 2.4 %collective-permute-start.18 = (bf16[768,256]{1,0:T(8,128)(2,1)S(1)}, bf16[768,256]{1,0:T(8,128)(2,1)S(1)}, u32[]{:S(2)}, u32[]{:S(2)}) collective-permute-start(bf16[768,256]{1,0:T(8,128)(2,1)S(1)} %get-tuple-element.46), channel_id=1, source_target_pairs={{0,16},{4,20},{8,24},{12,28},{16,0},{20,4},{24,8},{28,12},{32,48},... | collective-permute-start | bytes 1179656 | tf_op jit(solution)/shard_map/ppermute | solution.py:417
  42.4 1.3 %collective-permute-start.19 = (bf16[768,256]{1,0:T(8,128)(2,1)S(1)}, bf16[768,256]{1,0:T(8,128)(2,1)S(1)}, u32[]{:S(2)}, u32[]{:S(2)}) collective-permute-start(bf16[768,256]{1,0:T(8,128)(2,1)S(1)} %get-tuple-element.47), channel_id=1, source_target_pairs={{0,24},{4,28},{8,0},{12,4},{16,8},{20,12},{24,16},{28,20},{32,56},... | collective-permute-start | bytes 1179656 | tf_op jit(solution)/shard_map/ppermute | solution.py:417
  43.7 25.3 %all_to_all.10.sums = f32[8,8,384]{2,1,0:T(8,128)S(1)} all-to-all(f32[8,8,384]{2,1,0:T(8,128)S(1)} %get-tuple-element.38), channel_id=1, replica_groups=mesh['z'=8,'x'=4,'core'=2,'tp'=4] {'core','tp'}, dimensions={0} | all-to-all | bytes 196608 | tf_op jit(solution)/shard_map/all_to_all | solution.py:425
  69.0 12.0 %near.1 = (bf16[4,384,128]{2,1,0:T(8,128)(2,1)S(1)}, f32[4,384,128]{2,1,0:T(8,128)S(1)}, f32[4,384,256]{2,1,0:T(8,128)S(1)}) custom-call(s32[1]{0:T(128)} %get-tuple-element.37.reach, f32[8,8,384]{2,1,0:T(8,128)S(1)} %all_to_all.10.sums, f32[384,512]{1,0:T(8,128)S(1)} %get-tuple-element.39.first, bf16[2,192,512]{2,1,0:T(8,128)(2,1)S(1)} %get-tuple-element.51.keep, ...), custom_call_target="tpu_custom_call" | custom-call | tf_op jit(solution)/shard_map/near/pallas_call | solution.py:509
  81.0 8.0 %far.1 = (bf16[192,512]{1,0:T(8,128)(2,1)S(1)}, bf16[192,512]{1,0:T(8,128)(2,1)S(1)}, f32[8,8,192]{2,1,0:T(8,128)S(1)}, f32[4,384,128]{2,1,0:T(8,128)S(1)}, f32[4,384,256]{2,1,0:T(8,128)S(1)}) custom-call(s32[8]{0:T(128)S(1)} %get-tuple-element.28.info, s32[1]{0:T(128)} %get-tuple-element.37.reach, ...), custom_call_target="tpu_custom_call", output_to_operand_aliasing={{3}: (3, {}), {4}: (4, {})} | custom-call | tf_op jit(solution)/shard_map/far/pallas_call | solution.py:528
  89.4 7.7 %all_to_all.11.sums = f32[8,8,192]{2,1,0:T(8,128)S(1)} all-to-all(f32[8,8,192]{2,1,0:T(8,128)S(1)} %get-tuple-element.48), channel_id=1, replica_groups=mesh['z'=8,'x'=4,'core'=2,'tp'=4] {'core','tp'}, dimensions={0} | all-to-all | bytes 98304 | tf_op jit(solution)/shard_map/all_to_all | solution.py:425
  97.1 1.0 %last.1 = bf16[192,1024]{1,0:T(8,128)(2,1)} custom-call(f32[8,8,192]{2,1,0:T(8,128)S(1)} %all_to_all.11.sums, bf16[192,512]{1,0:T(8,128)(2,1)S(1)} %get-tuple-element.49.mine, bf16[192,512]{1,0:T(8,128)(2,1)S(1)} %collective-permute-done.20.theirs), custom_call_target="tpu_custom_call" | custom-call | tf_op jit(solution)/shard_map/last/pallas_call | solution.py:549
  (39 shorter events, 7.3 us)
Async XLA Ops:
  0.0 2.7 %copy-start.1 = (bf16[192,1024]{1,0:T(8,128)(2,1)S(1)}, bf16[192,1024]{1,0:T(8,128)(2,1)}, u32[]{:S(2)}) copy-start(bf16[192,1024]{1,0:T(8,128)(2,1)} %param.11) | copy-start | bytes 1179652
  0.0 2.7 %copy-start.2 = (bf16[192,1024]{1,0:T(8,128)(2,1)S(1)}, bf16[192,1024]{1,0:T(8,128)(2,1)}, u32[]{:S(2)}) copy-start(bf16[192,1024]{1,0:T(8,128)(2,1)} %param.7) | copy-start | bytes 1179652
  1.9 1.1 %copy-start = (s32[192]{0:T(256)S(1)}, s32[192]{0:T(256)}, u32[]{:S(2)}) copy-start(s32[192]{0:T(256)} %seg.1) | copy-start | bytes 2308
  1.9 2.7 %collective-permute-start.1 = (bf16[4,192,128]{2,1,0:T(8,128)(2,1)S(1)}, bf16[4,192,128]{2,1,0:T(8,128)(2,1)S(1)}, u32[]{:S(2)}, u32[]{:S(2)}) collective-permute-start(bf16[4,192,128]{2,1,0:T(8,128)(2,1)S(1)} %get-tuple-element.57), channel_id=1, source_target_pairs={{0,4},{4,0},{8,12},{12,8},{16,20},{20,16},{24,28},{28,24},{32,36},... | collective-permute-start | bytes 589832 | tf_op jit(solution)/shard_map/ppermute | solution.py:417
  2.9 11.2 %collective-permute-start.6 = (bf16[2,192,512]{2,1,0:T(8,128)(2,1)S(1)}, bf16[2,192,512]{2,1,0:T(8,128)(2,1)S(1)}, u32[]{:S(2)}, u32[]{:S(2)}) collective-permute-start(bf16[2,192,512]{2,1,0:T(8,128)(2,1)S(1)} %get-tuple-element.52), channel_id=1, source_target_pairs={{0,4},{4,0},{8,12},{12,8},{16,20},{20,16},{24,28},{28,24},{32,36},... | collective-permute-start | bytes 1179656 | tf_op jit(solution)/shard_map/ppermute | solution.py:417
  3.0 1.7 %collective-permute-start = (s32[192]{0:T(256)S(1)}, s32[192]{0:T(256)S(1)}, u32[]{:S(2)}, u32[]{:S(2)}) collective-permute-start(s32[192]{0:T(256)S(1)} %copy-done), channel_id=1, source_target_pairs={{0,4},{4,0},{8,12},{12,8},{16,20},{20,16},{24,28},{28,24},{32,36},... | collective-permute-start | bytes 2312 | tf_op jit(solution)/shard_map/ppermute | solution.py:417
  6.0 8.0 %collective-permute-start.5 = (bf16[384,256]{1,0:T(8,128)(2,1)S(1)}, bf16[384,256]{1,0:T(8,128)(2,1)S(1)}, u32[]{:S(2)}, u32[]{:S(2)}) collective-permute-start(bf16[384,256]{1,0:T(8,128)(2,1)S(1)} %get-tuple-element.30.own0), channel_id=1, source_target_pairs={{0,32},{4,36},{8,40},{12,44},{16,48},{20,52},{24,56},{28,60},{32,6... | collective-permute-start | bytes 589832 | tf_op jit(solution)/shard_map/ppermute | solution.py:417
  6.9 3.6 %collective-permute-start.4 = (bf16[144,128]{1,0:T(8,128)(2,1)S(1)}, bf16[144,128]{1,0:T(8,128)(2,1)S(1)}, u32[]{:S(2)}, u32[]{:S(2)}) collective-permute-start(bf16[144,128]{1,0:T(8,128)(2,1)S(1)} %get-tuple-element.29.own), channel_id=1, source_target_pairs={{0,24},{4,28},{8,0},{12,4},{16,8},{20,12},{24,16},{28,20},{32,56},... | collective-permute-start | bytes 110600 | tf_op jit(solution)/shard_map/ppermute | solution.py:417
  9.3 4.3 %collective-permute-start.3 = (bf16[144,128]{1,0:T(8,128)(2,1)S(1)}, bf16[144,128]{1,0:T(8,128)(2,1)S(1)}, u32[]{:S(2)}, u32[]{:S(2)}) collective-permute-start(bf16[144,128]{1,0:T(8,128)(2,1)S(1)} %get-tuple-element.29.own), channel_id=1, source_target_pairs={{0,16},{4,20},{8,24},{12,28},{16,0},{20,4},{24,8},{28,12},{32,48},... | collective-permute-start | bytes 110600 | tf_op jit(solution)/shard_map/ppermute | solution.py:417
  9.9 4.2 %collective-permute-start.2 = (bf16[144,128]{1,0:T(8,128)(2,1)S(1)}, bf16[144,128]{1,0:T(8,128)(2,1)S(1)}, u32[]{:S(2)}, u32[]{:S(2)}) collective-permute-start(bf16[144,128]{1,0:T(8,128)(2,1)S(1)} %get-tuple-element.29.own), channel_id=1, source_target_pairs={{0,8},{4,12},{8,16},{12,20},{16,24},{20,28},{24,0},{28,4},{32,40},... | collective-permute-start | bytes 110600 | tf_op jit(solution)/shard_map/ppermute | solution.py:417
  14.7 11.5 %collective-permute-start.11 = (bf16[384,256]{1,0:T(8,128)(2,1)S(1)}, bf16[384,256]{1,0:T(8,128)(2,1)S(1)}, u32[]{:S(2)}, u32[]{:S(2)}) collective-permute-start(bf16[384,256]{1,0:T(8,128)(2,1)S(1)} %get-tuple-element.36), channel_id=1, source_target_pairs={{0,32},{4,36},{8,40},{12,44},{16,48},{20,52},{24,56},{28,60},{32,6... | collective-permute-start | bytes 589832 | tf_op jit(solution)/shard_map/ppermute | solution.py:417
  15.5 7.9 %collective-permute-start.10 = (bf16[144,128]{1,0:T(8,128)(2,1)S(1)}, bf16[144,128]{1,0:T(8,128)(2,1)S(1)}, u32[]{:S(2)}, u32[]{:S(2)}) collective-permute-start(bf16[144,128]{1,0:T(8,128)(2,1)S(1)} %get-tuple-element.32), channel_id=1, source_target_pairs={{0,128},{4,132},{8,136},{12,140},{16,144},{20,148},{24,152},{28,15... | collective-permute-start | bytes 110600 | tf_op jit(solution)/shard_map/ppermute | solution.py:417
  16.6 7.4 %collective-permute-start.9 = (bf16[144,128]{1,0:T(8,128)(2,1)S(1)}, bf16[144,128]{1,0:T(8,128)(2,1)S(1)}, u32[]{:S(2)}, u32[]{:S(2)}) collective-permute-start(bf16[144,128]{1,0:T(8,128)(2,1)S(1)} %get-tuple-element.32), channel_id=1, source_target_pairs={{0,96},{4,100},{8,104},{12,108},{16,112},{20,116},{24,120},{28,124... | collective-permute-start | bytes 110600 | tf_op jit(solution)/shard_map/ppermute | solution.py:417
  20.4 5.7 %collective-permute-start.8 = (bf16[144,128]{1,0:T(8,128)(2,1)S(1)}, bf16[144,128]{1,0:T(8,128)(2,1)S(1)}, u32[]{:S(2)}, u32[]{:S(2)}) collective-permute-start(bf16[144,128]{1,0:T(8,128)(2,1)S(1)} %get-tuple-element.32), channel_id=1, source_target_pairs={{0,64},{4,68},{8,72},{12,76},{16,80},{20,84},{24,88},{28,92},{32,9... | collective-permute-start | bytes 110600 | tf_op jit(solution)/shard_map/ppermute | solution.py:417
  21.0 5.2 %collective-permute-start.7 = (bf16[144,128]{1,0:T(8,128)(2,1)S(1)}, bf16[144,128]{1,0:T(8,128)(2,1)S(1)}, u32[]{:S(2)}, u32[]{:S(2)}) collective-permute-start(bf16[144,128]{1,0:T(8,128)(2,1)S(1)} %get-tuple-element.32), channel_id=1, source_target_pairs={{0,32},{4,36},{8,40},{12,44},{16,48},{20,52},{24,56},{28,60},{32,6... | collective-permute-start | bytes 110600 | tf_op jit(solution)/shard_map/ppermute | solution.py:417
  27.8 5.1 %collective-permute-start.12 = (bf16[384,256]{1,0:T(8,128)(2,1)S(1)}, bf16[384,256]{1,0:T(8,128)(2,1)S(1)}, u32[]{:S(2)}, u32[]{:S(2)}) collective-permute-start(bf16[384,256]{1,0:T(8,128)(2,1)S(1)} %get-tuple-element.40), channel_id=1, source_target_pairs={{0,32},{4,36},{8,40},{12,44},{16,48},{20,52},{24,56},{28,60},{32,6... | collective-permute-start | bytes 589832 | tf_op jit(solution)/shard_map/ppermute | solution.py:417
  27.9 14.5 %collective-permute-start.16 = (bf16[768,256]{1,0:T(8,128)(2,1)S(1)}, bf16[768,256]{1,0:T(8,128)(2,1)S(1)}, u32[]{:S(2)}, u32[]{:S(2)}) collective-permute-start(bf16[768,256]{1,0:T(8,128)(2,1)S(1)} %get-tuple-element.41), channel_id=1, source_target_pairs={{0,24},{4,28},{8,0},{12,4},{16,8},{20,12},{24,16},{28,20},{32,56},... | collective-permute-start | bytes 1179656 | tf_op jit(solution)/shard_map/ppermute | solution.py:417
  32.9 6.2 %collective-permute-start.13 = (bf16[384,256]{1,0:T(8,128)(2,1)S(1)}, bf16[384,256]{1,0:T(8,128)(2,1)S(1)}, u32[]{:S(2)}, u32[]{:S(2)}) collective-permute-start(bf16[384,256]{1,0:T(8,128)(2,1)S(1)} %collective-permute-done.12.own3), channel_id=1, source_target_pairs={{0,32},{4,36},{8,40},{12,44},{16,48},{20,52},{24,56},{28,60},{32,6... | collective-permute-start | bytes 589832 | tf_op jit(solution)/shard_map/ppermute | solution.py:417
  32.9 36.1 %collective-permute-start.15 = (bf16[768,256]{1,0:T(8,128)(2,1)S(1)}, bf16[768,256]{1,0:T(8,128)(2,1)S(1)}, u32[]{:S(2)}, u32[]{:S(2)}) collective-permute-start(bf16[768,256]{1,0:T(8,128)(2,1)S(1)} %get-tuple-element.41), channel_id=1, source_target_pairs={{0,16},{4,20},{8,24},{12,28},{16,0},{20,4},{24,8},{28,12},{32,48},... | collective-permute-start | bytes 1179656 | tf_op jit(solution)/shard_map/ppermute | solution.py:417
  35.4 33.6 %collective-permute-start.14 = (bf16[768,256]{1,0:T(8,128)(2,1)S(1)}, bf16[768,256]{1,0:T(8,128)(2,1)S(1)}, u32[]{:S(2)}, u32[]{:S(2)}) collective-permute-start(bf16[768,256]{1,0:T(8,128)(2,1)S(1)} %get-tuple-element.41), channel_id=1, source_target_pairs={{0,8},{4,12},{8,16},{12,20},{16,24},{20,28},{24,0},{28,4},{32,40},... | collective-permute-start | bytes 1179656 | tf_op jit(solution)/shard_map/ppermute | solution.py:417
  39.2 41.8 %collective-permute-start.17 = (bf16[768,256]{1,0:T(8,128)(2,1)S(1)}, bf16[768,256]{1,0:T(8,128)(2,1)S(1)}, u32[]{:S(2)}, u32[]{:S(2)}) collective-permute-start(bf16[768,256]{1,0:T(8,128)(2,1)S(1)} %get-tuple-element.45), channel_id=1, source_target_pairs={{0,8},{4,12},{8,16},{12,20},{16,24},{20,28},{24,0},{28,4},{32,40},... | collective-permute-start | bytes 1179656 | tf_op jit(solution)/shard_map/ppermute | solution.py:417
  40.0 41.0 %collective-permute-start.18 = (bf16[768,256]{1,0:T(8,128)(2,1)S(1)}, bf16[768,256]{1,0:T(8,128)(2,1)S(1)}, u32[]{:S(2)}, u32[]{:S(2)}) collective-permute-start(bf16[768,256]{1,0:T(8,128)(2,1)S(1)} %get-tuple-element.46), channel_id=1, source_target_pairs={{0,16},{4,20},{8,24},{12,28},{16,0},{20,4},{24,8},{28,12},{32,48},... | collective-permute-start | bytes 1179656 | tf_op jit(solution)/shard_map/ppermute | solution.py:417
  42.4 38.6 %collective-permute-start.19 = (bf16[768,256]{1,0:T(8,128)(2,1)S(1)}, bf16[768,256]{1,0:T(8,128)(2,1)S(1)}, u32[]{:S(2)}, u32[]{:S(2)}) collective-permute-start(bf16[768,256]{1,0:T(8,128)(2,1)S(1)} %get-tuple-element.47), channel_id=1, source_target_pairs={{0,24},{4,28},{8,0},{12,4},{16,8},{20,12},{24,16},{28,20},{32,56},... | collective-permute-start | bytes 1179656 | tf_op jit(solution)/shard_map/ppermute | solution.py:417
  89.0 8.1 %collective-permute-start.20 = (bf16[192,512]{1,0:T(8,128)(2,1)S(1)}, bf16[192,512]{1,0:T(8,128)(2,1)S(1)}, u32[]{:S(2)}, u32[]{:S(2)}) collective-permute-start(bf16[192,512]{1,0:T(8,128)(2,1)S(1)} %get-tuple-element.50), channel_id=1, source_target_pairs={{0,4},{4,0},{8,12},{12,8},{16,20},{20,16},{24,28},{28,24},{32,36},... | collective-permute-start | bytes 589832 | tf_op jit(solution)/shard_map/ppermute | solution.py:417

commit v4 on v3

--- a/solution.py
+++ b/solution.py
@@ -222,7 +222,7 @@
     return lax.transpose(lax.rsqrt(total * (1.0 / WIDTH) + EPSILON), (1, 0))[:, :1]
 
 
-def payload_kernel(own0, own3, own4, *payloads):
+def payload_kernel(own0, own3, own4, _, *payloads):
     x = place()[1]
     for shift, payload in enumerate(payloads, 1):
         payload[:PAIR] = own3[...]
@@ -501,10 +501,10 @@
     payloads34 = call(
         payload_kernel,
         (shape((2 * PAIR, 2 * HEAD_DIM), BF16),) * 3,
-        [VMEM] * 3,
+        [VMEM] * 4,
         (VMEM,) * 3,
         name="payload",
-    )(own0, own3, own4)
+    )(own0, own3, own4, all_sums)
     others34 = [move(value, x_shift=shift) for shift, value in zip(x_shifts, payloads34)]
     queries, tops, acc = call(
         near_kernel,

time: 99.4 us -> 104 us (1.046)
  the two profiles are of different devices: /device:TPU:161 before, /device:TPU:101 now
where the time goes in v4:
time: 104 us; the launch traced here: 105 us
  starting transfers between devices  34.7 us (33%)
  Pallas kernels  29.7 us (29%)
  waiting for transfers between devices  28.7 us (28%)
  blocking collectives  9.3 us (9%)
  local copies, waits for them, and re-layouts  1.92 us (2%)
    ppermute x21, starting transfers between devices, move(): return lax.ppermute(value, CTX, pairs)  26.7 us
    ppermute x21, waiting for transfers between devices, move(): return lax.ppermute(value, CTX, pairs)  25.7 us
    pallas_call x1, Pallas kernels, shards(): call(near_kernel, (shape((REPEAT, PAIR, HEAD_DIM), BF16), shape((REPEAT,...  12.9 us
    pallas_call x1, Pallas kernels, shards(): call(far_kernel, (shape((TOK, COLS), BF16), shape((TOK, COLS), BF16), sha...  10 us
    all_to_all x1, blocking collectives, exchange(): return lax.all_to_all(sums, ('core', 'tp'), 0, 0, tiled=True)  9.3 us
    all_to_all x1, starting transfers between devices, exchange(): return lax.all_to_all(sums, ('core', 'tp'), 0, 0, tiled=True)  7.98 us
    all_to_all x1, waiting for transfers between devices, exchange(): return lax.all_to_all(sums, ('core', 'tp'), 0, 0, tiled=True)  2.96 us
  transfers between devices with their start and end apart: 22, of which 11 were waited for; matrix products, arithmetic and copies ran while one was open for 0% of the time, Pallas kernels for 16%

profile of v4, /device:TPU:101, one launch (start us, length us, event | category | flops | bytes accessed | tf_op | source)
XLA Modules:
  0.0 104.6 jit_solution(2350672048179475010)
XLA Ops:
  3.5 1.2 %collective-permute-done.seg_r = s32[192]{0:T(256)S(1)} collective-permute-done((s32[192]{0:T(256)S(1)}, s32[192]{0:T(256)S(1)}, u32[]{:S(2)}, u32[]{:S(2)}) %collective-permute-start) | collective-permute-done | bytes 800 | tf_op jit(solution)/shard_map/ppermute | solution.py:417
  4.7 1.4 %prep.1 = (bf16[384,256]{1,0:T(8,128)(2,1)S(1)}, bf16[384,256]{1,0:T(8,128)(2,1)S(1)}, bf16[144,128]{1,0:T(8,128)(2,1)S(1)}, s32[8]{0:T(128)S(1)}) custom-call(s32[192]{0:T(256)S(1)} %copy-done, s32[192]{0:T(256)S(1)} %collective-permute-done.seg_r, bf16[4,192,128]{2,1,0:T(8,128)(2,1)S(1)} %get-tuple-element.58.own, ...), custom_call_target="tpu_custom_call" | custom-call | tf_op jit(solution)/shard_map/prep/pallas_call | solution.py:442
  6.0 2.9 %collective-permute-start.5 = (bf16[384,256]{1,0:T(8,128)(2,1)S(1)}, bf16[384,256]{1,0:T(8,128)(2,1)S(1)}, u32[]{:S(2)}, u32[]{:S(2)}) collective-permute-start(bf16[384,256]{1,0:T(8,128)(2,1)S(1)} %get-tuple-element.30.own0), channel_id=1, source_target_pairs={{0,32},{4,36},{8,40},{12,44},{16,48},{20,52},{24,56},{28,60},{32,6... | collective-permute-start | bytes 589832 | tf_op jit(solution)/shard_map/ppermute | solution.py:417
  9.2 2.5 %collective-permute-start.3 = (bf16[144,128]{1,0:T(8,128)(2,1)S(1)}, bf16[144,128]{1,0:T(8,128)(2,1)S(1)}, u32[]{:S(2)}, u32[]{:S(2)}) collective-permute-start(bf16[144,128]{1,0:T(8,128)(2,1)S(1)} %get-tuple-element.29.own), channel_id=1, source_target_pairs={{0,16},{4,20},{8,24},{12,28},{16,0},{20,4},{24,8},{28,12},{32,48},... | collective-permute-start | bytes 110600 | tf_op jit(solution)/shard_map/ppermute | solution.py:417
  12.1 1.5 %collective-permute-done.3.from2 = bf16[144,128]{1,0:T(8,128)(2,1)S(1)} collective-permute-done((bf16[144,128]{1,0:T(8,128)(2,1)S(1)}, bf16[144,128]{1,0:T(8,128)(2,1)S(1)}, u32[]{:S(2)}, u32[]{:S(2)}) %collective-permute-start.3) | collective-permute-done | bytes 36896 | tf_op jit(solution)/shard_map/ppermute | solution.py:417
  13.5 1.5 %collective-permute-done.2.from1 = bf16[144,128]{1,0:T(8,128)(2,1)S(1)} collective-permute-done((bf16[144,128]{1,0:T(8,128)(2,1)S(1)}, bf16[144,128]{1,0:T(8,128)(2,1)S(1)}, u32[]{:S(2)}, u32[]{:S(2)}) %collective-permute-start.2) | collective-permute-done | bytes 36896 | tf_op jit(solution)/shard_map/ppermute | solution.py:417
  15.6 1.6 %collective-permute-start.11 = (bf16[384,256]{1,0:T(8,128)(2,1)S(1)}, bf16[384,256]{1,0:T(8,128)(2,1)S(1)}, u32[]{:S(2)}, u32[]{:S(2)}) collective-permute-start(bf16[384,256]{1,0:T(8,128)(2,1)S(1)} %get-tuple-element.36), channel_id=1, source_target_pairs={{0,32},{4,36},{8,40},{12,44},{16,48},{20,52},{24,56},{28,60},{32,6... | collective-permute-start | bytes 589832 | tf_op jit(solution)/shard_map/ppermute | solution.py:417
  17.2 1.6 %collective-permute-start.10 = (bf16[144,128]{1,0:T(8,128)(2,1)S(1)}, bf16[144,128]{1,0:T(8,128)(2,1)S(1)}, u32[]{:S(2)}, u32[]{:S(2)}) collective-permute-start(bf16[144,128]{1,0:T(8,128)(2,1)S(1)} %get-tuple-element.32), channel_id=1, source_target_pairs={{0,128},{4,132},{8,136},{12,140},{16,144},{20,148},{24,152},{28,15... | collective-permute-start | bytes 110600 | tf_op jit(solution)/shard_map/ppermute | solution.py:417
  18.9 2.5 %collective-permute-start.9 = (bf16[144,128]{1,0:T(8,128)(2,1)S(1)}, bf16[144,128]{1,0:T(8,128)(2,1)S(1)}, u32[]{:S(2)}, u32[]{:S(2)}) collective-permute-start(bf16[144,128]{1,0:T(8,128)(2,1)S(1)} %get-tuple-element.32), channel_id=1, source_target_pairs={{0,96},{4,100},{8,104},{12,108},{16,112},{20,116},{24,120},{28,124... | collective-permute-start | bytes 110600 | tf_op jit(solution)/shard_map/ppermute | solution.py:417
  21.4 1.4 %collective-permute-start.8 = (bf16[144,128]{1,0:T(8,128)(2,1)S(1)}, bf16[144,128]{1,0:T(8,128)(2,1)S(1)}, u32[]{:S(2)}, u32[]{:S(2)}) collective-permute-start(bf16[144,128]{1,0:T(8,128)(2,1)S(1)} %get-tuple-element.32), channel_id=1, source_target_pairs={{0,64},{4,68},{8,72},{12,76},{16,80},{20,84},{24,88},{28,92},{32,9... | collective-permute-start | bytes 110600 | tf_op jit(solution)/shard_map/ppermute | solution.py:417
  23.4 1.9 %inside.1 = (f32[384,512]{1,0:T(8,128)S(1)}, bf16[384,512]{1,0:T(8,128)(2,1)S(1)}) custom-call(s32[8]{0:T(128)S(1)} %get-tuple-element.28.info, bf16[2,192,512]{2,1,0:T(8,128)(2,1)S(1)} %get-tuple-element.51.keep, bf16[2,192,512]{2,1,0:T(8,128)(2,1)S(1)} %collective-permute-done.6.queries_r, bf16[384,256]{1,0:T(8,128)(2,1)S(1)} %get-tuple-element.33.packed), custom_call_target="tpu_custom_call" | custom-call | tf_op jit(solution)/shard_map/inside/pallas_call | solution.py:474
  27.6 1.8 %first.1 = (f32[384,512]{1,0:T(8,128)S(1)}, f32[8,8,384]{2,1,0:T(8,128)}, s32[1]{0:T(128)}, bf16[768,256]{1,0:T(8,128)(2,1)}, bf16[384,256]{1,0:T(8,128)(2,1)S(1)}) custom-call(s32[8]{0:T(128)S(1)} %get-tuple-element.28.info, f32[136,128]{1,0:T(8,128)S(1)} %get-tuple-element.31.prefix, bf16[144,128]{1,0:T(8,128)(2,1)S(1)} %collective-permute-done.7.from1, ...), custom_call_target="tpu_custom_call" | custom-call | tf_op jit(solution)/shard_map/first/pallas_call | solution.py:481
  29.4 2.5 %collective-permute-start.12 = (bf16[384,256]{1,0:T(8,128)(2,1)S(1)}, bf16[384,256]{1,0:T(8,128)(2,1)S(1)}, u32[]{:S(2)}, u32[]{:S(2)}) collective-permute-start(bf16[384,256]{1,0:T(8,128)(2,1)S(1)} %get-tuple-element.40), channel_id=1, source_target_pairs={{0,32},{4,36},{8,40},{12,44},{16,48},{20,52},{24,56},{28,60},{32,6... | collective-permute-start | bytes 589832 | tf_op jit(solution)/shard_map/ppermute | solution.py:417
  32.1 2.4 %collective-permute-done.12.own3 = bf16[384,256]{1,0:T(8,128)(2,1)S(1)} collective-permute-done((bf16[384,256]{1,0:T(8,128)(2,1)S(1)}, bf16[384,256]{1,0:T(8,128)(2,1)S(1)}, u32[]{:S(2)}, u32[]{:S(2)}) %collective-permute-start.12) | collective-permute-done | bytes 196640 | tf_op jit(solution)/shard_map/ppermute | solution.py:417
  34.5 3.1 %collective-permute-start.13 = (bf16[384,256]{1,0:T(8,128)(2,1)S(1)}, bf16[384,256]{1,0:T(8,128)(2,1)S(1)}, u32[]{:S(2)}, u32[]{:S(2)}) collective-permute-start(bf16[384,256]{1,0:T(8,128)(2,1)S(1)} %collective-permute-done.12.own3), channel_id=1, source_target_pairs={{0,32},{4,36},{8,40},{12,44},{16,48},{20,52},{24,56},{28,60},{32,6... | collective-permute-start | bytes 589832 | tf_op jit(solution)/shard_map/ppermute | solution.py:417
  37.6 8.0 %all-to-all-start = ((f32[8,8,384]{2,1,0:T(8,128)}), f32[8,8,384]{2,1,0:T(8,128)S(1)}, u32[]{:S(2)}, u32[]{:S(2)}) async-start(f32[8,8,384]{2,1,0:T(8,128)} %get-tuple-element.38), calls=%async_computation | async-start | bytes 196608 | tf_op jit(solution)/shard_map/all_to_all | solution.py:425
  47.6 3.0 %all-to-all-done.sums._ = f32[8,8,384]{2,1,0:T(8,128)S(1)} async-done(((f32[8,8,384]{2,1,0:T(8,128)}), f32[8,8,384]{2,1,0:T(8,128)S(1)}, u32[]{:S(2)}, u32[]{:S(2)}) %all-to-all-start) | async-done | bytes 98336 | tf_op jit(solution)/shard_map/all_to_all | solution.py:425
  52.2 1.7 %collective-permute-start.19 = (bf16[768,256]{1,0:T(8,128)(2,1)S(1)}, bf16[768,256]{1,0:T(8,128)(2,1)S(1)}, u32[]{:S(2)}, u32[]{:S(2)}) collective-permute-start(bf16[768,256]{1,0:T(8,128)(2,1)S(1)} %get-tuple-element.47), channel_id=1, source_target_pairs={{0,24},{4,28},{8,0},{12,4},{16,8},{20,12},{24,16},{28,20},{32,56},... | collective-permute-start | bytes 1179656 | tf_op jit(solution)/shard_map/ppermute | solution.py:417
  53.9 4.2 %collective-permute-done.15.refs_1_ = bf16[768,256]{1,0:T(8,128)(2,1)S(1)} collective-permute-done((bf16[768,256]{1,0:T(8,128)(2,1)}, bf16[768,256]{1,0:T(8,128)(2,1)S(1)}, u32[]{:S(2)}, u32[]{:S(2)}) %collective-permute-start.15) | collective-permute-done | bytes 393248 | tf_op jit(solution)/shard_map/ppermute | solution.py:417
  58.1 7.6 %collective-permute-done.14.refs_0_ = bf16[768,256]{1,0:T(8,128)(2,1)} collective-permute-done((bf16[768,256]{1,0:T(8,128)(2,1)}, bf16[768,256]{1,0:T(8,128)(2,1)}, u32[]{:S(2)}, u32[]{:S(2)}) %collective-permute-start.14) | collective-permute-done | bytes 393248 | tf_op jit(solution)/shard_map/ppermute | solution.py:417
  65.7 12.9 %near.1 = (bf16[4,384,128]{2,1,0:T(8,128)(2,1)S(1)}, f32[4,384,128]{2,1,0:T(8,128)S(1)}, f32[4,384,256]{2,1,0:T(8,128)S(1)}) custom-call(s32[1]{0:T(128)} %get-tuple-element.37.reach, f32[8,8,384]{2,1,0:T(8,128)S(1)} %all-to-all-done.sums._, f32[384,512]{1,0:T(8,128)S(1)} %get-tuple-element.39.first, bf16[2,192,512]{2,1,0:T(8,128)(2,1)S(1)} %get-tuple-element.51.keep, ...), custom_call_target="tpu_custom_call" | custom-call | tf_op jit(solution)/shard_map/near/pallas_call | solution.py:509
  78.7 4.7 %collective-permute-done.18.refs_1_ = bf16[768,256]{1,0:T(8,128)(2,1)S(1)} collective-permute-done((bf16[768,256]{1,0:T(8,128)(2,1)S(1)}, bf16[768,256]{1,0:T(8,128)(2,1)S(1)}, u32[]{:S(2)}, u32[]{:S(2)}) %collective-permute-start.18) | collective-permute-done | bytes 393248 | tf_op jit(solution)/shard_map/ppermute | solution.py:417
  83.4 10.0 %far.1 = (bf16[192,512]{1,0:T(8,128)(2,1)S(1)}, bf16[192,512]{1,0:T(8,128)(2,1)S(1)}, f32[8,8,192]{2,1,0:T(8,128)S(1)}, f32[4,384,128]{2,1,0:T(8,128)S(1)}, f32[4,384,256]{2,1,0:T(8,128)S(1)}) custom-call(s32[8]{0:T(128)S(1)} %get-tuple-element.28.info, s32[1]{0:T(128)} %get-tuple-element.37.reach, ...), custom_call_target="tpu_custom_call", output_to_operand_aliasing={{3}: (3, {}), {4}: (4, {})} | custom-call | tf_op jit(solution)/shard_map/far/pallas_call | solution.py:528
  94.3 9.3 %all_to_all.10.sums = f32[8,8,192]{2,1,0:T(8,128)S(1)} all-to-all(f32[8,8,192]{2,1,0:T(8,128)S(1)} %get-tuple-element.48), channel_id=1, replica_groups=mesh['z'=8,'x'=4,'core'=2,'tp'=4] {'core','tp'}, dimensions={0} | all-to-all | bytes 98304 | tf_op jit(solution)/shard_map/all_to_all | solution.py:425
  (40 shorter events, 13.3 us)
Async XLA Ops:
  0.0 2.7 %copy-start.1 = (bf16[192,1024]{1,0:T(8,128)(2,1)S(1)}, bf16[192,1024]{1,0:T(8,128)(2,1)}, u32[]{:S(2)}) copy-start(bf16[192,1024]{1,0:T(8,128)(2,1)} %param.11) | copy-start | bytes 1179652
  0.0 2.7 %copy-start.2 = (bf16[192,1024]{1,0:T(8,128)(2,1)S(1)}, bf16[192,1024]{1,0:T(8,128)(2,1)}, u32[]{:S(2)}) copy-start(bf16[192,1024]{1,0:T(8,128)(2,1)} %param.7) | copy-start | bytes 1179652
  1.9 2.7 %collective-permute-start.1 = (bf16[4,192,128]{2,1,0:T(8,128)(2,1)S(1)}, bf16[4,192,128]{2,1,0:T(8,128)(2,1)S(1)}, u32[]{:S(2)}, u32[]{:S(2)}) collective-permute-start(bf16[4,192,128]{2,1,0:T(8,128)(2,1)S(1)} %get-tuple-element.57), channel_id=1, source_target_pairs={{0,4},{4,0},{8,12},{12,8},{16,20},{20,16},{24,28},{28,24},{32,36},... | collective-permute-start | bytes 589832 | tf_op jit(solution)/shard_map/ppermute | solution.py:417
  2.9 12.2 %collective-permute-start.6 = (bf16[2,192,512]{2,1,0:T(8,128)(2,1)S(1)}, bf16[2,192,512]{2,1,0:T(8,128)(2,1)S(1)}, u32[]{:S(2)}, u32[]{:S(2)}) collective-permute-start(bf16[2,192,512]{2,1,0:T(8,128)(2,1)S(1)} %get-tuple-element.52), channel_id=1, source_target_pairs={{0,4},{4,0},{8,12},{12,8},{16,20},{20,16},{24,28},{28,24},{32,36},... | collective-permute-start | bytes 1179656 | tf_op jit(solution)/shard_map/ppermute | solution.py:417
  3.0 1.7 %collective-permute-start = (s32[192]{0:T(256)S(1)}, s32[192]{0:T(256)S(1)}, u32[]{:S(2)}, u32[]{:S(2)}) collective-permute-start(s32[192]{0:T(256)S(1)} %copy-done), channel_id=1, source_target_pairs={{0,4},{4,0},{8,12},{12,8},{16,20},{20,16},{24,28},{28,24},{32,36},... | collective-permute-start | bytes 2312 | tf_op jit(solution)/shard_map/ppermute | solution.py:417
  6.0 9.0 %collective-permute-start.5 = (bf16[384,256]{1,0:T(8,128)(2,1)S(1)}, bf16[384,256]{1,0:T(8,128)(2,1)S(1)}, u32[]{:S(2)}, u32[]{:S(2)}) collective-permute-start(bf16[384,256]{1,0:T(8,128)(2,1)S(1)} %get-tuple-element.30.own0), channel_id=1, source_target_pairs={{0,32},{4,36},{8,40},{12,44},{16,48},{20,52},{24,56},{28,60},{32,6... | collective-permute-start | bytes 589832 | tf_op jit(solution)/shard_map/ppermute | solution.py:417
  9.0 3.1 %collective-permute-start.4 = (bf16[144,128]{1,0:T(8,128)(2,1)S(1)}, bf16[144,128]{1,0:T(8,128)(2,1)S(1)}, u32[]{:S(2)}, u32[]{:S(2)}) collective-permute-start(bf16[144,128]{1,0:T(8,128)(2,1)S(1)} %get-tuple-element.29.own), channel_id=1, source_target_pairs={{0,24},{4,28},{8,0},{12,4},{16,8},{20,12},{24,16},{28,20},{32,56},... | collective-permute-start | bytes 110600 | tf_op jit(solution)/shard_map/ppermute | solution.py:417
  9.2 4.3 %collective-permute-start.3 = (bf16[144,128]{1,0:T(8,128)(2,1)S(1)}, bf16[144,128]{1,0:T(8,128)(2,1)S(1)}, u32[]{:S(2)}, u32[]{:S(2)}) collective-permute-start(bf16[144,128]{1,0:T(8,128)(2,1)S(1)} %get-tuple-element.29.own), channel_id=1, source_target_pairs={{0,16},{4,20},{8,24},{12,28},{16,0},{20,4},{24,8},{28,12},{32,48},... | collective-permute-start | bytes 110600 | tf_op jit(solution)/shard_map/ppermute | solution.py:417
  11.7 3.3 %collective-permute-start.2 = (bf16[144,128]{1,0:T(8,128)(2,1)S(1)}, bf16[144,128]{1,0:T(8,128)(2,1)S(1)}, u32[]{:S(2)}, u32[]{:S(2)}) collective-permute-start(bf16[144,128]{1,0:T(8,128)(2,1)S(1)} %get-tuple-element.29.own), channel_id=1, source_target_pairs={{0,8},{4,12},{8,16},{12,20},{16,24},{20,28},{24,0},{28,4},{32,40},... | collective-permute-start | bytes 110600 | tf_op jit(solution)/shard_map/ppermute | solution.py:417
  15.6 12.0 %collective-permute-start.11 = (bf16[384,256]{1,0:T(8,128)(2,1)S(1)}, bf16[384,256]{1,0:T(8,128)(2,1)S(1)}, u32[]{:S(2)}, u32[]{:S(2)}) collective-permute-start(bf16[384,256]{1,0:T(8,128)(2,1)S(1)} %get-tuple-element.36), channel_id=1, source_target_pairs={{0,32},{4,36},{8,40},{12,44},{16,48},{20,52},{24,56},{28,60},{32,6... | collective-permute-start | bytes 589832 | tf_op jit(solution)/shard_map/ppermute | solution.py:417
  17.2 8.1 %collective-permute-start.10 = (bf16[144,128]{1,0:T(8,128)(2,1)S(1)}, bf16[144,128]{1,0:T(8,128)(2,1)S(1)}, u32[]{:S(2)}, u32[]{:S(2)}) collective-permute-start(bf16[144,128]{1,0:T(8,128)(2,1)S(1)} %get-tuple-element.32), channel_id=1, source_target_pairs={{0,128},{4,132},{8,136},{12,140},{16,144},{20,148},{24,152},{28,15... | collective-permute-start | bytes 110600 | tf_op jit(solution)/shard_map/ppermute | solution.py:417
  18.9 6.5 %collective-permute-start.9 = (bf16[144,128]{1,0:T(8,128)(2,1)S(1)}, bf16[144,128]{1,0:T(8,128)(2,1)S(1)}, u32[]{:S(2)}, u32[]{:S(2)}) collective-permute-start(bf16[144,128]{1,0:T(8,128)(2,1)S(1)} %get-tuple-element.32), channel_id=1, source_target_pairs={{0,96},{4,100},{8,104},{12,108},{16,112},{20,116},{24,120},{28,124... | collective-permute-start | bytes 110600 | tf_op jit(solution)/shard_map/ppermute | solution.py:417
  21.4 5.2 %collective-permute-start.8 = (bf16[144,128]{1,0:T(8,128)(2,1)S(1)}, bf16[144,128]{1,0:T(8,128)(2,1)S(1)}, u32[]{:S(2)}, u32[]{:S(2)}) collective-permute-start(bf16[144,128]{1,0:T(8,128)(2,1)S(1)} %get-tuple-element.32), channel_id=1, source_target_pairs={{0,64},{4,68},{8,72},{12,76},{16,80},{20,84},{24,88},{28,92},{32,9... | collective-permute-start | bytes 110600 | tf_op jit(solution)/shard_map/ppermute | solution.py:417
  22.7 4.9 %collective-permute-start.7 = (bf16[144,128]{1,0:T(8,128)(2,1)S(1)}, bf16[144,128]{1,0:T(8,128)(2,1)S(1)}, u32[]{:S(2)}, u32[]{:S(2)}) collective-permute-start(bf16[144,128]{1,0:T(8,128)(2,1)S(1)} %get-tuple-element.32), channel_id=1, source_target_pairs={{0,32},{4,36},{8,40},{12,44},{16,48},{20,52},{24,56},{28,60},{32,6... | collective-permute-start | bytes 110600 | tf_op jit(solution)/shard_map/ppermute | solution.py:417
  29.4 5.1 %collective-permute-start.12 = (bf16[384,256]{1,0:T(8,128)(2,1)S(1)}, bf16[384,256]{1,0:T(8,128)(2,1)S(1)}, u32[]{:S(2)}, u32[]{:S(2)}) collective-permute-start(bf16[384,256]{1,0:T(8,128)(2,1)S(1)} %get-tuple-element.40), channel_id=1, source_target_pairs={{0,32},{4,36},{8,40},{12,44},{16,48},{20,52},{24,56},{28,60},{32,6... | collective-permute-start | bytes 589832 | tf_op jit(solution)/shard_map/ppermute | solution.py:417
  31.9 20.3 %collective-permute-start.16 = (bf16[768,256]{1,0:T(8,128)(2,1)}, bf16[768,256]{1,0:T(8,128)(2,1)S(1)}, u32[]{:S(2)}, u32[]{:S(2)}) collective-permute-start(bf16[768,256]{1,0:T(8,128)(2,1)} %get-tuple-element.41), channel_id=1, source_target_pairs={{0,24},{4,28},{8,0},{12,4},{16,8},{20,12},{24,16},{28,20},{32,56},... | collective-permute-start | bytes 1179656 | tf_op jit(solution)/shard_map/ppermute | solution.py:417
  34.5 16.1 %collective-permute-start.13 = (bf16[384,256]{1,0:T(8,128)(2,1)S(1)}, bf16[384,256]{1,0:T(8,128)(2,1)S(1)}, u32[]{:S(2)}, u32[]{:S(2)}) collective-permute-start(bf16[384,256]{1,0:T(8,128)(2,1)S(1)} %collective-permute-done.12.own3), channel_id=1, source_target_pairs={{0,32},{4,36},{8,40},{12,44},{16,48},{20,52},{24,56},{28,60},{32,6... | collective-permute-start | bytes 589832 | tf_op jit(solution)/shard_map/ppermute | solution.py:417
  37.6 13.0 %all-to-all-start = ((f32[8,8,384]{2,1,0:T(8,128)}), f32[8,8,384]{2,1,0:T(8,128)S(1)}, u32[]{:S(2)}, u32[]{:S(2)}) async-start(f32[8,8,384]{2,1,0:T(8,128)} %get-tuple-element.38), calls=%async_computation | async-start | bytes 196608 | tf_op jit(solution)/shard_map/all_to_all | solution.py:425
  45.6 12.5 %collective-permute-start.15 = (bf16[768,256]{1,0:T(8,128)(2,1)}, bf16[768,256]{1,0:T(8,128)(2,1)S(1)}, u32[]{:S(2)}, u32[]{:S(2)}) collective-permute-start(bf16[768,256]{1,0:T(8,128)(2,1)} %get-tuple-element.41), channel_id=1, source_target_pairs={{0,16},{4,20},{8,24},{12,28},{16,0},{20,4},{24,8},{28,12},{32,48},... | collective-permute-start | bytes 1179656 | tf_op jit(solution)/shard_map/ppermute | solution.py:417
  46.5 19.2 %collective-permute-start.14 = (bf16[768,256]{1,0:T(8,128)(2,1)}, bf16[768,256]{1,0:T(8,128)(2,1)}, u32[]{:S(2)}, u32[]{:S(2)}) collective-permute-start(bf16[768,256]{1,0:T(8,128)(2,1)} %get-tuple-element.41), channel_id=1, source_target_pairs={{0,8},{4,12},{8,16},{12,20},{16,24},{20,28},{24,0},{28,4},{32,40},... | collective-permute-start | bytes 1179656 | tf_op jit(solution)/shard_map/ppermute | solution.py:417
  50.7 28.0 %collective-permute-start.17 = (bf16[768,256]{1,0:T(8,128)(2,1)S(1)}, bf16[768,256]{1,0:T(8,128)(2,1)S(1)}, u32[]{:S(2)}, u32[]{:S(2)}) collective-permute-start(bf16[768,256]{1,0:T(8,128)(2,1)S(1)} %get-tuple-element.45), channel_id=1, source_target_pairs={{0,8},{4,12},{8,16},{12,20},{16,24},{20,28},{24,0},{28,4},{32,40},... | collective-permute-start | bytes 1179656 | tf_op jit(solution)/shard_map/ppermute | solution.py:417
  51.8 31.6 %collective-permute-start.18 = (bf16[768,256]{1,0:T(8,128)(2,1)S(1)}, bf16[768,256]{1,0:T(8,128)(2,1)S(1)}, u32[]{:S(2)}, u32[]{:S(2)}) collective-permute-start(bf16[768,256]{1,0:T(8,128)(2,1)S(1)} %get-tuple-element.46), channel_id=1, source_target_pairs={{0,16},{4,20},{8,24},{12,28},{16,0},{20,4},{24,8},{28,12},{32,48},... | collective-permute-start | bytes 1179656 | tf_op jit(solution)/shard_map/ppermute | solution.py:417
  52.2 31.2 %collective-permute-start.19 = (bf16[768,256]{1,0:T(8,128)(2,1)S(1)}, bf16[768,256]{1,0:T(8,128)(2,1)S(1)}, u32[]{:S(2)}, u32[]{:S(2)}) collective-permute-start(bf16[768,256]{1,0:T(8,128)(2,1)S(1)} %get-tuple-element.47), channel_id=1, source_target_pairs={{0,24},{4,28},{8,0},{12,4},{16,8},{20,12},{24,16},{28,20},{32,56},... | collective-permute-start | bytes 1179656 | tf_op jit(solution)/shard_map/ppermute | solution.py:417
  93.4 10.2 %collective-permute-start.20 = (bf16[192,512]{1,0:T(8,128)(2,1)S(1)}, bf16[192,512]{1,0:T(8,128)(2,1)S(1)}, u32[]{:S(2)}, u32[]{:S(2)}) collective-permute-start(bf16[192,512]{1,0:T(8,128)(2,1)S(1)} %get-tuple-element.50), channel_id=1, source_target_pairs={{0,4},{4,0},{8,12},{12,8},{16,20},{20,16},{24,28},{28,24},{32,36},... | collective-permute-start | bytes 589832 | tf_op jit(solution)/shard_map/ppermute | solution.py:417
  (1 other events, 1.1 us)

commit v5 on v2

--- a/solution.py
+++ b/solution.py
@@ -15,7 +15,6 @@
 REPEAT = 4
 COLS = REPEAT * HEAD_DIM
 Z, X, CORES, TP = 8, 4, 2, 4
-CHUNK = 2
 SCALE = HEAD_DIM ** (-0.5) * 1.4426950408889634
 
 F32 = jnp.float32
@@ -236,7 +235,7 @@
             payload[PAIR:] = own4[...]
 
 
-TILE = 128
+TILE = 384
 TILES = [(head, slice(at, at + TILE)) for head in range(REPEAT) for at in range(0, PAIR, TILE)]
 
 
@@ -269,8 +268,8 @@
 
 
 class Window:
-    def __init__(self, prior, blocks, kv, bounds, sems):
-        self.kv, self.bounds = kv, bounds
+    def __init__(self, prior, blocks, chunk, kv, bounds, sems):
+        self.kv, self.bounds, self.chunk = kv, bounds, chunk
         used = jnp.int32(0)
         self.copies = []
         for at, (ref, distance) in enumerate(blocks):
@@ -287,14 +286,17 @@
                 bounds[slot] = jnp.maximum(distance * PAIR - prior, 0)
 
             used = used + needed.astype(jnp.int32)
-        self.steps = (used + CHUNK - 1) // CHUNK
+        self.steps = (used + chunk - 1) // chunk
         kv[:, 2 * HEAD_DIM :] = jnp.ones((kv.shape[0], HEAD_DIM), BF16)
 
-        @pl.when(used % CHUNK != 0)
-        def _():
-            rows = pl.ds(pl.multiple_of(used * PAIR, PAIR), PAIR)
-            kv[rows, : 2 * HEAD_DIM] = jnp.zeros((PAIR, 2 * HEAD_DIM), BF16)
-            bounds[used] = jnp.int32(PAIR)
+        for extra in range(chunk - 1):
+
+            @pl.when(used + extra < self.steps * chunk)
+            def _():
+                spare = jnp.minimum(used + extra, bounds.shape[0] - 1)
+                rows = pl.ds(pl.multiple_of(spare * PAIR, PAIR), PAIR)
+                kv[rows, : 2 * HEAD_DIM] = jnp.zeros((PAIR, 2 * HEAD_DIM), BF16)
+                bounds[spare] = jnp.int32(PAIR)
 
     def absorb(self, queries, tops, acc):
         for needed, copy in self.copies:
@@ -302,22 +304,28 @@
 
         @pl.loop(0, self.steps)
         def _(step):
-            rows = pl.ds(pl.multiple_of(step * CHUNK * PAIR, CHUNK * PAIR), CHUNK * PAIR)
-            low0, low1 = self.bounds[step * CHUNK], self.bounds[step * CHUNK + 1]
-            whole = (low0 == 0) & (low1 == 0)
-
-            @pl.when(whole)
+            keys = self.chunk * PAIR
+            rows = pl.ds(pl.multiple_of(step * keys, keys), keys)
+            lows = [self.bounds[step * self.chunk + slot] for slot in range(self.chunk)]
+            hidden = lows[0]
+            for low in lows[1:]:
+                hidden = hidden + low
+
+            @pl.when(hidden == 0)
             def _():
                 sweep(queries, self.kv, tops, acc, rows)
 
-            @pl.when(jnp.logical_not(whole))
+            @pl.when(hidden != 0)
             def _():
-                column = lax.broadcasted_iota(jnp.int32, (1, CHUNK * PAIR), 1)
-                seen = column >= jnp.where(column < PAIR, low0, PAIR + low1)
-                sweep(queries, self.kv, tops, acc, rows, lambda part: seen)
-
-
-SLOTS = 10
+                column = lax.broadcasted_iota(jnp.int32, (1, keys), 1)
+                start = lows[0]
+                for slot in range(1, self.chunk):
+                    start = jnp.where(column >= slot * PAIR, slot * PAIR + lows[slot], start)
+                sweep(queries, self.kv, tops, acc, rows, lambda part: column >= start)
+
+
+NEAR_SLOTS, NEAR_CHUNK = 10, 5
+FAR_SLOTS, FAR_CHUNK = 6, 3
 
 
 def near_kernel(
@@ -331,7 +339,7 @@
         wrapped = jnp.where(x < shift, 4, 0)
         blocks.append((other.at[pl.ds(0, PAIR)], 4 + shift - wrapped))
         blocks.append((other.at[pl.ds(PAIR, PAIR)], 8 + shift - wrapped))
-    window = Window(reach[0], blocks, kv, bounds, sems)
+    window = Window(reach[0], blocks, NEAR_CHUNK, kv, bounds, sems)
     tops[...] = jnp.full(tops.shape, NEGATIVE, F32)
     acc[...] = jnp.zeros(acc.shape, F32)
     scales[...] = jnp.broadcast_to(row_scale(sums), (PAIR, HEAD_DIM))
@@ -352,7 +360,7 @@
         wrapped = x < shift
         blocks.append((other.at[pl.ds(0, PAIR)], 12 + shift - jnp.where(wrapped, 4, 0)))
         blocks.append((other.at[pl.ds(PAIR, PAIR)], shift + jnp.where(wrapped, 12, 0)))
-    window = Window(reach[0], blocks, kv, bounds, sems)
+    window = Window(reach[0], blocks, FAR_CHUNK, kv, bounds, sems)
     own[:, : 2 * HEAD_DIM] = own0[...]
     own[:, 2 * HEAD_DIM :] = jnp.ones((PAIR, HEAD_DIM), BF16)
     window.absorb(queries, tops, acc)
@@ -516,11 +524,12 @@
         [SMEM] + [VMEM] * 11,
         (VMEM,) * 3,
         scratch=(
-            pltpu.VMEM((SLOTS * PAIR, 3 * HEAD_DIM), BF16),
+            pltpu.VMEM((NEAR_SLOTS * PAIR, 3 * HEAD_DIM), BF16),
             pltpu.VMEM((PAIR, HEAD_DIM), F32),
-            pltpu.SMEM((SLOTS,), jnp.int32),
+            pltpu.SMEM((NEAR_SLOTS,), jnp.int32),
             pltpu.SemaphoreType.DMA((10,)),
         ),
+        limit=24,
         name="near",
     )(
         reach, all_sums, first, keep, queries_r, own1, own2, own3, own4, *others12
@@ -537,9 +546,9 @@
         [SMEM, SMEM] + [VMEM] * 7,
         (VMEM,) * 5,
         scratch=(
-            pltpu.VMEM((SLOTS * PAIR, 3 * HEAD_DIM), BF16),
+            pltpu.VMEM((FAR_SLOTS * PAIR, 3 * HEAD_DIM), BF16),
             pltpu.VMEM((PAIR, 3 * HEAD_DIM), BF16),
-            pltpu.SMEM((SLOTS,), jnp.int32),
+            pltpu.SMEM((FAR_SLOTS,), jnp.int32),
             pltpu.SemaphoreType.DMA((10,)),
         ),
         aliases={3: 3, 4: 4},

time: 96.8 us -> 96.2 us (level)
  the two profiles are of different devices: /device:TPU:103 before, /device:TPU:7 now
where the time goes in v5:
time: 96.2 us; the launch traced here: 95 us
  waiting for transfers between devices  34.8 us (36%)
  starting transfers between devices  22.5 us (23%)
  blocking collectives  20.7 us (22%)
  Pallas kernels  14.8 us (15%)
  local copies, waits for them, and re-layouts  1.92 us (2%)
    ppermute x21, waiting for transfers between devices, move(): return lax.ppermute(value, CTX, pairs)  34.8 us
    ppermute x21, starting transfers between devices, move(): return lax.ppermute(value, CTX, pairs)  22.5 us
    all_to_all x2, blocking collectives, exchange(): return lax.all_to_all(sums, ('core', 'tp'), 0, 0, tiled=True)  20.7 us
    pallas_call x1, Pallas kernels, shards(): call(far_kernel, (shape((TOK, COLS), BF16), shape((TOK, COLS), BF16), sha...  6.48 us
  transfers between devices with their start and end apart: 21, of which 11 were waited for; matrix products, arithmetic and copies ran while one was open for 0% of the time, Pallas kernels for 5%

profile of v5, /device:TPU:7, one launch (start us, length us, event | category | flops | bytes accessed | tf_op | source)
XLA Modules:
  0.0 95.0 jit_solution(16545986675808482875)
XLA Ops:
  3.5 1.2 %collective-permute-done.seg_r = s32[192]{0:T(256)S(1)} collective-permute-done((s32[192]{0:T(256)S(1)}, s32[192]{0:T(256)S(1)}, u32[]{:S(2)}, u32[]{:S(2)}) %collective-permute-start) | collective-permute-done | bytes 800 | tf_op jit(solution)/shard_map/ppermute | solution.py:425
  4.7 1.4 %prep.1 = (bf16[384,256]{1,0:T(8,128)(2,1)S(1)}, bf16[384,256]{1,0:T(8,128)(2,1)S(1)}, bf16[144,128]{1,0:T(8,128)(2,1)S(1)}, s32[8]{0:T(128)S(1)}) custom-call(s32[192]{0:T(256)S(1)} %copy-done, s32[192]{0:T(256)S(1)} %collective-permute-done.seg_r, bf16[4,192,128]{2,1,0:T(8,128)(2,1)S(1)} %get-tuple-element.58.own, ...), custom_call_target="tpu_custom_call" | custom-call | tf_op jit(solution)/shard_map/prep/pallas_call | solution.py:450
  6.0 1.7 %collective-permute-start.5 = (bf16[384,256]{1,0:T(8,128)(2,1)S(1)}, bf16[384,256]{1,0:T(8,128)(2,1)S(1)}, u32[]{:S(2)}, u32[]{:S(2)}) collective-permute-start(bf16[384,256]{1,0:T(8,128)(2,1)S(1)} %get-tuple-element.30.own0), channel_id=1, source_target_pairs={{0,32},{4,36},{8,40},{12,44},{16,48},{20,52},{24,56},{28,60},{32,6... | collective-permute-start | bytes 589832 | tf_op jit(solution)/shard_map/ppermute | solution.py:425
  8.3 1.0 %collective-permute-start.3 = (bf16[144,128]{1,0:T(8,128)(2,1)S(1)}, bf16[144,128]{1,0:T(8,128)(2,1)S(1)}, u32[]{:S(2)}, u32[]{:S(2)}) collective-permute-start(bf16[144,128]{1,0:T(8,128)(2,1)S(1)} %get-tuple-element.29.own), channel_id=1, source_target_pairs={{0,16},{4,20},{8,24},{12,28},{16,0},{20,4},{24,8},{28,12},{32,48},... | collective-permute-start | bytes 110600 | tf_op jit(solution)/shard_map/ppermute | solution.py:425
  9.3 1.6 %collective-permute-start.2 = (bf16[144,128]{1,0:T(8,128)(2,1)S(1)}, bf16[144,128]{1,0:T(8,128)(2,1)S(1)}, u32[]{:S(2)}, u32[]{:S(2)}) collective-permute-start(bf16[144,128]{1,0:T(8,128)(2,1)S(1)} %get-tuple-element.29.own), channel_id=1, source_target_pairs={{0,8},{4,12},{8,16},{12,20},{16,24},{20,28},{24,0},{28,4},{32,40},... | collective-permute-start | bytes 110600 | tf_op jit(solution)/shard_map/ppermute | solution.py:425
  13.0 3.8 %collective-permute-done.5.own1 = bf16[384,256]{1,0:T(8,128)(2,1)S(1)} collective-permute-done((bf16[384,256]{1,0:T(8,128)(2,1)S(1)}, bf16[384,256]{1,0:T(8,128)(2,1)S(1)}, u32[]{:S(2)}, u32[]{:S(2)}) %collective-permute-start.5) | collective-permute-done | bytes 196640 | tf_op jit(solution)/shard_map/ppermute | solution.py:425
  17.6 3.9 %collective-permute-start.10 = (bf16[144,128]{1,0:T(8,128)(2,1)S(1)}, bf16[144,128]{1,0:T(8,128)(2,1)S(1)}, u32[]{:S(2)}, u32[]{:S(2)}) collective-permute-start(bf16[144,128]{1,0:T(8,128)(2,1)S(1)} %get-tuple-element.32), channel_id=1, source_target_pairs={{0,128},{4,132},{8,136},{12,140},{16,144},{20,148},{24,152},{28,15... | collective-permute-start | bytes 110600 | tf_op jit(solution)/shard_map/ppermute | solution.py:425
  21.4 1.8 %collective-permute-start.9 = (bf16[144,128]{1,0:T(8,128)(2,1)S(1)}, bf16[144,128]{1,0:T(8,128)(2,1)S(1)}, u32[]{:S(2)}, u32[]{:S(2)}) collective-permute-start(bf16[144,128]{1,0:T(8,128)(2,1)S(1)} %get-tuple-element.32), channel_id=1, source_target_pairs={{0,96},{4,100},{8,104},{12,108},{16,112},{20,116},{24,120},{28,124... | collective-permute-start | bytes 110600 | tf_op jit(solution)/shard_map/ppermute | solution.py:425
  23.2 2.0 %collective-permute-start.7 = (bf16[144,128]{1,0:T(8,128)(2,1)S(1)}, bf16[144,128]{1,0:T(8,128)(2,1)S(1)}, u32[]{:S(2)}, u32[]{:S(2)}) collective-permute-start(bf16[144,128]{1,0:T(8,128)(2,1)S(1)} %get-tuple-element.32), channel_id=1, source_target_pairs={{0,32},{4,36},{8,40},{12,44},{16,48},{20,52},{24,56},{28,60},{32,6... | collective-permute-start | bytes 110600 | tf_op jit(solution)/shard_map/ppermute | solution.py:425
  25.2 1.9 %inside.1 = (f32[384,512]{1,0:T(8,128)S(1)}, bf16[384,512]{1,0:T(8,128)(2,1)S(1)}) custom-call(s32[8]{0:T(128)S(1)} %get-tuple-element.28.info, bf16[2,192,512]{2,1,0:T(8,128)(2,1)S(1)} %get-tuple-element.51.keep, bf16[2,192,512]{2,1,0:T(8,128)(2,1)S(1)} %collective-permute-done.6.queries_r, bf16[384,256]{1,0:T(8,128)(2,1)S(1)} %get-tuple-element.33.packed), custom_call_target="tpu_custom_call" | custom-call | tf_op jit(solution)/shard_map/inside/pallas_call | solution.py:482
  27.2 2.7 %collective-permute-done.8.from2 = bf16[144,128]{1,0:T(8,128)(2,1)S(1)} collective-permute-done((bf16[144,128]{1,0:T(8,128)(2,1)S(1)}, bf16[144,128]{1,0:T(8,128)(2,1)S(1)}, u32[]{:S(2)}, u32[]{:S(2)}) %collective-permute-start.8) | collective-permute-done | bytes 36896 | tf_op jit(solution)/shard_map/ppermute | solution.py:425
  30.0 1.3 %collective-permute-done.7.from1 = bf16[144,128]{1,0:T(8,128)(2,1)S(1)} collective-permute-done((bf16[144,128]{1,0:T(8,128)(2,1)S(1)}, bf16[144,128]{1,0:T(8,128)(2,1)S(1)}, u32[]{:S(2)}, u32[]{:S(2)}) %collective-permute-start.7) | collective-permute-done | bytes 36896 | tf_op jit(solution)/shard_map/ppermute | solution.py:425
  31.3 1.6 %first.1 = (f32[384,512]{1,0:T(8,128)S(1)}, f32[8,8,384]{2,1,0:T(8,128)S(1)}, s32[1]{0:T(128)}, bf16[768,256]{1,0:T(8,128)(2,1)S(1)}, bf16[384,256]{1,0:T(8,128)(2,1)S(1)}) custom-call(s32[8]{0:T(128)S(1)} %get-tuple-element.28.info, f32[136,128]{1,0:T(8,128)S(1)} %get-tuple-element.31.prefix, bf16[144,128]{1,0:T(8,128)(2,1)S(1)} %collective-permute-done.7.from1, ...), custom_call_target="tpu_custom_call" | custom-call | tf_op jit(solution)/shard_map/first/pallas_call | solution.py:489
  33.2 1.3 %collective-permute-start.15 = (bf16[768,256]{1,0:T(8,128)(2,1)S(1)}, bf16[768,256]{1,0:T(8,128)(2,1)S(1)}, u32[]{:S(2)}, u32[]{:S(2)}) collective-permute-start(bf16[768,256]{1,0:T(8,128)(2,1)S(1)} %get-tuple-element.41), channel_id=1, source_target_pairs={{0,16},{4,20},{8,24},{12,28},{16,0},{20,4},{24,8},{28,12},{32,48},... | collective-permute-start | bytes 1179656 | tf_op jit(solution)/shard_map/ppermute | solution.py:425
  34.5 1.8 %collective-permute-start.14 = (bf16[768,256]{1,0:T(8,128)(2,1)S(1)}, bf16[768,256]{1,0:T(8,128)(2,1)S(1)}, u32[]{:S(2)}, u32[]{:S(2)}) collective-permute-start(bf16[768,256]{1,0:T(8,128)(2,1)S(1)} %get-tuple-element.41), channel_id=1, source_target_pairs={{0,8},{4,12},{8,16},{12,20},{16,24},{20,28},{24,0},{28,4},{32,40},... | collective-permute-start | bytes 1179656 | tf_op jit(solution)/shard_map/ppermute | solution.py:425
  36.3 3.2 %collective-permute-done.12.own3 = bf16[384,256]{1,0:T(8,128)(2,1)S(1)} collective-permute-done((bf16[384,256]{1,0:T(8,128)(2,1)S(1)}, bf16[384,256]{1,0:T(8,128)(2,1)S(1)}, u32[]{:S(2)}, u32[]{:S(2)}) %collective-permute-start.12) | collective-permute-done | bytes 196640 | tf_op jit(solution)/shard_map/ppermute | solution.py:425
  39.5 11.4 %all_to_all.10.sums.refs_3_ = f32[8,8,384]{2,1,0:T(8,128)S(1)} all-to-all(f32[8,8,384]{2,1,0:T(8,128)S(1)} %get-tuple-element.38), channel_id=1, replica_groups=mesh['z'=8,'x'=4,'core'=2,'tp'=4] {'core','tp'}, dimensions={0} | all-to-all | bytes 196608 | tf_op jit(solution)/shard_map/all_to_all | solution.py:433
  51.0 2.4 %collective-permute-done.14.refs_0_ = bf16[768,256]{1,0:T(8,128)(2,1)S(1)} collective-permute-done((bf16[768,256]{1,0:T(8,128)(2,1)S(1)}, bf16[768,256]{1,0:T(8,128)(2,1)S(1)}, u32[]{:S(2)}, u32[]{:S(2)}) %collective-permute-start.14) | collective-permute-done | bytes 393248 | tf_op jit(solution)/shard_map/ppermute | solution.py:425
  53.4 3.5 %collective-permute-start.17 = (bf16[768,256]{1,0:T(8,128)(2,1)S(1)}, bf16[768,256]{1,0:T(8,128)(2,1)S(1)}, u32[]{:S(2)}, u32[]{:S(2)}) collective-permute-start(bf16[768,256]{1,0:T(8,128)(2,1)S(1)} %get-tuple-element.45), channel_id=1, source_target_pairs={{0,8},{4,12},{8,16},{12,20},{16,24},{20,28},{24,0},{28,4},{32,40},... | collective-permute-start | bytes 1179656 | tf_op jit(solution)/shard_map/ppermute | solution.py:425
  57.6 1.7 %near.1 = (bf16[4,384,128]{2,1,0:T(8,128)(2,1)S(1)}, f32[4,384,128]{2,1,0:T(8,128)S(1)}, f32[4,384,256]{2,1,0:T(8,128)S(1)}) custom-call(s32[1]{0:T(128)} %get-tuple-element.37.reach, f32[8,8,384]{2,1,0:T(8,128)S(1)} %all_to_all.10.sums.refs_3_, f32[384,512]{1,0:T(8,128)S(1)} %get-tuple-element.39.first, bf16[2,192,512]{2,1,0:T(8,128)(2,1)S(1)} %get-tuple-element.51.keep, ...), custom_call_target="tpu_custom_call" | custom-call | tf_op jit(solution)/shard_map/near/pallas_call | solution.py:517
  59.3 13.9 %collective-permute-done.17.refs_0_ = bf16[768,256]{1,0:T(8,128)(2,1)S(1)} collective-permute-done((bf16[768,256]{1,0:T(8,128)(2,1)S(1)}, bf16[768,256]{1,0:T(8,128)(2,1)S(1)}, u32[]{:S(2)}, u32[]{:S(2)}) %collective-permute-start.17) | collective-permute-done | bytes 393248 | tf_op jit(solution)/shard_map/ppermute | solution.py:425
  73.2 4.1 %collective-permute-done.19.refs_2_ = bf16[768,256]{1,0:T(8,128)(2,1)S(1)} collective-permute-done((bf16[768,256]{1,0:T(8,128)(2,1)S(1)}, bf16[768,256]{1,0:T(8,128)(2,1)S(1)}, u32[]{:S(2)}, u32[]{:S(2)}) %collective-permute-start.19) | collective-permute-done | bytes 393248 | tf_op jit(solution)/shard_map/ppermute | solution.py:425
  77.3 6.5 %far.1 = (bf16[192,512]{1,0:T(8,128)(2,1)S(1)}, bf16[192,512]{1,0:T(8,128)(2,1)S(1)}, f32[8,8,192]{2,1,0:T(8,128)S(1)}, f32[4,384,128]{2,1,0:T(8,128)S(1)}, f32[4,384,256]{2,1,0:T(8,128)S(1)}) custom-call(s32[8]{0:T(128)S(1)} %get-tuple-element.28.info, s32[1]{0:T(128)} %get-tuple-element.37.reach, ...), custom_call_target="tpu_custom_call", output_to_operand_aliasing={{3}: (3, {}), {4}: (4, {})} | custom-call | tf_op jit(solution)/shard_map/far/pallas_call | solution.py:537
  84.7 9.3 %all_to_all.11.sums = f32[8,8,192]{2,1,0:T(8,128)S(1)} all-to-all(f32[8,8,192]{2,1,0:T(8,128)S(1)} %get-tuple-element.48), channel_id=1, replica_groups=mesh['z'=8,'x'=4,'core'=2,'tp'=4] {'core','tp'}, dimensions={0} | all-to-all | bytes 98304 | tf_op jit(solution)/shard_map/all_to_all | solution.py:433
  (39 shorter events, 9.8 us)
Async XLA Ops:
  0.0 2.7 %copy-start.1 = (bf16[192,1024]{1,0:T(8,128)(2,1)S(1)}, bf16[192,1024]{1,0:T(8,128)(2,1)}, u32[]{:S(2)}) copy-start(bf16[192,1024]{1,0:T(8,128)(2,1)} %param.11) | copy-start | bytes 1179652
  0.0 2.7 %copy-start.2 = (bf16[192,1024]{1,0:T(8,128)(2,1)S(1)}, bf16[192,1024]{1,0:T(8,128)(2,1)}, u32[]{:S(2)}) copy-start(bf16[192,1024]{1,0:T(8,128)(2,1)} %param.7) | copy-start | bytes 1179652
  1.9 1.1 %copy-start = (s32[192]{0:T(256)S(1)}, s32[192]{0:T(256)}, u32[]{:S(2)}) copy-start(s32[192]{0:T(256)} %seg.1) | copy-start | bytes 2308
  1.9 2.7 %collective-permute-start.1 = (bf16[4,192,128]{2,1,0:T(8,128)(2,1)S(1)}, bf16[4,192,128]{2,1,0:T(8,128)(2,1)S(1)}, u32[]{:S(2)}, u32[]{:S(2)}) collective-permute-start(bf16[4,192,128]{2,1,0:T(8,128)(2,1)S(1)} %get-tuple-element.57), channel_id=1, source_target_pairs={{0,4},{4,0},{8,12},{12,8},{16,20},{20,16},{24,28},{28,24},{32,36},... | collective-permute-start | bytes 589832 | tf_op jit(solution)/shard_map/ppermute | solution.py:425
  2.9 14.0 %collective-permute-start.6 = (bf16[2,192,512]{2,1,0:T(8,128)(2,1)S(1)}, bf16[2,192,512]{2,1,0:T(8,128)(2,1)S(1)}, u32[]{:S(2)}, u32[]{:S(2)}) collective-permute-start(bf16[2,192,512]{2,1,0:T(8,128)(2,1)S(1)} %get-tuple-element.52), channel_id=1, source_target_pairs={{0,4},{4,0},{8,12},{12,8},{16,20},{20,16},{24,28},{28,24},{32,36},... | collective-permute-start | bytes 1179656 | tf_op jit(solution)/shard_map/ppermute | solution.py:425
  3.0 1.7 %collective-permute-start = (s32[192]{0:T(256)S(1)}, s32[192]{0:T(256)S(1)}, u32[]{:S(2)}, u32[]{:S(2)}) collective-permute-start(s32[192]{0:T(256)S(1)} %copy-done), channel_id=1, source_target_pairs={{0,4},{4,0},{8,12},{12,8},{16,20},{20,16},{24,28},{28,24},{32,36},... | collective-permute-start | bytes 2312 | tf_op jit(solution)/shard_map/ppermute | solution.py:425
  6.0 10.8 %collective-permute-start.5 = (bf16[384,256]{1,0:T(8,128)(2,1)S(1)}, bf16[384,256]{1,0:T(8,128)(2,1)S(1)}, u32[]{:S(2)}, u32[]{:S(2)}) collective-permute-start(bf16[384,256]{1,0:T(8,128)(2,1)S(1)} %get-tuple-element.30.own0), channel_id=1, source_target_pairs={{0,32},{4,36},{8,40},{12,44},{16,48},{20,52},{24,56},{28,60},{32,6... | collective-permute-start | bytes 589832 | tf_op jit(solution)/shard_map/ppermute | solution.py:425
  7.8 4.0 %collective-permute-start.4 = (bf16[144,128]{1,0:T(8,128)(2,1)S(1)}, bf16[144,128]{1,0:T(8,128)(2,1)S(1)}, u32[]{:S(2)}, u32[]{:S(2)}) collective-permute-start(bf16[144,128]{1,0:T(8,128)(2,1)S(1)} %get-tuple-element.29.own), channel_id=1, source_target_pairs={{0,24},{4,28},{8,0},{12,4},{16,8},{20,12},{24,16},{28,20},{32,56},... | collective-permute-start | bytes 110600 | tf_op jit(solution)/shard_map/ppermute | solution.py:425
  8.3 4.3 %collective-permute-start.3 = (bf16[144,128]{1,0:T(8,128)(2,1)S(1)}, bf16[144,128]{1,0:T(8,128)(2,1)S(1)}, u32[]{:S(2)}, u32[]{:S(2)}) collective-permute-start(bf16[144,128]{1,0:T(8,128)(2,1)S(1)} %get-tuple-element.29.own), channel_id=1, source_target_pairs={{0,16},{4,20},{8,24},{12,28},{16,0},{20,4},{24,8},{28,12},{32,48},... | collective-permute-start | bytes 110600 | tf_op jit(solution)/shard_map/ppermute | solution.py:425
  9.3 3.7 %collective-permute-start.2 = (bf16[144,128]{1,0:T(8,128)(2,1)S(1)}, bf16[144,128]{1,0:T(8,128)(2,1)S(1)}, u32[]{:S(2)}, u32[]{:S(2)}) collective-permute-start(bf16[144,128]{1,0:T(8,128)(2,1)S(1)} %get-tuple-element.29.own), channel_id=1, source_target_pairs={{0,8},{4,12},{8,16},{12,20},{16,24},{20,28},{24,0},{28,4},{32,40},... | collective-permute-start | bytes 110600 | tf_op jit(solution)/shard_map/ppermute | solution.py:425
  17.5 13.8 %collective-permute-start.11 = (bf16[384,256]{1,0:T(8,128)(2,1)S(1)}, bf16[384,256]{1,0:T(8,128)(2,1)S(1)}, u32[]{:S(2)}, u32[]{:S(2)}) collective-permute-start(bf16[384,256]{1,0:T(8,128)(2,1)S(1)} %get-tuple-element.36), channel_id=1, source_target_pairs={{0,32},{4,36},{8,40},{12,44},{16,48},{20,52},{24,56},{28,60},{32,6... | collective-permute-start | bytes 589832 | tf_op jit(solution)/shard_map/ppermute | solution.py:425
  17.6 9.6 %collective-permute-start.10 = (bf16[144,128]{1,0:T(8,128)(2,1)S(1)}, bf16[144,128]{1,0:T(8,128)(2,1)S(1)}, u32[]{:S(2)}, u32[]{:S(2)}) collective-permute-start(bf16[144,128]{1,0:T(8,128)(2,1)S(1)} %get-tuple-element.32), channel_id=1, source_target_pairs={{0,128},{4,132},{8,136},{12,140},{16,144},{20,148},{24,152},{28,15... | collective-permute-start | bytes 110600 | tf_op jit(solution)/shard_map/ppermute | solution.py:425
  21.4 5.8 %collective-permute-start.9 = (bf16[144,128]{1,0:T(8,128)(2,1)S(1)}, bf16[144,128]{1,0:T(8,128)(2,1)S(1)}, u32[]{:S(2)}, u32[]{:S(2)}) collective-permute-start(bf16[144,128]{1,0:T(8,128)(2,1)S(1)} %get-tuple-element.32), channel_id=1, source_target_pairs={{0,96},{4,100},{8,104},{12,108},{16,112},{20,116},{24,120},{28,124... | collective-permute-start | bytes 110600 | tf_op jit(solution)/shard_map/ppermute | solution.py:425
  23.2 6.8 %collective-permute-start.8 = (bf16[144,128]{1,0:T(8,128)(2,1)S(1)}, bf16[144,128]{1,0:T(8,128)(2,1)S(1)}, u32[]{:S(2)}, u32[]{:S(2)}) collective-permute-start(bf16[144,128]{1,0:T(8,128)(2,1)S(1)} %get-tuple-element.32), channel_id=1, source_target_pairs={{0,64},{4,68},{8,72},{12,76},{16,80},{20,84},{24,88},{28,92},{32,9... | collective-permute-start | bytes 110600 | tf_op jit(solution)/shard_map/ppermute | solution.py:425
  23.2 8.1 %collective-permute-start.7 = (bf16[144,128]{1,0:T(8,128)(2,1)S(1)}, bf16[144,128]{1,0:T(8,128)(2,1)S(1)}, u32[]{:S(2)}, u32[]{:S(2)}) collective-permute-start(bf16[144,128]{1,0:T(8,128)(2,1)S(1)} %get-tuple-element.32), channel_id=1, source_target_pairs={{0,32},{4,36},{8,40},{12,44},{16,48},{20,52},{24,56},{28,60},{32,6... | collective-permute-start | bytes 110600 | tf_op jit(solution)/shard_map/ppermute | solution.py:425
  32.9 6.6 %collective-permute-start.12 = (bf16[384,256]{1,0:T(8,128)(2,1)S(1)}, bf16[384,256]{1,0:T(8,128)(2,1)S(1)}, u32[]{:S(2)}, u32[]{:S(2)}) collective-permute-start(bf16[384,256]{1,0:T(8,128)(2,1)S(1)} %get-tuple-element.40), channel_id=1, source_target_pairs={{0,32},{4,36},{8,40},{12,44},{16,48},{20,52},{24,56},{28,60},{32,6... | collective-permute-start | bytes 589832 | tf_op jit(solution)/shard_map/ppermute | solution.py:425
  33.1 17.9 %collective-permute-start.16 = (bf16[768,256]{1,0:T(8,128)(2,1)S(1)}, bf16[768,256]{1,0:T(8,128)(2,1)S(1)}, u32[]{:S(2)}, u32[]{:S(2)}) collective-permute-start(bf16[768,256]{1,0:T(8,128)(2,1)S(1)} %get-tuple-element.41), channel_id=1, source_target_pairs={{0,24},{4,28},{8,0},{12,4},{16,8},{20,12},{24,16},{28,20},{32,56},... | collective-permute-start | bytes 1179656 | tf_op jit(solution)/shard_map/ppermute | solution.py:425
  33.2 17.7 %collective-permute-start.15 = (bf16[768,256]{1,0:T(8,128)(2,1)S(1)}, bf16[768,256]{1,0:T(8,128)(2,1)S(1)}, u32[]{:S(2)}, u32[]{:S(2)}) collective-permute-start(bf16[768,256]{1,0:T(8,128)(2,1)S(1)} %get-tuple-element.41), channel_id=1, source_target_pairs={{0,16},{4,20},{8,24},{12,28},{16,0},{20,4},{24,8},{28,12},{32,48},... | collective-permute-start | bytes 1179656 | tf_op jit(solution)/shard_map/ppermute | solution.py:425
  34.5 18.8 %collective-permute-start.14 = (bf16[768,256]{1,0:T(8,128)(2,1)S(1)}, bf16[768,256]{1,0:T(8,128)(2,1)S(1)}, u32[]{:S(2)}, u32[]{:S(2)}) collective-permute-start(bf16[768,256]{1,0:T(8,128)(2,1)S(1)} %get-tuple-element.41), channel_id=1, source_target_pairs={{0,8},{4,12},{8,16},{12,20},{16,24},{20,28},{24,0},{28,4},{32,40},... | collective-permute-start | bytes 1179656 | tf_op jit(solution)/shard_map/ppermute | solution.py:425
  39.5 11.4 %collective-permute-start.13 = (bf16[384,256]{1,0:T(8,128)(2,1)S(1)}, bf16[384,256]{1,0:T(8,128)(2,1)S(1)}, u32[]{:S(2)}, u32[]{:S(2)}) collective-permute-start(bf16[384,256]{1,0:T(8,128)(2,1)S(1)} %collective-permute-done.12.own3), channel_id=1, source_target_pairs={{0,32},{4,36},{8,40},{12,44},{16,48},{20,52},{24,56},{28,60},{32,6... | collective-permute-start | bytes 589832 | tf_op jit(solution)/shard_map/ppermute | solution.py:425
  53.4 19.8 %collective-permute-start.17 = (bf16[768,256]{1,0:T(8,128)(2,1)S(1)}, bf16[768,256]{1,0:T(8,128)(2,1)S(1)}, u32[]{:S(2)}, u32[]{:S(2)}) collective-permute-start(bf16[768,256]{1,0:T(8,128)(2,1)S(1)} %get-tuple-element.45), channel_id=1, source_target_pairs={{0,8},{4,12},{8,16},{12,20},{16,24},{20,28},{24,0},{28,4},{32,40},... | collective-permute-start | bytes 1179656 | tf_op jit(solution)/shard_map/ppermute | solution.py:425
  56.9 16.3 %collective-permute-start.18 = (bf16[768,256]{1,0:T(8,128)(2,1)S(1)}, bf16[768,256]{1,0:T(8,128)(2,1)S(1)}, u32[]{:S(2)}, u32[]{:S(2)}) collective-permute-start(bf16[768,256]{1,0:T(8,128)(2,1)S(1)} %get-tuple-element.46), channel_id=1, source_target_pairs={{0,16},{4,20},{8,24},{12,28},{16,0},{20,4},{24,8},{28,12},{32,48},... | collective-permute-start | bytes 1179656 | tf_op jit(solution)/shard_map/ppermute | solution.py:425
  56.9 20.3 %collective-permute-start.19 = (bf16[768,256]{1,0:T(8,128)(2,1)S(1)}, bf16[768,256]{1,0:T(8,128)(2,1)S(1)}, u32[]{:S(2)}, u32[]{:S(2)}) collective-permute-start(bf16[768,256]{1,0:T(8,128)(2,1)S(1)} %get-tuple-element.47), channel_id=1, source_target_pairs={{0,24},{4,28},{8,0},{12,4},{16,8},{20,12},{24,16},{28,20},{32,56},... | collective-permute-start | bytes 1179656 | tf_op jit(solution)/shard_map/ppermute | solution.py:425
  83.7 10.3 %collective-permute-start.20 = (bf16[192,512]{1,0:T(8,128)(2,1)S(1)}, bf16[192,512]{1,0:T(8,128)(2,1)S(1)}, u32[]{:S(2)}, u32[]{:S(2)}) collective-permute-start(bf16[192,512]{1,0:T(8,128)(2,1)S(1)} %get-tuple-element.50), channel_id=1, source_target_pairs={{0,4},{4,0},{8,12},{12,8},{16,20},{20,16},{24,28},{28,24},{32,36},... | collective-permute-start | bytes 589832 | tf_op jit(solution)/shard_map/ppermute | solution.py:425
